TPU v7x, 32 devices: a whole 2x2x4 slice. The times are simulated.
32 devices in a mesh: outer: 4 (over x, core), inner: 2 (over y), tensor: 4 (over z).
Axes of the slice: x: 2, y: 2, z: 4, core: 2. Of those that a mesh axis runs over, the one named last changes fastest.
Arguments:
- hidden_in: bfloat16 [1536, 4096], P(('outer', 'inner', 'tensor')), may hold values from -15 to 15
- norm_gain: float32 [4096], replicated, may hold values from 0.5 to 5
- w_query: bfloat16 [4096, 4096], P('inner', 'tensor'), may hold values from -0.110485435 to 0.110485435
- w_key: bfloat16 [4096, 1024], P('inner', 'tensor'), may hold values from -0.110485435 to 0.110485435
- value_weight: bfloat16 [4096, 1024], P('inner', 'tensor'), may hold values from -0.09375 to 0.09375
- w_out: bfloat16 [4096, 4096], P('tensor'), may hold values from -0.09375 to 0.09375
- doc_ids: int32 [1536], P(('outer', 'inner')), may hold values from 0 to 5, as said below
- positions: int32 [1536], P(('outer', 'inner')), may hold values from 0 to 65535, as said below
Outputs:
- layer_out: bfloat16 [1536, 4096], P(('outer', 'inner', 'tensor'))
Inputs may be any that keep to these rules, and one draw needn't show every extreme that they name: `doc_ids`: document numbers never fall along the sequence; each of the 6 documents has at least one token, and exactly one of them has 960 tokens. Document numbers may be sent packed or coded. `positions`: inside a document the position rises by one from each token to the next; one document other than the one of 960 tokens ends at position 65535.
All inputs are finite; a program needn't handle non-finite values.
Results may differ from a plain program's by a relative error of at most 0.012.
The roundings to bfloat16 on the way count: a program that leaves them out, or rounds other values in their place, can miss the bound.
Values may be sent and summed in bfloat16 or wider, within the bound.
No kernel may reach another device: no remote copies, remote signals or barrier semaphores. Data moves between devices by JAX's collectives and lax.ppermute only.
A program may use at most 128 MiB of HBM per device.

v0:
```python
import math

import jax
import jax.numpy as jnp
from jax import lax
from jax.sharding import PartitionSpec as P

HEAD_SIZE = 128


rope_base = 500000.0
yarn_factor = 8.0
trained_context = 8192.0
beta_fast = 32.0
beta_slow = 1.0
norm_epsilon = 1e-05
masked_score = -1e30


def yarn_inverse(head_dim):
    half_dim = head_dim // 2

    def correction(rotations):
        return (
            head_dim
            * math.log(trained_context / (rotations * 2.0 * math.pi))
            / (2.0 * math.log(rope_base))
        )

    lowest = max(math.floor(correction(beta_fast)), 0)
    highest = min(math.ceil(correction(beta_slow)), head_dim - 1)
    spread = max(highest - lowest, 0.001)
    values = []
    for column in range(half_dim):
        extrapolated = rope_base ** (-2.0 * column / head_dim)
        ramp = min(max((column - lowest) / spread, 0.0), 1.0)
        values.append(extrapolated / yarn_factor * ramp + extrapolated * (1.0 - ramp))
    return values


def yarn_tables(positions, head_dim):
    inverse = jnp.asarray(yarn_inverse(head_dim), dtype=jnp.float32)
    attention_gain = 0.1 * math.log(yarn_factor) + 1.0
    angles = positions.astype(jnp.float32)[:, None] * inverse[None, :]
    return (jnp.cos(angles) * attention_gain, jnp.sin(angles) * attention_gain)


def apply_rotation(heads, cosine_table, sine_table):
    half_dim = heads.shape[-1] // 2
    first_half = heads[..., :half_dim]
    second_half = heads[..., half_dim:]
    cos_rows = cosine_table[:, None, :]
    sin_rows = sine_table[:, None, :]
    return jnp.concatenate(
        [
            first_half * cos_rows - second_half * sin_rows,
            second_half * cos_rows + first_half * sin_rows,
        ],
        axis=-1,
    )


def rms_normed(hidden_in, norm_gain):
    widened = hidden_in.astype(jnp.float32)
    power = jnp.mean(widened * widened, axis=-1, keepdims=True)
    return (widened * lax.rsqrt(power + norm_epsilon) * norm_gain).astype(jnp.bfloat16)


def body(hidden_in, norm_gain, w_query, w_key, value_weight, w_out, doc_ids, positions):
    normed = rms_normed(hidden_in, norm_gain)
    block_rows = lax.all_gather(normed, "tensor", axis=0, tiled=True)
    tokens_here = block_rows.shape[0]
    query_width = w_query.shape[1]
    key_width = w_key.shape[1]
    inner_count = lax.axis_size("inner")
    slice_width = w_query.shape[0]
    arranged = block_rows.reshape(tokens_here, inner_count, slice_width)
    received = lax.all_to_all(arranged, "inner", split_axis=1, concat_axis=0, tiled=True)
    received = received.reshape(inner_count * tokens_here, slice_width)
    stacked = jnp.concatenate([w_query, w_key, value_weight], axis=1)
    combined = lax.psum_scatter(
        jnp.dot(received, stacked, preferred_element_type=jnp.float32),
        "inner",
        scatter_dimension=0,
        tiled=True,
    )
    queries = combined[:, :query_width]
    key_matrix = combined[:, query_width : query_width + key_width]
    value_matrix = combined[:, query_width + key_width :]
    value_matrix = value_matrix.astype(jnp.bfloat16)
    heads_query = query_width // HEAD_SIZE
    heads_key = key_width // HEAD_SIZE
    queries_per_group = heads_query // heads_key
    cosine_table, sine_table = yarn_tables(positions, HEAD_SIZE)
    query_rot = (
        apply_rotation(
            queries.reshape(tokens_here, heads_query, HEAD_SIZE), cosine_table, sine_table
        )
        .astype(jnp.bfloat16)
        .reshape(tokens_here, query_width)
    )
    rotated_keys = (
        apply_rotation(
            key_matrix.reshape(tokens_here, heads_key, HEAD_SIZE), cosine_table, sine_table
        )
        .astype(jnp.bfloat16)
        .reshape(tokens_here, key_width)
    )
    documents = lax.all_gather(doc_ids, ("outer", "inner"), axis=0, tiled=True)
    length_all = documents.shape[0]
    block_index = lax.axis_index(("outer", "inner"))
    sequence_index = jnp.arange(length_all, dtype=jnp.int32)
    query_documents = lax.dynamic_slice_in_dim(documents, block_index * tokens_here, tokens_here, 0)
    query_index = lax.dynamic_slice_in_dim(
        sequence_index, block_index * tokens_here, tokens_here, 0
    )
    row_documents = jnp.tile(query_documents, queries_per_group)
    row_index = jnp.tile(query_index, queries_per_group)
    top_index = jnp.max(query_index)
    top_document = jnp.max(query_documents)
    low_document = jnp.min(query_documents)
    grouped_heads = jnp.transpose(
        query_rot.reshape(tokens_here, heads_key, queries_per_group, HEAD_SIZE), (1, 2, 0, 3)
    ).reshape(heads_key, queries_per_group * tokens_here, HEAD_SIZE)
    score_scale = HEAD_SIZE ** (-0.5)

    def key_block(running, block_keys, block_values, first_row):
        row_count = block_keys.shape[0]
        piece_index = lax.dynamic_slice_in_dim(sequence_index, first_row, row_count, 0)
        piece_documents = lax.dynamic_slice_in_dim(documents, first_row, row_count, 0)
        live = (
            (jnp.min(piece_index) <= top_index)
            & (jnp.min(piece_documents) <= top_document)
            & (jnp.max(piece_documents) >= low_document)
        )

        def attend(current):
            row_peaks, totals, summed = current
            heads_keys = block_keys.reshape(row_count, heads_key, HEAD_SIZE)
            heads_values = block_values.reshape(row_count, heads_key, HEAD_SIZE)
            scores = (
                jnp.einsum(
                    "hqd,khd->hqk", grouped_heads, heads_keys, preferred_element_type=jnp.float32
                )
                * score_scale
            )
            allowed = (row_index[:, None] >= piece_index[None, :]) & (
                row_documents[:, None] == piece_documents[None, :]
            )
            scores = jnp.where(allowed[None], scores, masked_score)
            fresh = jnp.maximum(row_peaks, jnp.max(scores, axis=-1))
            weights = jnp.where(allowed[None], jnp.exp(scores - fresh[..., None]), 0.0)
            shrink = jnp.exp(row_peaks - fresh)
            totals = totals * shrink + jnp.sum(weights, axis=-1)
            summed = summed * shrink[..., None] + jnp.einsum(
                "hqk,khd->hqd",
                weights.astype(jnp.bfloat16),
                heads_values,
                preferred_element_type=jnp.float32,
            )
            return (fresh, totals, summed)

        return lax.cond(live, attend, lambda current: current, running)

    initial = (
        jnp.full((heads_key, queries_per_group * tokens_here), masked_score, jnp.float32),
        jnp.zeros((heads_key, queries_per_group * tokens_here), jnp.float32),
        jnp.zeros((heads_key, queries_per_group * tokens_here, HEAD_SIZE), jnp.float32),
    )
    piece_keys = lax.all_gather(rotated_keys, ("outer", "inner"), axis=0, tiled=True)
    piece_values = lax.all_gather(value_matrix, ("outer", "inner"), axis=0, tiled=True)
    row_count = piece_keys.shape[0]
    step_rows = 512
    steps_count = row_count // step_rows
    split_keys = piece_keys.reshape(steps_count, step_rows, key_width)
    split_values = piece_values.reshape(steps_count, step_rows, key_width)
    offsets = jnp.arange(steps_count, dtype=jnp.int32) * step_rows

    def scan_step(current, inputs):
        block_keys, block_values, offset = inputs
        return (key_block(current, block_keys, block_values, offset), None)

    result, unused = lax.scan(scan_step, initial, (split_keys, split_values, offsets))
    row_peaks, totals, summed = result
    heads_out = (summed / totals[..., None]).astype(jnp.bfloat16)
    attended = jnp.transpose(
        heads_out.reshape(heads_key, queries_per_group, tokens_here, HEAD_SIZE), (2, 0, 1, 3)
    ).reshape(tokens_here, query_width)
    full_term = jnp.dot(attended, w_out, preferred_element_type=jnp.float32)
    projected = lax.psum_scatter(
        full_term.astype(jnp.bfloat16), "tensor", scatter_dimension=0, tiled=True
    ).astype(jnp.float32)
    return (hidden_in.astype(jnp.float32) + projected).astype(jnp.bfloat16)


def solution(mesh):
    in_specs = (
        P(("outer", "inner", "tensor"), None),
        P(),
        P("inner", "tensor"),
        P("inner", "tensor"),
        P("inner", "tensor"),
        P("tensor", None),
        P(("outer", "inner")),
        P(("outer", "inner")),
    )
    out_specs = P(("outer", "inner", "tensor"), None)
    return jax.shard_map(body, mesh=mesh, in_specs=in_specs, out_specs=out_specs, check_vma=False)
```

profile of v0, /device:TPU:2, one launch (start us, length us, event | category | flops | bytes accessed | tf_op | source)
XLA Modules:
  0.0 233.2 jit_solution(8369973157437633230)
XLA Ops:
  6.5 1.2 fusion.22
  7.7 1.9 fusion.24
  9.7 38.4 %all-gather.2.cloned.1.call-done = bf16[192,4096]{1,0:T(8,128)(2,1)} async-done(((bf16[48,4096]{1,0:T(8,128)(2,1)}), bf16[192,4096]{1,0:T(8,128)(2,1)}) %all-gather.2.cloned.1.call-update) | async-done | bytes 1572880 | tf_op jit(solution)/shard_map/all_gather | solution.py:71
  48.1 1.7 copy.39
  49.8 22.0 %all_to_all.15 = bf16[192,2,2048]{2,0,1:T(8,128)(2,1)S(1)} all-to-all(bf16[192,2,2048]{2,0,1:T(8,128)(2,1)S(1)} %bitcast.56), channel_id=1, replica_groups=mesh['outer'=4,'inner'=2,'tensor'=4] {'inner'}, dimensions={1} | all-to-all | bytes 3145728 | tf_op jit(solution)/shard_map/all_to_all | solution.py:78
  71.9 4.8 %fusion.16 = f32[384,1536]{1,0:T(8,128)} fusion(bf16[384,2048]{1,0:T(8,128)(2,1)S(1)} %bitcast.60, bf16[2048,256]{1,0:T(8,128)(2,1)S(1)} %copy-done.5, bf16[2048,256]{1,0:T(8,128)(2,1)S(1)} %copy-done.6, bf16[2048,1024]{1,0:T(8,128)(2,1)S(1)} %copy-done.4), kind=kOutput, calls=%fused_computation.18 | convolution fusion | flops 2434793472 | bytes 10223616 | tf_op jit(solution)/shard_map/dot_general | solution.py:82
  78.3 6.6 %all-reduce = s32[1536]{0:T(1024)S(1)} all-reduce(s32[1536]{0:T(1024)S(1)} %dynamic-update-slice), channel_id=1, replica_groups=mesh['outer'=4,'inner'=2,'tensor'=4] {'outer','inner'}, use_global_device_ids=true, to_apply=%add | all-reduce | flops 1536 | bytes 12288
  87.1 22.7 %reduce-scatter.3.cloned.1.call-done = f32[192,1536]{1,0:T(8,128)} async-done(((f32[384,1536]{1,0:T(8,128)}), f32[192,1536]{1,0:T(8,128)}) %reduce-scatter.3.cloned.1.call-update) | async-done | bytes 1179664 | tf_op jit(solution)/shard_map/reduce_scatter | solution.py:81
  109.8 1.2 slice_bitcast_fusion
  112.7 17.5 %all_gather.14 = bf16[1536,256]{1,0:T(8,128)(2,1)S(1)} all-gather(bf16[192,256]{1,0:T(8,128)(2,1)S(1)} %bitcast.65), channel_id=1, replica_groups=mesh['outer'=4,'inner'=2,'tensor'=4] {'outer','inner'}, dimensions={0}, use_global_device_ids=true | all-gather | bytes 884736 | tf_op jit(solution)/shard_map/all_gather | solution.py:170
  130.6 0.9 slice.46
  131.5 18.1 %all_gather.15 = bf16[1536,256]{1,0:T(8,128)(2,1)S(1)} all-gather(bf16[192,256]{1,0:T(8,128)(2,1)S(1)} %slice.46), channel_id=1, replica_groups=mesh['outer'=4,'inner'=2,'tensor'=4] {'outer','inner'}, dimensions={0}, use_global_device_ids=true | all-gather | bytes 884736 | tf_op jit(solution)/shard_map/all_gather | solution.py:171
  150.2 31.1 %while.15 = (s32[]{:T(128)}, f32[2,768]{1,0:T(2,128)S(1)}, f32[2,768]{1,0:T(2,128)S(1)}, f32[2,768,128]{2,1,0:T(8,128)S(1)}, s32[3]{0:T(128)}, /*index=5*/s32[15...) while((s32[]{:T(128)}, f32[2,768]{1,0:T(2,128)S(1)}, ...), condition=%wide.region_13.14_spmd.clone, body=%wide.region_5.13_spmd.clone.sunk | while | flops 414454272 | bytes 14686109 | solution.py:183
  150.2 1.3 dynamic_slice.46
  157.9 3.9 %conditional.3 = ((f32[2,768]{1,0:T(2,128)S(1)}, f32[2,768]{1,0:T(2,128)S(1)}, f32[2,768,128]{2,1,0:T(8,128)S(1)})) conditional(s32[]{:T(128)} %convert_element_type.68, (f32[2,768]{1,0:T(2,128)S(1)}, f32[2,768]{1,0:T(2,128)S(1)}, f32[2,768,128]{2,1,0:T(8,128)S(1)}) %tuple.54, (s32[192]{0:T(256)S(1)}, s32[512]{0:T(512)S(1)}, s32[192]{0:T(256)S(1)}, ...), branch_computations={%region_9.9_spmd, %region_10.12_spmd} | conditional | flops 414452736 | bytes 14677540 | solution.py:163
  160.3 1.5 fusion.10
  161.8 1.3 dynamic_slice.46
  169.6 3.9 %conditional.3 = ((f32[2,768]{1,0:T(2,128)S(1)}, f32[2,768]{1,0:T(2,128)S(1)}, f32[2,768,128]{2,1,0:T(8,128)S(1)})) conditional(s32[]{:T(128)} %convert_element_type.68, (f32[2,768]{1,0:T(2,128)S(1)}, f32[2,768]{1,0:T(2,128)S(1)}, f32[2,768,128]{2,1,0:T(8,128)S(1)}) %tuple.54, (s32[192]{0:T(256)S(1)}, s32[512]{0:T(512)S(1)}, s32[192]{0:T(256)S(1)}, ...), branch_computations={%region_9.9_spmd, %region_10.12_spmd} | conditional | flops 414452736 | bytes 14677540 | solution.py:163
  170.2 0.9 fusion.4
  172.0 1.5 fusion.10
  173.5 1.3 dynamic_slice.46
  182.2 6.4 %convolution_convert_fusion = bf16[192,4096]{1,0:T(8,128)(2,1)} fusion(bf16[192,1024]{1,0:T(8,128)(2,1)S(1)} %reshape.181, bf16[1024,4096]{1,0:T(8,128)(2,1)} %param.18), kind=kOutput, calls=%fused_computation.24 | convolution fusion | flops 1611399168 | bytes 10354688 | tf_op jit(solution)/shard_map/dot_general | solution.py:189
  188.6 36.2 %reduce-scatter.5.cloned.1.call-done = bf16[48,4096]{1,0:T(8,128)(2,1)} async-done(((bf16[192,4096]{1,0:T(8,128)(2,1)}), bf16[48,4096]{1,0:T(8,128)(2,1)}) %reduce-scatter.5.cloned.1.call-update) | async-done | bytes 393232 | tf_op jit(solution)/shard_map/reduce_scatter | solution.py:190
  224.8 1.8 fusion.25
  (76 shorter events, 12.8 us)
Async XLA Ops:
  6.5 41.6 %all-gather.2.cloned.1.call-start = ((), (), s32[]{:S(2)}) async-start(), calls=%async_computation.3 | async-start | bytes 1966080 | tf_op jit(solution)/shard_map/all_gather | solution.py:71
  9.7 100.1 %reduce-scatter.3.cloned.1.call-start = ((), (), s32[]{:S(2)}) async-start(), calls=%async_computation.4 | async-start | bytes 3538944 | tf_op jit(solution)/shard_map/reduce_scatter | solution.py:81
  48.1 23.7 %copy-start.4 = (bf16[2048,1024]{1,0:T(8,128)(2,1)S(1)}, bf16[2048,1024]{1,0:T(8,128)(2,1)}, u32[]{:S(2)}) copy-start(bf16[2048,1024]{1,0:T(8,128)(2,1)} %param.15) | copy-start | bytes 12582916
  48.1 23.7 %copy-start.5 = (bf16[2048,256]{1,0:T(8,128)(2,1)S(1)}, bf16[2048,256]{1,0:T(8,128)(2,1)}, u32[]{:S(2)}) copy-start(bf16[2048,256]{1,0:T(8,128)(2,1)} %param.17) | copy-start | bytes 3145732
  48.1 23.7 %copy-start.6 = (bf16[2048,256]{1,0:T(8,128)(2,1)S(1)}, bf16[2048,256]{1,0:T(8,128)(2,1)}, u32[]{:S(2)}) copy-start(bf16[2048,256]{1,0:T(8,128)(2,1)} %param.16) | copy-start | bytes 3145732
  71.8 4.9 %copy-start.1 = (s32[192]{0:T(256)S(1)}, s32[192]{0:T(256)}, u32[]{:S(2)}) copy-start(s32[192]{0:T(256)} %param.20) | copy-start | bytes 2308
  71.8 5.0 %copy-start.7 = (u32[32]{0:T(128)S(1)}, u32[32]{0:T(128)}, u32[]{:S(2)}) copy-start(u32[32]{0:T(128)} %constant.81) | copy-start | bytes 388
  71.9 6.1 %copy-start.2 = (s32[192]{0:T(256)S(1)}, s32[192]{0:T(256)}, u32[]{:S(2)}) copy-start(s32[192]{0:T(256)} %param.19) | copy-start | bytes 2308
  71.9 14.8 %copy-start.3 = (f32[64]{0:T(128)S(1)}, f32[64]{0:T(128)}, u32[]{:S(2)}) copy-start(f32[64]{0:T(128)} %constant.77.clone) | copy-start | bytes 772
  76.7 148.1 %reduce-scatter.5.cloned.1.call-start = ((), (), s32[]{:S(2)}) async-start(), calls=%async_computation.5 | async-start | bytes 1966080 | tf_op jit(solution)/shard_map/reduce_scatter | solution.py:190
  111.0 0.9 slice-start
  182.1 42.7 %copy-start = (bf16[48,4096]{1,0:T(8,128)(2,1)S(1)}, bf16[48,4096]{1,0:T(8,128)(2,1)}, u32[]{:S(2)}) copy-start(bf16[48,4096]{1,0:T(8,128)(2,1)} %param.13) | copy-start | bytes 1179652
Sparse Core Ops, SparseCore 0:
  9.8 38.3 all-gather.1
  76.8 32.9 reduce-scatter.2
  188.7 36.0 reduce-scatter.4
where the time goes:
time: 237 us; the launch traced here: 233 us
  waiting for transfers between devices  97.4 us (41%)
  blocking collectives  64.2 us (27%)
  loops' own time  17.3 us (7%)
  matrix products  15.9 us (7%)
  between operations  13.9 us (6%)
  other arithmetic  13.6 us (6%)
  local copies, waits for them, and re-layouts  10.7 us (5%)
    all_gather x1, waiting for transfers between devices, body(): block_rows = lax.all_gather(normed, 'tensor', axis=0, tiled=True)  38.4 us
    reduce_scatter x1, waiting for transfers between devices, body(): lax.psum_scatter(full_term.astype(jnp.bfloat16), 'tensor', scatter_dimens...  36.2 us
    reduce_scatter x1, waiting for transfers between devices, body(): lax.psum_scatter(jnp.dot(received, stacked, preferred_element_type=jnp.fl...  22.7 us
    all_to_all x1, blocking collectives, body(): lax.all_to_all(arranged, 'inner', split_axis=1, concat_axis=0, tiled=True)  22 us
    all_gather x1, blocking collectives, body(): lax.all_gather(value_matrix, ('outer', 'inner'), axis=0, tiled=True)  18.1 us
    all_gather x1, blocking collectives, body(): lax.all_gather(rotated_keys, ('outer', 'inner'), axis=0, tiled=True)  17.5 us
    another operation x1, loops' own time, body(): lax.scan(scan_step, initial, (split_keys, split_values, offsets))  17.2 us
    unnamed x1, blocking collectives  6.55 us
  transfers between devices with their start and end apart: 3, of which 3 were waited for; matrix products, arithmetic and copies ran while one was open for 1% of the time, Pallas kernels for 0%

commit v1 on v0

--- a/solution.py
+++ b/solution.py
@@ -3,6 +3,8 @@
 import jax
 import jax.numpy as jnp
 from jax import lax
+from jax.experimental import pallas as pl
+from jax.experimental.pallas import tpu as pltpu
 from jax.sharding import PartitionSpec as P
 
 HEAD_SIZE = 128
@@ -193,6 +195,257 @@
     return (hidden_in.astype(jnp.float32) + projected).astype(jnp.bfloat16)
 
 
+def swap_pairs(axis_size, flip):
+    return [(place, place ^ flip) for place in range(axis_size)]
+
+
+def by_xor(parts, index):
+    count = len(parts)
+    bit = 1
+    while bit < count:
+        parts = [jnp.where((index & bit) != 0, parts[k ^ bit], parts[k]) for k in range(count)]
+        bit *= 2
+    return parts
+
+
+def attention_kernel(
+    live, query_kept, query_came, cosines, sines, query_index, query_start, key_index, pairs,
+    out, peaks, totals, summed,
+):
+    tokens = query_kept.shape[0]
+    heads = query_kept.shape[1] // HEAD_SIZE
+    score_scale = HEAD_SIZE ** (-0.5)
+    step = pl.program_id(0)
+    whole = query_kept[...] + query_came[...]
+    cosine_rows = cosines[...]
+    sine_rows = sines[...]
+    rotated = []
+    for head in range(heads):
+        part = whole[:, head * HEAD_SIZE : (head + 1) * HEAD_SIZE]
+        turned = pltpu.roll(part, HEAD_SIZE // 2, 1)
+        rotated.append((part * cosine_rows + turned * sine_rows).astype(jnp.bfloat16))
+    stacked = jnp.concatenate(rotated, axis=0)
+    row_index = query_index[...]
+    row_start = query_start[...]
+
+    def block_scores(block):
+        keys = pairs[block, :, :HEAD_SIZE]
+        scores = lax.dot_general(
+            stacked, keys, (((1,), (1,)), ((), ())), preferred_element_type=jnp.float32
+        )
+        places = key_index[block]
+        allowed = (places <= row_index) & (places >= row_start)
+        scores = scores.reshape(heads, tokens, -1) * score_scale
+        return jnp.where(allowed[None], scores, masked_score).reshape(heads * tokens, -1)
+
+    def weighted(block, weights):
+        return jnp.dot(
+            weights.astype(jnp.bfloat16), pairs[block, :, HEAD_SIZE:],
+            preferred_element_type=jnp.float32,
+        )
+
+    scores = block_scores(0)
+    peak = jnp.max(scores, axis=-1, keepdims=True)
+    weights = jnp.exp(scores - peak)
+    peaks[...] = peak
+    totals[...] = jnp.sum(weights, axis=-1, keepdims=True)
+    summed[...] = weighted(0, weights)
+    for block in range(1, pairs.shape[0]):
+
+        @pl.when(live[step, block] != 0)
+        def _():
+            scores = block_scores(block)
+            before = peaks[...]
+            peak = jnp.maximum(before, jnp.max(scores, axis=-1, keepdims=True))
+            weights = jnp.exp(scores - peak)
+            shrink = jnp.exp(before - peak)
+            peaks[...] = peak
+            totals[...] = totals[...] * shrink + jnp.sum(weights, axis=-1, keepdims=True)
+            summed[...] = summed[...] * shrink + weighted(block, weights)
+
+    result = (summed[...] / totals[...]).astype(jnp.bfloat16)
+    for head in range(heads):
+        out[:, head * HEAD_SIZE : (head + 1) * HEAD_SIZE] = result[head * tokens : (head + 1) * tokens]
+
+
+def attend_rows(
+    tokens, live, query_kept, query_came, cosines, sines, query_index, query_start, key_index, pairs
+):
+    rows, width = query_kept.shape
+    heads = width // HEAD_SIZE
+    row_block = lambda wide: pl.BlockSpec((tokens, wide), lambda step, live: (step, 0))
+    whole_block = lambda array: pl.BlockSpec(array.shape, lambda step, live: (0, 0, 0))
+    keys_count = pairs.shape[0] * pairs.shape[1]
+    return pl.pallas_call(
+        attention_kernel,
+        grid_spec=pltpu.PrefetchScalarGridSpec(
+            num_scalar_prefetch=1,
+            grid=(rows // tokens,),
+            in_specs=[
+                row_block(width), row_block(width), row_block(HEAD_SIZE), row_block(HEAD_SIZE),
+                row_block(1), row_block(1), whole_block(key_index), whole_block(pairs),
+            ],
+            out_specs=row_block(width),
+            scratch_shapes=[
+                pltpu.VMEM((heads * tokens, 1), jnp.float32),
+                pltpu.VMEM((heads * tokens, 1), jnp.float32),
+                pltpu.VMEM((heads * tokens, HEAD_SIZE), jnp.float32),
+            ],
+        ),
+        out_shape=jax.ShapeDtypeStruct((rows, width), jnp.bfloat16),
+        compiler_params=pltpu.CompilerParams(vmem_limit_bytes=24 * 1024 * 1024),
+        cost_estimate=pl.CostEstimate(
+            flops=4 * rows * heads * keys_count * HEAD_SIZE,
+            bytes_accessed=2 * keys_count * 2 * HEAD_SIZE + 10 * rows * width,
+            transcendentals=rows * heads * keys_count,
+        ),
+    )(live, query_kept, query_came, cosines, sines, query_index, query_start, key_index, pairs)
+
+
+def short_body(hidden_in, norm_gain, w_query, w_key, value_weight, w_out, doc_ids, positions):
+    place_outer = lax.axis_index("outer")
+    place_inner = lax.axis_index("inner")
+    place_tensor = lax.axis_index("tensor")
+    outer_count = lax.axis_size("outer")
+    rows = hidden_in.shape[0]
+    half_width = w_query.shape[0]
+    query_half = w_query.shape[1] // 2
+    key_half = w_key.shape[1] // 2
+    block_rows = doc_ids.shape[0]
+    across_inner = swap_pairs(2, 1)
+
+    def send(value, axis, pairs):
+        return lax.ppermute(value, axis, pairs)
+
+    normed = rms_normed(hidden_in, norm_gain)
+    first, second = normed[:, :half_width], normed[:, half_width:]
+    lower = place_inner == 0
+    mine = jnp.where(lower, first, second)
+    others = jnp.where(lower, second, first)
+    theirs = send(others, "inner", across_inner)
+
+    def gather_rows(chunk):
+        two = send(chunk, "tensor", swap_pairs(4, 2))
+        one = send(chunk, "tensor", swap_pairs(4, 1))
+        middle = send(chunk, "tensor", [(1, 2), (2, 1)])
+        ends = send(two, "tensor", [(1, 0), (2, 3)])
+        return [chunk, one, two, middle + ends]
+
+    slots = list(zip(gather_rows(mine), gather_rows(theirs)))
+
+    facts = jnp.stack([doc_ids, positions])
+    facts = jnp.stack([facts, send(facts, "inner", across_inner)])
+    documents = facts[:, 0]
+    bit = 1
+    all_documents = documents.reshape(-1)
+    while bit < outer_count:
+        came = send(all_documents, "outer", swap_pairs(outer_count, bit))
+        all_documents = jnp.concatenate([all_documents, came])
+        bit *= 2
+
+    def relative(parts):
+        pieces = [parts[:, k * rows : (k + 1) * rows] for k in range(4)]
+        return jnp.stack(by_xor(pieces, place_tensor)).reshape(-1)
+
+    row_documents = relative(documents)
+    row_positions = relative(facts[:, 1])
+    starts = jnp.sum((all_documents[None, :] < row_documents[:, None]).astype(jnp.int32), axis=1)
+    slot_number = jnp.arange(4, dtype=jnp.int32)[:, None, None]
+    part_number = jnp.arange(2, dtype=jnp.int32)[None, :, None]
+    row_number = jnp.arange(rows, dtype=jnp.int32)[None, None, :]
+    inside = (
+        (place_inner ^ part_number) * block_rows + (place_tensor ^ slot_number) * rows + row_number
+    ).reshape(-1)
+    outer_rows = 2 * block_rows
+    blocks = place_outer ^ jnp.arange(outer_count, dtype=jnp.int32)
+    row_index = place_outer * outer_rows + inside
+    key_index = (blocks[:, None] * outer_rows + inside[None, :])[:, None, :]
+    slot_rows = 2 * rows
+    earliest = jnp.min(starts.reshape(4, slot_rows), axis=1)
+    live = (
+        (blocks[None, :] <= place_outer) & ((blocks[None, :] + 1) * outer_rows > earliest[:, None])
+    ).astype(jnp.int32)
+    inverse = jnp.asarray(yarn_inverse(HEAD_SIZE) * 2, dtype=jnp.float32)
+    signs = jnp.asarray([-1.0] * (HEAD_SIZE // 2) + [1.0] * (HEAD_SIZE // 2), dtype=jnp.float32)
+    attention_gain = 0.1 * math.log(yarn_factor) + 1.0
+    angles = row_positions.astype(jnp.float32)[:, None] * inverse[None, :]
+    cosines = jnp.cos(angles) * attention_gain
+    sines = jnp.sin(angles) * attention_gain * signs
+
+    def columns(weight, width, which):
+        return lax.dynamic_slice_in_dim(weight, which * width, width, 1)
+
+    def split_weights(which):
+        pair = [columns(w_key, key_half, which), columns(value_weight, key_half, which)]
+        return jnp.concatenate(pair, axis=1), columns(w_query, query_half, which)
+
+    pair_kept, query_kept_weight = split_weights(place_inner)
+    pair_sent, query_sent_weight = split_weights(1 - place_inner)
+
+    def product(left, right):
+        return jnp.dot(left, right, preferred_element_type=jnp.float32)
+
+    def project(group):
+        straight = jnp.concatenate([chunk for slot in group for chunk in slot])
+        flipped = jnp.concatenate([chunk for slot in group for chunk in slot[::-1]])
+        pair_came = send(product(flipped, pair_sent), "inner", across_inner)
+        query_came = send(product(flipped, query_sent_weight), "inner", across_inner)
+        pair = product(straight, pair_kept) + pair_came
+        return pair, product(straight, query_kept_weight), query_came
+
+    def rotate_keys(pair, first_row):
+        count = pair.shape[0]
+        keys, values = pair[:, :HEAD_SIZE], pair[:, HEAD_SIZE:]
+        half = HEAD_SIZE // 2
+        turned = jnp.concatenate([keys[:, half:], keys[:, :half]], axis=1)
+        cosine_rows = cosines[first_row : first_row + count]
+        sine_rows = sines[first_row : first_row + count]
+        keys = keys * cosine_rows + turned * sine_rows
+        return jnp.concatenate([keys, values], axis=1).astype(jnp.bfloat16)
+
+    def gather_pairs(pair):
+        found = [pair]
+        for flip in range(1, outer_count):
+            found.append(send(pair, "outer", swap_pairs(outer_count, flip)))
+        return jnp.stack(found)
+
+    pair_01, query_kept_01, query_came_01 = project(slots[:2])
+    pair_2, query_kept_2, query_came_2 = project(slots[2:3])
+    pair_3, query_kept_3, query_came_3 = project(slots[3:])
+    early = gather_pairs(rotate_keys(jnp.concatenate([pair_01, pair_2]), 0))
+    late = gather_pairs(rotate_keys(pair_3, 3 * slot_rows))
+    pairs = jnp.concatenate([early, late], axis=1)
+
+    def attend(slot, count, query_kept, query_came):
+        rows_of = lambda array: array[slot * slot_rows : (slot + count) * slot_rows]
+        return attend_rows(
+            slot_rows, live[slot : slot + count], query_kept, query_came,
+            rows_of(cosines), rows_of(sines),
+            rows_of(row_index)[:, None], rows_of(starts)[:, None], key_index, pairs,
+        )
+
+    def projected(attended):
+        count = attended.shape[0] // slot_rows
+        parts = attended.reshape(count, 2, rows, attended.shape[1])
+        here = parts[:, 0].reshape(count * rows, -1)
+        came = send(parts[:, 1].reshape(count * rows, -1), "inner", across_inner)
+        joined = jnp.concatenate(
+            [jnp.where(lower, here, came), jnp.where(lower, came, here)], axis=1
+        )
+        return product(joined, w_out)
+
+    term_3 = projected(attend(3, 1, query_kept_3, query_came_3)).astype(jnp.bfloat16)
+    inward = send(term_3, "tensor", [(0, 1), (3, 2)])
+    middle = send(term_3, "tensor", [(1, 2), (2, 1)])
+    term_2 = projected(attend(2, 1, query_kept_2, query_came_2)) + inward.astype(jnp.float32)
+    came_2 = send(term_2.astype(jnp.bfloat16), "tensor", swap_pairs(4, 2))
+    terms = projected(attend(0, 2, query_kept_01, query_came_01))
+    came_1 = send(terms[rows:].astype(jnp.bfloat16), "tensor", swap_pairs(4, 1))
+    total = terms[:rows] + came_1.astype(jnp.float32)
+    total = total + middle.astype(jnp.float32) + came_2.astype(jnp.float32)
+    return (hidden_in.astype(jnp.float32) + total).astype(jnp.bfloat16)
+
+
 def solution(mesh):
     in_specs = (
         P(("outer", "inner", "tensor"), None),
@@ -205,4 +458,22 @@
         P(("outer", "inner")),
     )
     out_specs = P(("outer", "inner", "tensor"), None)
-    return jax.shard_map(body, mesh=mesh, in_specs=in_specs, out_specs=out_specs, check_vma=False)
+
+    def chosen(*arrays):
+        outer_count = mesh.shape["outer"]
+        key_heads = arrays[3].shape[1] // HEAD_SIZE // mesh.shape["tensor"]
+        short = (
+            mesh.shape["tensor"] == 4
+            and mesh.shape["inner"] == 2
+            and key_heads == 2
+            and outer_count & (outer_count - 1) == 0
+            and arrays[0].shape[0] % (mesh.size * 16) == 0
+            and arrays[0].shape[0] // outer_count <= 512
+        )
+        mapped = jax.shard_map(
+            short_body if short else body,
+            mesh=mesh, in_specs=in_specs, out_specs=out_specs, check_vma=False,
+        )
+        return mapped(*arrays)
+
+    return chosen

time: 237 us -> 121 us (0.51); the launches traced: 233 us -> 122 us
  blocking collectives: 64.2 us -> 0 us
  waiting for transfers between devices: 97.4 us -> 49.3 us
  starting transfers between devices: 0.09 us -> 35.8 us
  loops' own time: 17.3 us -> 0 us
  between operations: 13.9 us -> 0.58 us
  Pallas kernels: 0 us -> 10.9 us
  local copies, waits for them, and re-layouts: 10.7 us -> 3.78 us
  other arithmetic: 13.6 us -> 7.18 us
    reduce_scatter x2 -> x0, waiting for transfers between devices: 58.9 us -> none  [the longest x1 36.2 us: body(): lax.psum_scatter(full_term.astype(jnp.bfloat16), 'tensor', scatter_dimens...]
    ppermute x0 -> x31, waiting for transfers between devices: none -> 49.3 us  [send(): return lax.ppermute(value, axis, pairs)]
    all_gather x1 -> x0, waiting for transfers between devices: 38.4 us -> none  [body(): block_rows = lax.all_gather(normed, 'tensor', axis=0, tiled=True)]
    ppermute x0 -> x31, starting transfers between devices: none -> 35.8 us  [send(): return lax.ppermute(value, axis, pairs)]
    all_gather x2 -> x0, blocking collectives: 35.6 us -> none  [the longest x1 18.1 us: body(): lax.all_gather(value_matrix, ('outer', 'inner'), axis=0, tiled=True)]
    all_to_all x1 -> x0, blocking collectives: 22 us -> none  [body(): lax.all_to_all(arranged, 'inner', split_axis=1, concat_axis=0, tiled=True)]
    another operation x4 -> x0, loops' own time: 17.3 us -> none  [the longest x1 17.2 us: body(): lax.scan(scan_step, initial, (split_keys, split_values, offsets))]
    pallas_call x0 -> x3, Pallas kernels: none -> 10.9 us  [attend_rows(): pl.pallas_call(attention_kernel, grid_spec=pltpu.PrefetchScalarGridSpec(n...]
  transfers between devices with their start and end apart: 3 -> 31, of which waited for: 3 -> 12; matrix products, arithmetic and copies ran while one was open for 1% -> 17% of each run, Pallas kernels for 0% -> 9%
where the time goes in v1:
time: 121 us; the launch traced here: 122 us
  waiting for transfers between devices  49.3 us (41%)
  starting transfers between devices  35.8 us (30%)
  matrix products  14.2 us (12%)
  Pallas kernels  10.9 us (9%)
  other arithmetic  7.18 us (6%)
  local copies, waits for them, and re-layouts  3.78 us (3%)
    ppermute x31, waiting for transfers between devices, send(): return lax.ppermute(value, axis, pairs)  49.3 us
    ppermute x31, starting transfers between devices, send(): return lax.ppermute(value, axis, pairs)  35.8 us
    dot_general x15, matrix products, product(): return jnp.dot(left, right, preferred_element_type=jnp.float32)  14.2 us
    pallas_call x3, Pallas kernels, attend_rows(): pl.pallas_call(attention_kernel, grid_spec=pltpu.PrefetchScalarGridSpec(n...  10.9 us
  transfers between devices with their start and end apart: 31, of which 12 were waited for; matrix products, arithmetic and copies ran while one was open for 17% of the time, Pallas kernels for 9%

profile of v1, /device:TPU:2, one launch (start us, length us, event | category | flops | bytes accessed | tf_op | source)
XLA Modules:
  0.0 121.7 jit_solution(1017739059187624332)
XLA Ops:
  3.2 1.6 %collective-permute-start.4 = (bf16[48,2048]{1,0:T(8,128)(2,1)S(1)}, bf16[48,2048]{1,0:T(8,128)(2,1)}, u32[]{:S(2)}, u32[]{:S(2)}) collective-permute-start(bf16[48,2048]{1,0:T(8,128)(2,1)S(1)} %get-tuple-element.9), channel_id=1, source_target_pairs={{0,1},{1,0},{2,3},{3,2},{4,5},{5,4},{6,7},{7,6},{8,9},{9,8},{10,11... | collective-permute-start | bytes 589832 | tf_op jit(solution)/shard_map/ppermute | solution.py:318
  4.7 2.6 %collective-permute-start.8 = (bf16[48,2048]{1,0:T(8,128)(2,1)S(1)}, bf16[48,2048]{1,0:T(8,128)(2,1)S(1)}, u32[]{:S(2)}, u32[]{:S(2)}) collective-permute-start(bf16[48,2048]{1,0:T(8,128)(2,1)S(1)} %get-tuple-element.9), channel_id=1, source_target_pairs={{0,2},{1,3},{2,0},{3,1},{4,6},{5,7},{6,4},{7,5},{8,10},{9,11},{10,... | collective-permute-start | bytes 589832 | tf_op jit(solution)/shard_map/ppermute | solution.py:318
  8.0 1.6 %collective-permute-start.3 = (bf16[48,2048]{1,0:T(8,128)(2,1)}, bf16[48,2048]{1,0:T(8,128)(2,1)}, u32[]{:S(2)}, u32[]{:S(2)}) collective-permute-start(bf16[48,2048]{1,0:T(8,128)(2,1)} %get-tuple-element.10), channel_id=1, source_target_pairs={{0,4},{4,0},{1,5},{5,1},{2,6},{6,2},{3,7},{7,3},{8,12},{12,8},{9,1... | collective-permute-start | bytes 589832 | tf_op jit(solution)/shard_map/ppermute | solution.py:318
  11.3 2.3 %constant_dynamic-slice_fusion.2 = (bf16[2048,128]{1,0:T(8,128)(2,1)S(1)}, bf16[2048,128]{1,0:T(8,128)(2,1)S(1)}, bf16[2048,128]{1,0:T(8,128)(2,1)}, bf16[2048,128]{1,0:T(8,128)(2,1)S(1)}) fusion(bf16[2048,256]{1,0:T(8,128)(2,1)S(1)} %copy-done.2, s32[]{:T(128)S(6)} %select_n.152, s32[]{:T(128)S(6)} %select_n.153, bf16[2048,256]{1,0:T(8,128)(2,1)} %param.13), kind=kLoop, calls=%fused_computation.111 | loop fusion | bytes 4194312 | tf_op jit(solution)/shard_map/dynamic_slice | solution.py:376
  16.6 3.0 %collective-permute-done.2 = s32[768]{0:T(1024)S(1)} collective-permute-done((s32[768]{0:T(1024)S(1)}, s32[768]{0:T(1024)S(1)}, u32[]{:S(2)}, u32[]{:S(2)}) %collective-permute-start.2) | collective-permute-done | bytes 3104 | tf_op jit(solution)/shard_map/ppermute | solution.py:318
  20.6 1.9 %collective-permute-start.5 = (bf16[48,2048]{1,0:T(8,128)(2,1)}, bf16[48,2048]{1,0:T(8,128)(2,1)S(1)}, u32[]{:S(2)}, u32[]{:S(2)}) collective-permute-start(bf16[48,2048]{1,0:T(8,128)(2,1)} %collective-permute-done.3), channel_id=1, source_target_pairs={{0,1},{1,0},{2,3},{3,2},{4,5},{5,4},{6,7},{7,6},{8,9},{9,8},{10,11... | collective-permute-start | bytes 589832 | tf_op jit(solution)/shard_map/ppermute | solution.py:318
  25.7 7.1 %collective-permute-done.5 = bf16[48,2048]{1,0:T(8,128)(2,1)S(1)} collective-permute-done((bf16[48,2048]{1,0:T(8,128)(2,1)}, bf16[48,2048]{1,0:T(8,128)(2,1)S(1)}, u32[]{:S(2)}, u32[]{:S(2)}) %collective-permute-start.5) | collective-permute-done | bytes 196640 | tf_op jit(solution)/shard_map/ppermute | solution.py:318
  32.7 1.8 %fusion.21 = f32[192,256]{1,0:T(8,128)S(1)} fusion(bf16[2048,128]{1,0:T(8,128)(2,1)S(1)} %get-tuple-element.8, bf16[2048,128]{1,0:T(8,128)(2,1)} %get-tuple-element.50, bf16[48,2048]{1,0:T(8,128)(2,1)} %collective-permute-done.4, bf16[48,2048]{1,0:T(8,128)(2,1)S(1)} %collective-permute-done.5, bf16[48,2048]{1,0:T(8,128)(2,1)S(1)} %get-tuple-element.9, ...), kind=kOutput, calls=%fused_computation.45 | convolution fusion | flops 206569472 | bytes 2031616 | tf_op jit(solution)/shard_map/dot_general | solution.py:386
  34.5 1.6 %collective-permute-start.7 = (f32[192,256]{1,0:T(8,128)S(1)}, f32[192,256]{1,0:T(8,128)S(1)}, u32[]{:S(2)}, u32[]{:S(2)}) collective-permute-start(f32[192,256]{1,0:T(8,128)S(1)} %fusion.21), channel_id=1, source_target_pairs={{0,4},{4,0},{1,5},{5,1},{2,6},{6,2},{3,7},{7,3},{8,12},{12,8},{9,1... | collective-permute-start | bytes 589832 | tf_op jit(solution)/shard_map/ppermute | solution.py:318
  37.5 1.6 %fusion.5 = f32[192,512]{1,0:T(8,128)S(1)} fusion(bf16[2048,1024]{1,0:T(8,128)(2,1)S(1)} %copy-done, s32[]{:T(128)S(6)} %select_n.143, bf16[48,2048]{1,0:T(8,128)(2,1)} %collective-permute-done.4, bf16[48,2048]{1,0:T(8,128)(2,1)S(1)} %collective-permute-done.5, bf16[48,2048]{1,0:T(8,128)(2,1)S(1)} %get-tuple-element.9, ...), kind=kOutput, calls=%fused_computation.8 | convolution fusion | flops 405798912 | bytes 3276804 | tf_op jit(solution)/shard_map/dot_general | solution.py:386
  39.6 1.6 %collective-permute-start.27 = (f32[96,512]{1,0:T(8,128)S(1)}, f32[96,512]{1,0:T(8,128)S(1)}, u32[]{:S(2)}, u32[]{:S(2)}) collective-permute-start(f32[96,512]{1,0:T(8,128)S(1)} %fusion.1), channel_id=1, source_target_pairs={{0,4},{4,0},{1,5},{5,1},{2,6},{6,2},{3,7},{7,3},{8,12},{12,8},{9,1... | collective-permute-start | bytes 589832 | tf_op jit(solution)/shard_map/ppermute | solution.py:318
  42.6 1.6 %fusion.11.query_kept = f32[192,512]{1,0:T(8,128)S(1)} fusion(bf16[2048,1024]{1,0:T(8,128)(2,1)S(1)} %copy-done, s32[]{:T(128)S(6)} %select_n.142, bf16[48,2048]{1,0:T(8,128)(2,1)S(1)} %collective-permute-done.5, bf16[48,2048]{1,0:T(8,128)(2,1)} %collective-permute-done.4, bf16[48,2048]{1,0:T(8,128)(2,1)} %collective-permute-done.3, ...), kind=kOutput, calls=%fused_computation.14 | convolution fusion | flops 405798912 | bytes 3276804 | tf_op jit(solution)/shard_map/dot_general | solution.py:386
  50.7 3.6 %collective-permute-done.18 = f32[96,256]{1,0:T(8,128)S(1)} collective-permute-done((f32[96,256]{1,0:T(8,128)S(1)}, f32[96,256]{1,0:T(8,128)S(1)}, u32[]{:S(2)}, u32[]{:S(2)}) %collective-permute-start.18) | collective-permute-done | bytes 98336 | tf_op jit(solution)/shard_map/ppermute | solution.py:318
  59.8 2.8 %shard_map.102 = bf16[96,512]{1,0:T(8,128)(2,1)S(1)} custom-call(s32[1,4]{1,0:T(1,128)S(1)} %get-tuple-element.38.live, f32[96,512]{1,0:T(8,128)S(1)} %fusion.7.query_kept, f32[96,512]{1,0:T(8,128)S(1)} %collective-permute-done.27.query_came, f32[96,128]{1,0:T(8,128)S(1)} %get-tuple-element.15.cosines, f32[96,128]{1,0:T(8,128)S(1)} %get-tuple-element.13.sines, ...), custom_call_target="tpu_custom_call" | custom-call | flops 301989888 | bytes 1277952 | tf_op jit(solution)/shard_map/pallas_call | solution.py:279
  63.2 9.8 %collective-permute-done.24.query_came = f32[96,512]{1,0:T(8,128)S(1)} collective-permute-done((f32[96,512]{1,0:T(8,128)S(1)}, f32[96,512]{1,0:T(8,128)S(1)}, u32[]{:S(2)}, u32[]{:S(2)}) %collective-permute-start.24) | collective-permute-done | bytes 196640 | tf_op jit(solution)/shard_map/ppermute | solution.py:318
  73.0 3.0 %shard_map.101 = bf16[96,512]{1,0:T(8,128)(2,1)S(1)} custom-call(s32[1,4]{1,0:T(1,128)S(1)} %get-tuple-element.39.live, f32[96,512]{1,0:T(8,128)S(1)} %fusion.9.query_kept, f32[96,512]{1,0:T(8,128)S(1)} %collective-permute-done.24.query_came, f32[96,128]{1,0:T(8,128)S(1)} %get-tuple-element.16.cosines, f32[96,128]{1,0:T(8,128)S(1)} %get-tuple-element.17.sines, ...), custom_call_target="tpu_custom_call" | custom-call | flops 301989888 | bytes 1277952 | tf_op jit(solution)/shard_map/pallas_call | solution.py:279
  76.6 5.1 %shard_map.100 = bf16[192,512]{1,0:T(8,128)(2,1)S(1)} custom-call(s32[2,4]{1,0:T(2,128)S(1)} %slice.147.live, f32[192,512]{1,0:T(8,128)S(1)} %fusion.11.query_kept, f32[192,512]{1,0:T(8,128)S(1)} %collective-permute-done.6.query_came, f32[192,128]{1,0:T(8,128)S(1)} %slice.199.cosines, f32[192,128]{1,0:T(8,128)S(1)} %slice.200.sines, ...), custom_call_target="tpu_custom_call" | custom-call | flops 603979776 | bytes 1769472 | tf_op jit(solution)/shard_map/pallas_call | solution.py:279
  81.7 1.6 %collective-permute-start.22 = (bf16[96,512]{1,0:T(8,128)(2,1)S(1)}, bf16[96,512]{1,0:T(8,128)(2,1)S(1)}, u32[]{:S(2)}, u32[]{:S(2)}) collective-permute-start(bf16[96,512]{1,0:T(8,128)(2,1)S(1)} %bitcast.89), channel_id=1, source_target_pairs={{0,4},{4,0},{1,5},{5,1},{2,6},{6,2},{3,7},{7,3},{8,12},{12,8},{9,1... | collective-permute-start | bytes 294920 | tf_op jit(solution)/shard_map/ppermute | solution.py:318
  83.4 1.6 %convolution_convert_fusion = bf16[48,4096]{1,0:T(8,128)(2,1)S(1)} fusion(bf16[1024,4096]{1,0:T(8,128)(2,1)S(1)} %bitcast.82, bf16[48,512]{1,0:T(8,128)(2,1)S(1)} %get-tuple-element.27, bf16[48,512]{1,0:T(8,128)(2,1)S(1)} %get-tuple-element.26), kind=kOutput, calls=%fused_computation.2 | convolution fusion | flops 403046400 | bytes 8880128 | tf_op jit(solution)/shard_map/dot_general | solution.py:386
  85.0 4.4 %collective-permute-start.29 = (bf16[48,4096]{1,0:T(8,128)(2,1)S(1)}, bf16[48,4096]{1,0:T(8,128)(2,1)S(1)}, u32[]{:S(2)}, u32[]{:S(2)}) collective-permute-start(bf16[48,4096]{1,0:T(8,128)(2,1)S(1)} %convolution_convert_fusion), channel_id=1, source_target_pairs={{0,1},{3,2},{4,5},{7,6},{8,9},{11,10},{12,13},{15,14},{16,17},{19,... | collective-permute-start | bytes 1179656 | tf_op jit(solution)/shard_map/ppermute | solution.py:318
  93.1 5.7 %collective-permute-done.29 = bf16[48,4096]{1,0:T(8,128)(2,1)S(1)} collective-permute-done((bf16[48,4096]{1,0:T(8,128)(2,1)S(1)}, bf16[48,4096]{1,0:T(8,128)(2,1)S(1)}, u32[]{:S(2)}, u32[]{:S(2)}) %collective-permute-start.29) | collective-permute-done | bytes 393248 | tf_op jit(solution)/shard_map/ppermute | solution.py:318
  100.4 2.5 %collective-permute-start.30 = (bf16[48,4096]{1,0:T(8,128)(2,1)S(1)}, bf16[48,4096]{1,0:T(8,128)(2,1)S(1)}, u32[]{:S(2)}, u32[]{:S(2)}) collective-permute-start(bf16[48,4096]{1,0:T(8,128)(2,1)S(1)} %fusion), channel_id=1, source_target_pairs={{0,2},{1,3},{2,0},{3,1},{4,6},{5,7},{6,4},{7,5},{8,10},{9,11},{10,... | collective-permute-start | bytes 1179656 | tf_op jit(solution)/shard_map/ppermute | solution.py:318
  102.9 4.4 %collective-permute-done.23 = bf16[48,4096]{1,0:T(8,128)(2,1)S(1)} collective-permute-done((bf16[48,4096]{1,0:T(8,128)(2,1)S(1)}, bf16[48,4096]{1,0:T(8,128)(2,1)S(1)}, u32[]{:S(2)}, u32[]{:S(2)}) %collective-permute-start.23) | collective-permute-done | bytes 393248 | tf_op jit(solution)/shard_map/ppermute | solution.py:318
  107.3 13.5 %collective-permute-done.30 = bf16[48,4096]{1,0:T(8,128)(2,1)S(1)} collective-permute-done((bf16[48,4096]{1,0:T(8,128)(2,1)S(1)}, bf16[48,4096]{1,0:T(8,128)(2,1)S(1)}, u32[]{:S(2)}, u32[]{:S(2)}) %collective-permute-start.30) | collective-permute-done | bytes 393248 | tf_op jit(solution)/shard_map/ppermute | solution.py:318
  (143 shorter events, 35.1 us)
Async XLA Ops:
  3.2 21.8 %collective-permute-start.4 = (bf16[48,2048]{1,0:T(8,128)(2,1)S(1)}, bf16[48,2048]{1,0:T(8,128)(2,1)}, u32[]{:S(2)}, u32[]{:S(2)}) collective-permute-start(bf16[48,2048]{1,0:T(8,128)(2,1)S(1)} %get-tuple-element.9), channel_id=1, source_target_pairs={{0,1},{1,0},{2,3},{3,2},{4,5},{5,4},{6,7},{7,6},{8,9},{9,8},{10,11... | collective-permute-start | bytes 589832 | tf_op jit(solution)/shard_map/ppermute | solution.py:318
  4.7 18.9 %collective-permute-start.8 = (bf16[48,2048]{1,0:T(8,128)(2,1)S(1)}, bf16[48,2048]{1,0:T(8,128)(2,1)S(1)}, u32[]{:S(2)}, u32[]{:S(2)}) collective-permute-start(bf16[48,2048]{1,0:T(8,128)(2,1)S(1)} %get-tuple-element.9), channel_id=1, source_target_pairs={{0,2},{1,3},{2,0},{3,1},{4,6},{5,7},{6,4},{7,5},{8,10},{9,11},{10,... | collective-permute-start | bytes 589832 | tf_op jit(solution)/shard_map/ppermute | solution.py:318
  7.3 32.3 %collective-permute-start.14 = (bf16[48,2048]{1,0:T(8,128)(2,1)S(1)}, bf16[48,2048]{1,0:T(8,128)(2,1)S(1)}, u32[]{:S(2)}, u32[]{:S(2)}) collective-permute-start(bf16[48,2048]{1,0:T(8,128)(2,1)S(1)} %get-tuple-element.9), channel_id=1, source_target_pairs={{1,2},{2,1},{5,6},{6,5},{9,10},{10,9},{13,14},{14,13},{17,18},{18,... | collective-permute-start | bytes 589832 | tf_op jit(solution)/shard_map/ppermute | solution.py:318
  8.0 12.6 %collective-permute-start.3 = (bf16[48,2048]{1,0:T(8,128)(2,1)}, bf16[48,2048]{1,0:T(8,128)(2,1)}, u32[]{:S(2)}, u32[]{:S(2)}) collective-permute-start(bf16[48,2048]{1,0:T(8,128)(2,1)} %get-tuple-element.10), channel_id=1, source_target_pairs={{0,4},{4,0},{1,5},{5,1},{2,6},{6,2},{3,7},{7,3},{8,12},{12,8},{9,1... | collective-permute-start | bytes 589832 | tf_op jit(solution)/shard_map/ppermute | solution.py:318
  20.6 12.1 %collective-permute-start.5 = (bf16[48,2048]{1,0:T(8,128)(2,1)}, bf16[48,2048]{1,0:T(8,128)(2,1)S(1)}, u32[]{:S(2)}, u32[]{:S(2)}) collective-permute-start(bf16[48,2048]{1,0:T(8,128)(2,1)} %collective-permute-done.3), channel_id=1, source_target_pairs={{0,1},{1,0},{2,3},{3,2},{4,5},{5,4},{6,7},{7,6},{8,9},{9,8},{10,11... | collective-permute-start | bytes 589832 | tf_op jit(solution)/shard_map/ppermute | solution.py:318
  22.6 13.5 %collective-permute-start.9 = (bf16[48,2048]{1,0:T(8,128)(2,1)}, bf16[48,2048]{1,0:T(8,128)(2,1)S(1)}, u32[]{:S(2)}, u32[]{:S(2)}) collective-permute-start(bf16[48,2048]{1,0:T(8,128)(2,1)} %collective-permute-done.3), channel_id=1, source_target_pairs={{0,2},{1,3},{2,0},{3,1},{4,6},{5,7},{6,4},{7,5},{8,10},{9,11},{10,... | collective-permute-start | bytes 589832 | tf_op jit(solution)/shard_map/ppermute | solution.py:318
  23.7 17.5 %collective-permute-start.15 = (bf16[48,2048]{1,0:T(8,128)(2,1)S(1)}, bf16[48,2048]{1,0:T(8,128)(2,1)S(1)}, u32[]{:S(2)}, u32[]{:S(2)}) collective-permute-start(bf16[48,2048]{1,0:T(8,128)(2,1)S(1)} %collective-permute-done.8), channel_id=1, source_target_pairs={{1,0},{2,3},{5,4},{6,7},{9,8},{10,11},{13,12},{14,15},{17,16},{18,... | collective-permute-start | bytes 589832 | tf_op jit(solution)/shard_map/ppermute | solution.py:318
  25.0 21.9 %collective-permute-start.16 = (bf16[48,2048]{1,0:T(8,128)(2,1)}, bf16[48,2048]{1,0:T(8,128)(2,1)S(1)}, u32[]{:S(2)}, u32[]{:S(2)}) collective-permute-start(bf16[48,2048]{1,0:T(8,128)(2,1)} %collective-permute-done.3), channel_id=1, source_target_pairs={{1,2},{2,1},{5,6},{6,5},{9,10},{10,9},{13,14},{14,13},{17,18},{18,... | collective-permute-start | bytes 589832 | tf_op jit(solution)/shard_map/ppermute | solution.py:318
  34.5 10.0 %collective-permute-start.7 = (f32[192,256]{1,0:T(8,128)S(1)}, f32[192,256]{1,0:T(8,128)S(1)}, u32[]{:S(2)}, u32[]{:S(2)}) collective-permute-start(f32[192,256]{1,0:T(8,128)S(1)} %fusion.21), channel_id=1, source_target_pairs={{0,4},{4,0},{1,5},{5,1},{2,6},{6,2},{3,7},{7,3},{8,12},{12,8},{9,1... | collective-permute-start | bytes 589832 | tf_op jit(solution)/shard_map/ppermute | solution.py:318
  36.5 7.7 %collective-permute-start.10 = (f32[96,256]{1,0:T(8,128)S(1)}, f32[96,256]{1,0:T(8,128)S(1)}, u32[]{:S(2)}, u32[]{:S(2)}) collective-permute-start(f32[96,256]{1,0:T(8,128)S(1)} %fusion.20), channel_id=1, source_target_pairs={{0,4},{4,0},{1,5},{5,1},{2,6},{6,2},{3,7},{7,3},{8,12},{12,8},{9,1... | collective-permute-start | bytes 294920 | tf_op jit(solution)/shard_map/ppermute | solution.py:318
  39.6 20.1 %collective-permute-start.27 = (f32[96,512]{1,0:T(8,128)S(1)}, f32[96,512]{1,0:T(8,128)S(1)}, u32[]{:S(2)}, u32[]{:S(2)}) collective-permute-start(f32[96,512]{1,0:T(8,128)S(1)} %fusion.1), channel_id=1, source_target_pairs={{0,4},{4,0},{1,5},{5,1},{2,6},{6,2},{3,7},{7,3},{8,12},{12,8},{9,1... | collective-permute-start | bytes 589832 | tf_op jit(solution)/shard_map/ppermute | solution.py:318
  41.2 7.6 %collective-permute-start.17 = (bf16[48,2048]{1,0:T(8,128)(2,1)S(1)}, bf16[48,2048]{1,0:T(8,128)(2,1)S(1)}, u32[]{:S(2)}, u32[]{:S(2)}) collective-permute-start(bf16[48,2048]{1,0:T(8,128)(2,1)S(1)} %collective-permute-done.9), channel_id=1, source_target_pairs={{1,0},{2,3},{5,4},{6,7},{9,8},{10,11},{13,12},{14,15},{17,16},{18,... | collective-permute-start | bytes 589832 | tf_op jit(solution)/shard_map/ppermute | solution.py:318
  46.2 8.7 %collective-permute-start.11 = (bf16[288,256]{1,0:T(8,128)(2,1)S(1)}, bf16[288,256]{1,0:T(8,128)(2,1)S(1)}, u32[]{:S(2)}, u32[]{:S(2)}) collective-permute-start(bf16[288,256]{1,0:T(8,128)(2,1)S(1)} %pad_maximum_fusion.17), channel_id=1, source_target_pairs={{0,8},{8,0},{16,24},{24,16},{1,9},{9,1},{17,25},{25,17},{2,10},{10... | collective-permute-start | bytes 442376 | tf_op jit(solution)/shard_map/ppermute | solution.py:318
  46.3 9.3 %collective-permute-start.12 = (bf16[288,256]{1,0:T(8,128)(2,1)S(1)}, bf16[288,256]{1,0:T(8,128)(2,1)S(1)}, u32[]{:S(2)}, u32[]{:S(2)}) collective-permute-start(bf16[288,256]{1,0:T(8,128)(2,1)S(1)} %pad_maximum_fusion.17), channel_id=1, source_target_pairs={{0,16},{8,24},{16,0},{24,8},{1,17},{9,25},{17,1},{25,9},{2,18},{10... | collective-permute-start | bytes 442376 | tf_op jit(solution)/shard_map/ppermute | solution.py:318
  46.9 9.9 %collective-permute-start.13 = (bf16[288,256]{1,0:T(8,128)(2,1)S(1)}, bf16[288,256]{1,0:T(8,128)(2,1)S(1)}, u32[]{:S(2)}, u32[]{:S(2)}) collective-permute-start(bf16[288,256]{1,0:T(8,128)(2,1)S(1)} %pad_maximum_fusion.17), channel_id=1, source_target_pairs={{0,24},{8,16},{16,8},{24,0},{1,25},{9,17},{17,9},{25,1},{2,26},{10... | collective-permute-start | bytes 442376 | tf_op jit(solution)/shard_map/ppermute | solution.py:318
  56.8 19.8 %collective-permute-start.6 = (f32[192,512]{1,0:T(8,128)S(1)}, f32[192,512]{1,0:T(8,128)S(1)}, u32[]{:S(2)}, u32[]{:S(2)}) collective-permute-start(f32[192,512]{1,0:T(8,128)S(1)} %fusion.5), channel_id=1, source_target_pairs={{0,4},{4,0},{1,5},{5,1},{2,6},{6,2},{3,7},{7,3},{8,12},{12,8},{9,1... | collective-permute-start | bytes 1179656 | tf_op jit(solution)/shard_map/ppermute | solution.py:318
  57.4 15.6 %collective-permute-start.24 = (f32[96,512]{1,0:T(8,128)S(1)}, f32[96,512]{1,0:T(8,128)S(1)}, u32[]{:S(2)}, u32[]{:S(2)}) collective-permute-start(f32[96,512]{1,0:T(8,128)S(1)} %fusion.3), channel_id=1, source_target_pairs={{0,4},{4,0},{1,5},{5,1},{2,6},{6,2},{3,7},{7,3},{8,12},{12,8},{9,1... | collective-permute-start | bytes 589832 | tf_op jit(solution)/shard_map/ppermute | solution.py:318
  62.6 20.7 %collective-permute-start.28 = (bf16[48,512]{1,0:T(8,128)(2,1)S(1)}, bf16[48,512]{1,0:T(8,128)(2,1)S(1)}, u32[]{:S(2)}, u32[]{:S(2)}) collective-permute-start(bf16[48,512]{1,0:T(8,128)(2,1)S(1)} %slice_bitcast_fusion), channel_id=1, source_target_pairs={{0,4},{4,0},{1,5},{5,1},{2,6},{6,2},{3,7},{7,3},{8,12},{12,8},{9,1... | collective-permute-start | bytes 147464 | tf_op jit(solution)/shard_map/ppermute | solution.py:318
  76.0 7.3 %collective-permute-start.25 = (bf16[48,512]{1,0:T(8,128)(2,1)S(1)}, bf16[48,512]{1,0:T(8,128)(2,1)S(1)}, u32[]{:S(2)}, u32[]{:S(2)}) collective-permute-start(bf16[48,512]{1,0:T(8,128)(2,1)S(1)} %slice_bitcast_fusion.2), channel_id=1, source_target_pairs={{0,4},{4,0},{1,5},{5,1},{2,6},{6,2},{3,7},{7,3},{8,12},{12,8},{9,1... | collective-permute-start | bytes 147464 | tf_op jit(solution)/shard_map/ppermute | solution.py:318
  81.7 8.4 %collective-permute-start.22 = (bf16[96,512]{1,0:T(8,128)(2,1)S(1)}, bf16[96,512]{1,0:T(8,128)(2,1)S(1)}, u32[]{:S(2)}, u32[]{:S(2)}) collective-permute-start(bf16[96,512]{1,0:T(8,128)(2,1)S(1)} %bitcast.89), channel_id=1, source_target_pairs={{0,4},{4,0},{1,5},{5,1},{2,6},{6,2},{3,7},{7,3},{8,12},{12,8},{9,1... | collective-permute-start | bytes 294920 | tf_op jit(solution)/shard_map/ppermute | solution.py:318
  85.0 13.9 %collective-permute-start.29 = (bf16[48,4096]{1,0:T(8,128)(2,1)S(1)}, bf16[48,4096]{1,0:T(8,128)(2,1)S(1)}, u32[]{:S(2)}, u32[]{:S(2)}) collective-permute-start(bf16[48,4096]{1,0:T(8,128)(2,1)S(1)} %convolution_convert_fusion), channel_id=1, source_target_pairs={{0,1},{3,2},{4,5},{7,6},{8,9},{11,10},{12,13},{15,14},{16,17},{19,... | collective-permute-start | bytes 1179656 | tf_op jit(solution)/shard_map/ppermute | solution.py:318
  89.4 13.5 %collective-permute-start.26 = (bf16[48,4096]{1,0:T(8,128)(2,1)S(1)}, bf16[48,4096]{1,0:T(8,128)(2,1)S(1)}, u32[]{:S(2)}, u32[]{:S(2)}) collective-permute-start(bf16[48,4096]{1,0:T(8,128)(2,1)S(1)} %convolution_convert_fusion), channel_id=1, source_target_pairs={{1,2},{2,1},{5,6},{6,5},{9,10},{10,9},{13,14},{14,13},{17,18},{18,... | collective-permute-start | bytes 1179656 | tf_op jit(solution)/shard_map/ppermute | solution.py:318
  91.6 15.7 %collective-permute-start.23 = (bf16[48,4096]{1,0:T(8,128)(2,1)S(1)}, bf16[48,4096]{1,0:T(8,128)(2,1)S(1)}, u32[]{:S(2)}, u32[]{:S(2)}) collective-permute-start(bf16[48,4096]{1,0:T(8,128)(2,1)S(1)} %slice.375), channel_id=1, source_target_pairs={{0,1},{1,0},{2,3},{3,2},{4,5},{5,4},{6,7},{7,6},{8,9},{9,8},{10,11... | collective-permute-start | bytes 1179656 | tf_op jit(solution)/shard_map/ppermute | solution.py:318
  100.4 20.3 %collective-permute-start.30 = (bf16[48,4096]{1,0:T(8,128)(2,1)S(1)}, bf16[48,4096]{1,0:T(8,128)(2,1)S(1)}, u32[]{:S(2)}, u32[]{:S(2)}) collective-permute-start(bf16[48,4096]{1,0:T(8,128)(2,1)S(1)} %fusion), channel_id=1, source_target_pairs={{0,2},{1,3},{2,0},{3,1},{4,6},{5,7},{6,4},{7,5},{8,10},{9,11},{10,... | collective-permute-start | bytes 1179656 | tf_op jit(solution)/shard_map/ppermute | solution.py:318
  (15 other events, 135.7 us)

commit v2 on v0

--- a/solution.py
+++ b/solution.py
@@ -1,8 +1,11 @@
+import functools
 import math
 
 import jax
 import jax.numpy as jnp
 from jax import lax
+from jax.experimental import pallas as pl
+from jax.experimental.pallas import tpu as pltpu
 from jax.sharding import PartitionSpec as P
 
 HEAD_SIZE = 128
@@ -15,6 +18,7 @@
 beta_slow = 1.0
 norm_epsilon = 1e-05
 masked_score = -1e30
+sum_type = jnp.bfloat16
 
 
 def yarn_inverse(head_dim):
@@ -193,6 +197,361 @@
     return (hidden_in.astype(jnp.float32) + projected).astype(jnp.bfloat16)
 
 
+def swap_pairs(axis_size, flip):
+    return [(place, place ^ flip) for place in range(axis_size)]
+
+
+def by_xor(parts, index):
+    count = len(parts)
+    bit = 1
+    while bit < count:
+        parts = [jnp.where((index & bit) != 0, parts[k ^ bit], parts[k]) for k in range(count)]
+        bit *= 2
+    return parts
+
+
+def after(value, *others):
+    return lax.optimization_barrier((value,) + others)[0]
+
+
+def whole_spec(array):
+    zeros = (0,) * array.ndim
+    return pl.BlockSpec(array.shape, lambda step, which: zeros)
+
+
+def call_kernel(kernel, name, which, arrays, specs, outs, steps=1, scratch=(), mebibytes=16):
+    shapes = [jax.ShapeDtypeStruct(shape, dtype) for shape, dtype, unused in outs]
+    out_specs = [
+        whole_spec(shape) if spec is None else spec for shape, (a, b, spec) in zip(shapes, outs)
+    ]
+    found = pl.pallas_call(
+        kernel,
+        name=name,
+        grid_spec=pltpu.PrefetchScalarGridSpec(
+            num_scalar_prefetch=1,
+            grid=(steps,),
+            in_specs=[
+                whole_spec(array) if spec is None else spec for array, spec in zip(arrays, specs)
+            ],
+            out_specs=out_specs,
+            scratch_shapes=list(scratch),
+        ),
+        out_shape=shapes,
+        compiler_params=pltpu.CompilerParams(vmem_limit_bytes=mebibytes * 1024 * 1024),
+    )(which, *arrays)
+    return found
+
+
+def norm_kernel(which, hidden, gain, mine, others):
+    half_width = mine.shape[1]
+    widened = hidden[...].astype(jnp.float32)
+    power = jnp.mean(widened * widened, axis=-1, keepdims=True)
+    normed = (widened * lax.rsqrt(power + norm_epsilon) * gain[...]).astype(jnp.bfloat16)
+
+    @pl.when(which[0] == 0)
+    def _():
+        mine[...] = normed[:, :half_width]
+        others[...] = normed[:, half_width:]
+
+    @pl.when(which[0] != 0)
+    def _():
+        mine[...] = normed[:, half_width:]
+        others[...] = normed[:, :half_width]
+
+
+def stacked_rows(chunks):
+    return jnp.concatenate(
+        [
+            chunk[...] if len(pair) == 1 else pair[0][...] + pair[1][...]
+            for pair in chunks
+            for chunk in pair[:1]
+        ],
+        axis=0,
+    )
+
+
+def split_chunks(refs, widths):
+    chunks = []
+    place = 0
+    for width in widths:
+        chunks.append(refs[place : place + width])
+        place += width
+    return chunks, refs[place:]
+
+
+def product(left, right):
+    return jnp.dot(left, right, preferred_element_type=jnp.float32)
+
+
+def stack_kernel(widths, which, *refs):
+    chunks, (out,) = split_chunks(refs, widths)
+    out[...] = stacked_rows(chunks)
+
+
+def other_part(value, rows):
+    pieces = [value[place : place + rows] for place in range(0, value.shape[0], rows)]
+    return jnp.concatenate([pieces[k ^ 1] for k in range(len(pieces))], axis=0)
+
+
+def rotated(part, cosine_rows, sine_rows):
+    return part * cosine_rows + pltpu.roll(part, HEAD_SIZE // 2, 1) * sine_rows
+
+
+def pair_kernel(rows, which, keys, values, came, cosines, sines, *refs):
+    out = refs[-1]
+    count = keys.shape[0]
+    added = other_part(came[...], rows).astype(jnp.float32)
+    whole = rotated(keys[...] + added[:, :HEAD_SIZE], cosines[...], sines[...])
+    out[:count, :HEAD_SIZE] = whole.astype(jnp.bfloat16)
+    out[:count, HEAD_SIZE:] = (values[...] + added[:, HEAD_SIZE:]).astype(jnp.bfloat16)
+    if len(refs) == 2:
+        out[count:, :] = refs[0][...]
+
+
+def attention_kernel(
+    slot, blocks, rows, which, kept, came, cosines, sines, query_document, key_document, *refs
+):
+    early, late, (out, peaks, totals, summed) = refs[:blocks], refs[blocks : 2 * blocks], refs[2 * blocks :]
+    tokens, width = came.shape
+    heads = width // HEAD_SIZE
+    score_scale = HEAD_SIZE ** (-0.5)
+    early_rows = key_document.shape[2] - late[0].shape[0]
+    block_rows = 4 * rows
+    whole = kept[...] + other_part(came[...], rows).astype(jnp.float32)
+    stacked = jnp.concatenate(
+        [
+            rotated(whole[:, place : place + HEAD_SIZE], cosines[...], sines[...]).astype(
+                jnp.bfloat16
+            )
+            for place in range(0, width, HEAD_SIZE)
+        ],
+        axis=0,
+    )
+    place_outer, place_inner, place_tensor = which[0], which[1], which[2]
+    document = query_document[...]
+
+    def inside(slot_number, part_number, row_number):
+        return (place_inner ^ part_number) * block_rows + (place_tensor ^ slot_number) * rows + row_number
+
+    line = lax.broadcasted_iota(jnp.int32, (tokens, 1), 0)
+    second = (line >= rows).astype(jnp.int32)
+    row_index = place_outer * 2 * block_rows + inside(slot, second, line - rows * second)
+    line = lax.broadcasted_iota(jnp.int32, (1, 2 * block_rows), 1)
+    slots = sum((line >= 2 * rows * number).astype(jnp.int32) for number in range(1, 4))
+    left = line - 2 * rows * slots
+    second = (left >= rows).astype(jnp.int32)
+    key_place = inside(slots, second, left - rows * second)
+
+    def joined(block, start):
+        stop = start + HEAD_SIZE
+        return jnp.concatenate([early[block][:early_rows, start:stop], late[block][:, start:stop]], axis=0)
+
+    def block_scores(block):
+        scores = lax.dot_general(
+            stacked, joined(block, 0), (((1,), (1,)), ((), ())), preferred_element_type=jnp.float32
+        )
+        places = (place_outer ^ block) * 2 * block_rows + key_place
+        allowed = (places <= row_index) & (key_document[block] == document)
+        scores = scores.reshape(heads, tokens, -1) * score_scale
+        return jnp.where(allowed[None], scores, masked_score).reshape(heads * tokens, -1)
+
+    def weighted(block, weights):
+        return product(weights.astype(jnp.bfloat16), joined(block, HEAD_SIZE))
+
+    scores = block_scores(0)
+    peak = jnp.max(scores, axis=-1, keepdims=True)
+    weights = jnp.exp(scores - peak)
+    peaks[...] = peak
+    totals[...] = jnp.sum(weights, axis=-1, keepdims=True)
+    summed[...] = weighted(0, weights)
+    for block in range(1, blocks):
+
+        @pl.when((place_outer ^ block) < place_outer)
+        def _():
+            scores = block_scores(block)
+            before = peaks[...]
+            peak = jnp.maximum(before, jnp.max(scores, axis=-1, keepdims=True))
+            weights = jnp.exp(scores - peak)
+            shrink = jnp.exp(before - peak)
+            peaks[...] = peak
+            totals[...] = totals[...] * shrink + jnp.sum(weights, axis=-1, keepdims=True)
+            summed[...] = summed[...] * shrink + weighted(block, weights)
+
+    result = (summed[...] / totals[...]).astype(jnp.bfloat16)
+    for head in range(heads):
+        out[:, head * HEAD_SIZE : (head + 1) * HEAD_SIZE] = result[head * tokens : (head + 1) * tokens]
+
+
+def short_body(hidden_in, norm_gain, w_query, w_key, value_weight, w_out, doc_ids, positions):
+    place_outer = lax.axis_index("outer")
+    place_inner = lax.axis_index("inner")
+    place_tensor = lax.axis_index("tensor")
+    outer_count = lax.axis_size("outer")
+    rows, width = hidden_in.shape
+    half_width = w_query.shape[0]
+    query_half = w_query.shape[1] // 2
+    slot_rows = 2 * rows
+    early_rows = 3 * slot_rows
+    bf16 = jnp.bfloat16
+    across_inner = swap_pairs(2, 1)
+    which = place_inner.reshape(1)
+
+    def send(value, axis, pairs):
+        return lax.ppermute(value, axis, pairs)
+
+    def send_across(value, pairs):
+        both = [(a * 4 + b, (1 - a) * 4 + c) for a in range(2) for b, c in pairs]
+        return lax.ppermute(value, ("inner", "tensor"), both)
+
+    half = ((rows, half_width), bf16, None)
+    mine, others = call_kernel(
+        norm_kernel, "norm", which, [hidden_in, norm_gain.reshape(1, width)], [None] * 2, [half] * 2
+    )
+    two, one, middle = swap_pairs(4, 2), swap_pairs(4, 1), [(1, 2), (2, 1)]
+    two_mine = send(mine, "tensor", two)
+    two_theirs = send_across(others, two)
+    one_mine = send(mine, "tensor", one)
+    one_theirs = send_across(others, one)
+    theirs = send(others, "inner", across_inner)
+    early = [[mine], [theirs], [one_mine], [one_theirs], [two_mine], [two_theirs]]
+
+    facts = jnp.stack([doc_ids, positions])
+    facts = jnp.stack([facts, send(facts, "inner", across_inner)])
+
+    def relative(parts):
+        pieces = [parts[:, k * rows : (k + 1) * rows] for k in range(4)]
+        return jnp.stack(by_xor(pieces, place_tensor)).reshape(-1)
+
+    documents = relative(facts[:, 0])
+    row_positions = relative(facts[:, 1])
+    padding = 16 * 2 * HEAD_SIZE - documents.shape[0]
+    document_rows = jnp.pad(documents, (0, padding)).astype(bf16).reshape(16, 2 * HEAD_SIZE)
+    inverse = jnp.asarray(yarn_inverse(HEAD_SIZE) * 2, dtype=jnp.float32)
+    signs = jnp.asarray([-1.0] * (HEAD_SIZE // 2) + [1.0] * (HEAD_SIZE // 2), dtype=jnp.float32)
+    attention_gain = 0.1 * math.log(yarn_factor) + 1.0
+    angles = row_positions.astype(jnp.float32)[:, None] * inverse[None, :]
+    cosines = jnp.cos(angles) * attention_gain
+    sines = jnp.sin(angles) * attention_gain * signs
+
+    tables = (cosines, sines)
+    ends_mine = send(after(two_mine, *tables), "tensor", [(1, 0), (2, 3)])
+    middle_mine = send(after(mine, two_mine, *tables), "tensor", middle)
+    ends_theirs = send(after(two_theirs, *tables), "tensor", [(1, 0), (2, 3)])
+    middle_theirs = send_across(after(others, two_mine, *tables), middle)
+    late = [[middle_mine, ends_mine], [middle_theirs, ends_theirs]]
+
+    def stack(name, chunks):
+        flat = [array for chunk in chunks for array in chunk]
+        return call_kernel(
+            functools.partial(stack_kernel, [len(chunk) for chunk in chunks]), name, which, flat,
+            [None] * len(flat), [((len(chunks) * rows, half_width), bf16, None)],
+        )[0]
+
+    def sent_half(whole):
+        wide = whole.shape[1] // 2
+        return lax.dynamic_slice_in_dim(whole, (1 - place_inner) * wide, wide, 1).astype(sum_type)
+
+    def project_pair(stacked):
+        keys, values = product(stacked, w_key), product(stacked, value_weight)
+        gone = jnp.concatenate([sent_half(keys), sent_half(values)], axis=1)
+        return keys, values, send(gone, "inner", across_inner)
+
+    def project_query(stacked):
+        queries = product(stacked, w_query)
+        return queries, send(sent_half(queries), "inner", across_inner)
+
+    def gather_pairs(pair):
+        found = [pair]
+        for flip in range(1, outer_count):
+            found.append(send(pair, "outer", swap_pairs(outer_count, flip)))
+        return found
+
+    def rotate_pair(projected, first, extra):
+        keys, values, came = projected
+        count = came.shape[0]
+        half_spec = pl.BlockSpec((count, HEAD_SIZE), lambda step, which: (0, which[0]))
+        table_spec = pl.BlockSpec((count, HEAD_SIZE), lambda step, which: (first // count, 0))
+        out_rows = count + sum(array.shape[0] for array in extra)
+        return call_kernel(
+            functools.partial(pair_kernel, rows), "pair", which,
+            [keys, values, came, cosines, sines] + extra,
+            [half_spec, half_spec, None, table_spec, table_spec] + [None] * len(extra),
+            [((out_rows, 2 * HEAD_SIZE), bf16, None)],
+        )[0]
+
+    early_stacked = stack("early_rows", early)
+    early_projected = project_pair(early_stacked)
+    late_stacked = stack("late_rows", late)
+    late_projected = project_pair(late_stacked)
+    early_queries, early_came = project_query(after(early_stacked, late_projected[0]))
+    late_queries, late_came = project_query(late_stacked)
+    early_pairs = gather_pairs(rotate_pair(early_projected, 0, [document_rows]))
+    late_pairs = gather_pairs(rotate_pair(late_projected, early_rows, []))
+    key_documents = jnp.stack(
+        [array[early_rows:].reshape(1, -1)[:, : 4 * slot_rows] for array in early_pairs]
+    ).astype(jnp.int32)
+
+    places = jnp.stack([place_outer, place_inner, place_tensor])
+
+    def attend(slot, *wait):
+        queries, came = (late_queries, late_came) if slot == 3 else (early_queries, early_came)
+        block = slot % 3
+        if wait:
+            came = after(came, *wait)
+        rows_spec = lambda wide, block: pl.BlockSpec((slot_rows, wide), lambda step, which: (block, 0))
+        half_spec = pl.BlockSpec((slot_rows, query_half), lambda step, which: (block, which[1]))
+        stacked = query_half // HEAD_SIZE * slot_rows
+        return call_kernel(
+            functools.partial(attention_kernel, slot, outer_count, rows), "attention", places,
+            [queries, came, cosines, sines, documents[:, None], key_documents] + early_pairs + late_pairs,
+            [
+                half_spec, rows_spec(query_half, block),
+                rows_spec(HEAD_SIZE, slot), rows_spec(HEAD_SIZE, slot), rows_spec(1, slot),
+            ] + [None] * (1 + 2 * outer_count),
+            [((slot_rows, query_half), bf16, None)],
+            scratch=[
+                pltpu.VMEM((stacked, 1), jnp.float32),
+                pltpu.VMEM((stacked, 1), jnp.float32),
+                pltpu.VMEM((stacked, HEAD_SIZE), jnp.float32),
+            ],
+        )[0]
+
+    lower = place_inner == 0
+
+    def joined(slot, *wait):
+        attended = attend(slot, *wait)
+        here = attended[:rows]
+        came = send(attended[rows:], "inner", across_inner)
+        return jnp.concatenate(
+            [jnp.where(lower, here, came), jnp.where(lower, came, here)], axis=1
+        )
+
+    out_half = w_out.shape[1] // 2
+    left, right = w_out[:, :out_half], w_out[:, out_half:]
+    inward, outward = [(0, 1), (3, 2)], [(1, 0), (2, 3)]
+    rows_3 = joined(3)
+    rows_2 = joined(2)
+    term_left = product(rows_3, left).astype(bf16)
+    inward_left = send(term_left, "tensor", inward)
+    term_right = product(rows_3, right).astype(bf16)
+    came_middle = send(jnp.concatenate([term_left, term_right], axis=1), "tensor", middle)
+    inward_right = send(term_right, "tensor", inward)
+    rows_1 = joined(1, term_left, term_right)
+    rows_0 = joined(0, term_left, term_right)
+    term_1 = product(rows_1, w_out).astype(bf16)
+    came_outward = send(term_1, "tensor", outward)
+    sum_left = product(rows_2, left) + after(inward_left, term_1).astype(jnp.float32)
+    two_left = send(sum_left.astype(bf16), "tensor", two)
+    sum_right = product(rows_2, right) + inward_right.astype(jnp.float32)
+    two_right = send(sum_right.astype(bf16), "tensor", two)
+    came_inward = send(after(term_1, inward_right), "tensor", inward)
+    total = lax.optimization_barrier(product(rows_0, w_out))
+    total = total + hidden_in.astype(jnp.float32) + came_outward.astype(jnp.float32)
+    total = total + came_inward.astype(jnp.float32) + came_middle.astype(jnp.float32)
+    came_2 = jnp.concatenate([two_left, two_right], axis=1)
+    return (total + came_2.astype(jnp.float32)).astype(bf16)
+
+
 def solution(mesh):
     in_specs = (
         P(("outer", "inner", "tensor"), None),
@@ -205,4 +564,22 @@
         P(("outer", "inner")),
     )
     out_specs = P(("outer", "inner", "tensor"), None)
-    return jax.shard_map(body, mesh=mesh, in_specs=in_specs, out_specs=out_specs, check_vma=False)
+
+    def chosen(*arrays):
+        outer_count = mesh.shape["outer"]
+        key_heads = arrays[3].shape[1] // HEAD_SIZE // mesh.shape["tensor"]
+        short = (
+            mesh.shape["tensor"] == 4
+            and mesh.shape["inner"] == 2
+            and key_heads == 2
+            and outer_count & (outer_count - 1) == 0
+            and arrays[0].shape[0] % (mesh.size * 16) == 0
+            and arrays[0].shape[0] // outer_count <= 512
+        )
+        mapped = jax.shard_map(
+            short_body if short else body,
+            mesh=mesh, in_specs=in_specs, out_specs=out_specs, check_vma=False,
+        )
+        return mapped(*arrays)
+
+    return chosen

time: 237 us -> 112 us (0.47); the launches traced: 233 us -> 111 us
  blocking collectives: 64.2 us -> 0 us
  waiting for transfers between devices: 97.4 us -> 40.5 us
  starting transfers between devices: 0.09 us -> 41.9 us
  loops' own time: 17.3 us -> 0 us
  between operations: 13.9 us -> 0.64 us
  Pallas kernels: 0 us -> 12 us
  other arithmetic: 13.6 us -> 2.89 us
  local copies, waits for them, and re-layouts: 10.7 us -> 2.37 us
  matrix products: 15.9 us -> 10.4 us
    reduce_scatter x2 -> x0, waiting for transfers between devices: 58.9 us -> none  [the longest x1 36.2 us: body(): lax.psum_scatter(full_term.astype(jnp.bfloat16), 'tensor', scatter_dimens...]
    ppermute x0 -> x31, starting transfers between devices: none -> 41.9 us  [the longest x28 32.6 us: send(): return lax.ppermute(value, axis, pairs)]
    ppermute x0 -> x31, waiting for transfers between devices: none -> 40.5 us  [the longest x28 36.4 us: send(): return lax.ppermute(value, axis, pairs)]
    all_gather x1 -> x0, waiting for transfers between devices: 38.4 us -> none  [body(): block_rows = lax.all_gather(normed, 'tensor', axis=0, tiled=True)]
    all_gather x2 -> x0, blocking collectives: 35.6 us -> none  [the longest x1 18.1 us: body(): lax.all_gather(value_matrix, ('outer', 'inner'), axis=0, tiled=True)]
    all_to_all x1 -> x0, blocking collectives: 22 us -> none  [body(): lax.all_to_all(arranged, 'inner', split_axis=1, concat_axis=0, tiled=True)]
    another operation x4 -> x0, loops' own time: 17.3 us -> none  [the longest x1 17.2 us: body(): lax.scan(scan_step, initial, (split_keys, split_values, offsets))]
    pallas_call x0 -> x9, Pallas kernels: none -> 12 us  [call_kernel(): pl.pallas_call(kernel, name=name, grid_spec=pltpu.PrefetchScalarGridSpec(...]
  transfers between devices with their start and end apart: 3 -> 31, of which waited for: 3 -> 13; matrix products, arithmetic and copies ran while one was open for 1% -> 11% of each run, Pallas kernels for 0% -> 8%
where the time goes in v2:
time: 112 us; the launch traced here: 111 us
  starting transfers between devices  41.9 us (37%)
  waiting for transfers between devices  40.5 us (36%)
  Pallas kernels  12 us (11%)
  matrix products  10.4 us (9%)
  other arithmetic  2.89 us (3%)
  local copies, waits for them, and re-layouts  2.37 us (2%)
    ppermute x28, waiting for transfers between devices, send(): return lax.ppermute(value, axis, pairs)  36.4 us
    ppermute x28, starting transfers between devices, send(): return lax.ppermute(value, axis, pairs)  32.6 us
    pallas_call x9, Pallas kernels, call_kernel(): pl.pallas_call(kernel, name=name, grid_spec=pltpu.PrefetchScalarGridSpec(...  12 us
    dot_general x12, matrix products, product(): return jnp.dot(left, right, preferred_element_type=jnp.float32)  10.4 us
    ppermute x3, starting transfers between devices, send_across(): return lax.ppermute(value, ('inner', 'tensor'), both)  9.3 us
    ppermute x3, waiting for transfers between devices, send_across(): return lax.ppermute(value, ('inner', 'tensor'), both)  4.06 us
  transfers between devices with their start and end apart: 31, of which 13 were waited for; matrix products, arithmetic and copies ran while one was open for 11% of the time, Pallas kernels for 8%

profile of v2, /device:TPU:2, one launch (start us, length us, event | category | flops | bytes accessed | tf_op | source)
XLA Modules:
  0.0 110.7 jit_solution(6894153112459417804)
XLA Ops:
  2.0 3.6 %collective-permute-start.4 = (bf16[48,2048]{1,0:T(8,128)(2,1)S(1)}, bf16[48,2048]{1,0:T(8,128)(2,1)S(1)}, u32[]{:S(2)}, u32[]{:S(2)}) collective-permute-start(bf16[48,2048]{1,0:T(8,128)(2,1)S(1)} %get-tuple-element.19), channel_id=1, source_target_pairs={{0,6},{1,7},{2,4},{3,5},{4,2},{5,3},{6,0},{7,1},{8,14},{9,15},{10,... | collective-permute-start | bytes 589832 | tf_op jit(solution)/shard_map/ppermute | solution.py:404
  6.5 1.6 %collective-permute-start.1 = (bf16[48,2048]{1,0:T(8,128)(2,1)S(1)}, bf16[48,2048]{1,0:T(8,128)(2,1)S(1)}, u32[]{:S(2)}, u32[]{:S(2)}) collective-permute-start(bf16[48,2048]{1,0:T(8,128)(2,1)S(1)} %get-tuple-element.17.refs_0_), channel_id=1, source_target_pairs={{0,1},{1,0},{2,3},{3,2},{4,5},{5,4},{6,7},{7,6},{8,9},{9,8},{10,11... | collective-permute-start | bytes 589832 | tf_op jit(solution)/shard_map/ppermute | solution.py:400
  8.8 1.6 %collective-permute-start.5 = (s32[2,192]{1,0:T(2,128)S(1)}, s32[2,192]{1,0:T(2,128)S(1)}, u32[]{:S(2)}, u32[]{:S(2)}) collective-permute-start(s32[2,192]{1,0:T(2,128)S(1)} %get-tuple-element.47), channel_id=1, source_target_pairs={{0,4},{4,0},{1,5},{5,1},{2,6},{6,2},{3,7},{7,3},{8,12},{12,8},{9,1... | collective-permute-start | bytes 4616 | tf_op jit(solution)/shard_map/ppermute | solution.py:400
  10.4 2.0 %collective-permute-done.5 = s32[2,192]{1,0:T(2,128)S(1)} collective-permute-done((s32[2,192]{1,0:T(2,128)S(1)}, s32[2,192]{1,0:T(2,128)S(1)}, u32[]{:S(2)}, u32[]{:S(2)}) %collective-permute-start.5) | collective-permute-done | bytes 1568 | tf_op jit(solution)/shard_map/ppermute | solution.py:400
  12.4 5.0 %collective-permute-start.2 = (bf16[48,2048]{1,0:T(8,128)(2,1)S(1)}, bf16[48,2048]{1,0:T(8,128)(2,1)S(1)}, u32[]{:S(2)}, u32[]{:S(2)}) collective-permute-start(bf16[48,2048]{1,0:T(8,128)(2,1)S(1)} %get-tuple-element.19), channel_id=1, source_target_pairs={{0,5},{1,4},{2,7},{3,6},{4,1},{5,0},{6,3},{7,2},{8,13},{9,12},{10,... | collective-permute-start | bytes 589832 | tf_op jit(solution)/shard_map/ppermute | solution.py:404
  18.0 5.4 %collective-permute-done.3.refs_4_ = bf16[48,2048]{1,0:T(8,128)(2,1)S(1)} collective-permute-done((bf16[48,2048]{1,0:T(8,128)(2,1)S(1)}, bf16[48,2048]{1,0:T(8,128)(2,1)S(1)}, u32[]{:S(2)}, u32[]{:S(2)}) %collective-permute-start.3) | collective-permute-done | bytes 196640 | tf_op jit(solution)/shard_map/ppermute | solution.py:400
  23.4 4.1 %collective-permute-done.2.refs_3_ = bf16[48,2048]{1,0:T(8,128)(2,1)S(1)} collective-permute-done((bf16[48,2048]{1,0:T(8,128)(2,1)S(1)}, bf16[48,2048]{1,0:T(8,128)(2,1)S(1)}, u32[]{:S(2)}, u32[]{:S(2)}) %collective-permute-start.2) | collective-permute-done | bytes 196640 | tf_op jit(solution)/shard_map/ppermute | solution.py:404
  28.6 1.6 %collective-permute-start.12 = (bf16[288,256]{1,0:T(8,128)(2,1)S(1)}, bf16[288,256]{1,0:T(8,128)(2,1)S(1)}, u32[]{:S(2)}, u32[]{:S(2)}) collective-permute-start(bf16[288,256]{1,0:T(8,128)(2,1)S(1)} %pad_maximum_fusion.1), channel_id=1, source_target_pairs={{0,4},{4,0},{1,5},{5,1},{2,6},{6,2},{3,7},{7,3},{8,12},{12,8},{9,1... | collective-permute-start | bytes 442376 | tf_op jit(solution)/shard_map/ppermute | solution.py:400
  37.1 6.4 %collective-permute-done.7.refs_1_ = bf16[48,2048]{1,0:T(8,128)(2,1)S(1)} collective-permute-done((bf16[48,2048]{1,0:T(8,128)(2,1)S(1)}, bf16[48,2048]{1,0:T(8,128)(2,1)S(1)}, u32[]{:S(2)}, u32[]{:S(2)}) %collective-permute-start.7) | collective-permute-done | bytes 196640 | tf_op jit(solution)/shard_map/ppermute | solution.py:400
  43.5 2.7 %collective-permute-done.9.refs_3_ = bf16[48,2048]{1,0:T(8,128)(2,1)S(1)} collective-permute-done((bf16[48,2048]{1,0:T(8,128)(2,1)S(1)}, bf16[48,2048]{1,0:T(8,128)(2,1)S(1)}, u32[]{:S(2)}, u32[]{:S(2)}) %collective-permute-start.9) | collective-permute-done | bytes 196640 | tf_op jit(solution)/shard_map/ppermute | solution.py:400
  51.3 2.0 %collective-permute-done.16.came = bf16[96,256]{1,0:T(8,128)(2,1)S(1)} collective-permute-done((bf16[96,256]{1,0:T(8,128)(2,1)S(1)}, bf16[96,256]{1,0:T(8,128)(2,1)S(1)}, u32[]{:S(2)}, u32[]{:S(2)}) %collective-permute-start.16) | collective-permute-done | bytes 49184 | tf_op jit(solution)/shard_map/ppermute | solution.py:400
  55.5 2.5 %collective-permute-done.18.refs_6_ = bf16[96,256]{1,0:T(8,128)(2,1)S(1)} collective-permute-done((bf16[96,256]{1,0:T(8,128)(2,1)S(1)}, bf16[96,256]{1,0:T(8,128)(2,1)S(1)}, u32[]{:S(2)}, u32[]{:S(2)}) %collective-permute-start.18) | collective-permute-done | bytes 49184 | tf_op jit(solution)/shard_map/ppermute | solution.py:400
  58.2 2.8 %attention.4 = bf16[96,512]{1,0:T(8,128)(2,1)S(1)} custom-call(s32[3]{0:T(128)S(1)} %pad_add_fusion.3.which, f32[96,1024]{1,0:T(8,128)S(1)} %fusion.48.kept, bf16[96,512]{1,0:T(8,128)(2,1)S(1)} %collective-permute-done.11.came, f32[384,128]{1,0:T(8,128)S(1)} %get-tuple-element.38.cosines, f32[384,128]{1,0:T(8,128)S(1)} %get-tuple-element.37.sines, ...), custom_call_target="tpu_custom_call" | custom-call | tf_op jit(solution)/shard_map/attention/pallas_call | solution.py:227
  63.2 2.4 %collective-permute-done.20 = bf16[48,512]{1,0:T(8,128)(2,1)S(1)} collective-permute-done((bf16[48,512]{1,0:T(8,128)(2,1)S(1)}, bf16[48,512]{1,0:T(8,128)(2,1)S(1)}, u32[]{:S(2)}, u32[]{:S(2)}) %collective-permute-start.20) | collective-permute-done | bytes 49184 | tf_op jit(solution)/shard_map/ppermute | solution.py:400
  70.1 1.8 %collective-permute-done.10.came = bf16[288,512]{1,0:T(8,128)(2,1)S(1)} collective-permute-done((bf16[288,512]{1,0:T(8,128)(2,1)S(1)}, bf16[288,512]{1,0:T(8,128)(2,1)S(1)}, u32[]{:S(2)}, u32[]{:S(2)}) %collective-permute-start.10) | collective-permute-done | bytes 294944 | tf_op jit(solution)/shard_map/ppermute | solution.py:400
  71.9 3.0 %attention.6 = bf16[96,512]{1,0:T(8,128)(2,1)S(1)} custom-call(s32[3]{0:T(128)S(1)} %pad_add_fusion.3.which, f32[288,1024]{1,0:T(8,128)S(1)} %fusion.47.kept, bf16[288,512]{1,0:T(8,128)(2,1)S(1)} %collective-permute-done.10.came, f32[384,128]{1,0:T(8,128)S(1)} %get-tuple-element.38.cosines, f32[384,128]{1,0:T(8,128)S(1)} %get-tuple-element.37.sines, ...), custom_call_target="tpu_custom_call" | custom-call | tf_op jit(solution)/shard_map/attention/pallas_call | solution.py:227
  76.7 2.8 %attention.7 = bf16[96,512]{1,0:T(8,128)(2,1)S(1)} custom-call(s32[3]{0:T(128)S(1)} %pad_add_fusion.3.which, f32[288,1024]{1,0:T(8,128)S(1)} %fusion.47.kept, bf16[288,512]{1,0:T(8,128)(2,1)S(1)} %collective-permute-done.10.came, f32[384,128]{1,0:T(8,128)S(1)} %get-tuple-element.38.cosines, f32[384,128]{1,0:T(8,128)S(1)} %get-tuple-element.37.sines, ...), custom_call_target="tpu_custom_call" | custom-call | tf_op jit(solution)/shard_map/attention/pallas_call | solution.py:227
  80.6 2.8 %attention.5 = bf16[96,512]{1,0:T(8,128)(2,1)S(1)} custom-call(s32[3]{0:T(128)S(1)} %pad_add_fusion.3.which, f32[288,1024]{1,0:T(8,128)S(1)} %fusion.47.kept, bf16[288,512]{1,0:T(8,128)(2,1)S(1)} %collective-permute-done.10.came, f32[384,128]{1,0:T(8,128)S(1)} %get-tuple-element.38.cosines, f32[384,128]{1,0:T(8,128)S(1)} %get-tuple-element.37.sines, ...), custom_call_target="tpu_custom_call" | custom-call | tf_op jit(solution)/shard_map/attention/pallas_call | solution.py:227
  84.6 1.6 %convolution_convert_fusion = bf16[48,4096]{1,0:T(8,128)(2,1)S(1)} fusion(bf16[1024,4096]{1,0:T(8,128)(2,1)S(1)} %bitcast.68, bf16[48,512]{1,0:T(8,128)(2,1)S(1)} %get-tuple-element.32, bf16[48,512]{1,0:T(8,128)(2,1)S(1)} %get-tuple-element.31), kind=kOutput, calls=%fused_computation | convolution fusion | flops 403046400 | bytes 8880128 | tf_op jit(solution)/shard_map/dot_general | solution.py:283
  88.5 3.2 %collective-permute-start.29 = (bf16[48,2048]{1,0:T(8,128)(2,1)S(1)}, bf16[48,2048]{1,0:T(8,128)(2,1)S(1)}, u32[]{:S(2)}, u32[]{:S(2)}) collective-permute-start(bf16[48,2048]{1,0:T(8,128)(2,1)S(1)} %fusion.17), channel_id=1, source_target_pairs={{0,2},{1,3},{2,0},{3,1},{4,6},{5,7},{6,4},{7,5},{8,10},{9,11},{10,... | collective-permute-start | bytes 589832 | tf_op jit(solution)/shard_map/ppermute | solution.py:400
  92.6 4.3 %collective-permute-start.25 = (bf16[48,4096]{1,0:T(8,128)(2,1)S(1)}, bf16[48,4096]{1,0:T(8,128)(2,1)S(1)}, u32[]{:S(2)}, u32[]{:S(2)}) collective-permute-start(bf16[48,4096]{1,0:T(8,128)(2,1)S(1)} %convolution_convert_fusion), channel_id=1, source_target_pairs={{0,1},{3,2},{4,5},{7,6},{8,9},{11,10},{12,13},{15,14},{16,17},{19,... | collective-permute-start | bytes 1179656 | tf_op jit(solution)/shard_map/ppermute | solution.py:400
  97.0 1.6 %fusion.28 = f32[48,4096]{1,0:T(8,128)S(1)} fusion(bf16[1024,4096]{1,0:T(8,128)(2,1)S(1)} %bitcast.68, bf16[48,512]{1,0:T(8,128)(2,1)S(1)} %get-tuple-element.30, bf16[48,512]{1,0:T(8,128)(2,1)S(1)} %get-tuple-element.29), kind=kOutput, calls=%fused_computation.27 | convolution fusion | flops 402849792 | bytes 9273344 | tf_op jit(solution)/shard_map/dot_general | solution.py:283
  98.6 6.9 %collective-permute-done.29 = bf16[48,2048]{1,0:T(8,128)(2,1)S(1)} collective-permute-done((bf16[48,2048]{1,0:T(8,128)(2,1)S(1)}, bf16[48,2048]{1,0:T(8,128)(2,1)S(1)}, u32[]{:S(2)}, u32[]{:S(2)}) %collective-permute-start.29) | collective-permute-done | bytes 196640 | tf_op jit(solution)/shard_map/ppermute | solution.py:400
  105.4 4.2 %collective-permute-done.30 = bf16[48,2048]{1,0:T(8,128)(2,1)S(1)} collective-permute-done((bf16[48,2048]{1,0:T(8,128)(2,1)S(1)}, bf16[48,2048]{1,0:T(8,128)(2,1)S(1)}, u32[]{:S(2)}, u32[]{:S(2)}) %collective-permute-start.30) | collective-permute-done | bytes 196640 | tf_op jit(solution)/shard_map/ppermute | solution.py:400
  (124 shorter events, 34.5 us)
Async XLA Ops:
  2.0 21.3 %collective-permute-start.4 = (bf16[48,2048]{1,0:T(8,128)(2,1)S(1)}, bf16[48,2048]{1,0:T(8,128)(2,1)S(1)}, u32[]{:S(2)}, u32[]{:S(2)}) collective-permute-start(bf16[48,2048]{1,0:T(8,128)(2,1)S(1)} %get-tuple-element.19), channel_id=1, source_target_pairs={{0,6},{1,7},{2,4},{3,5},{4,2},{5,3},{6,0},{7,1},{8,14},{9,15},{10,... | collective-permute-start | bytes 589832 | tf_op jit(solution)/shard_map/ppermute | solution.py:404
  5.7 17.7 %collective-permute-start = (bf16[48,2048]{1,0:T(8,128)(2,1)S(1)}, bf16[48,2048]{1,0:T(8,128)(2,1)S(1)}, u32[]{:S(2)}, u32[]{:S(2)}) collective-permute-start(bf16[48,2048]{1,0:T(8,128)(2,1)S(1)} %get-tuple-element.19), channel_id=1, source_target_pairs={{0,4},{4,0},{1,5},{5,1},{2,6},{6,2},{3,7},{7,3},{8,12},{12,8},{9,1... | collective-permute-start | bytes 589832 | tf_op jit(solution)/shard_map/ppermute | solution.py:400
  6.2 17.2 %collective-permute-start.3 = (bf16[48,2048]{1,0:T(8,128)(2,1)S(1)}, bf16[48,2048]{1,0:T(8,128)(2,1)S(1)}, u32[]{:S(2)}, u32[]{:S(2)}) collective-permute-start(bf16[48,2048]{1,0:T(8,128)(2,1)S(1)} %get-tuple-element.17.refs_0_), channel_id=1, source_target_pairs={{0,2},{1,3},{2,0},{3,1},{4,6},{5,7},{6,4},{7,5},{8,10},{9,11},{10,... | collective-permute-start | bytes 589832 | tf_op jit(solution)/shard_map/ppermute | solution.py:400
  6.5 16.9 %collective-permute-start.1 = (bf16[48,2048]{1,0:T(8,128)(2,1)S(1)}, bf16[48,2048]{1,0:T(8,128)(2,1)S(1)}, u32[]{:S(2)}, u32[]{:S(2)}) collective-permute-start(bf16[48,2048]{1,0:T(8,128)(2,1)S(1)} %get-tuple-element.17.refs_0_), channel_id=1, source_target_pairs={{0,1},{1,0},{2,3},{3,2},{4,5},{5,4},{6,7},{7,6},{8,9},{9,8},{10,11... | collective-permute-start | bytes 589832 | tf_op jit(solution)/shard_map/ppermute | solution.py:400
  12.4 15.0 %collective-permute-start.2 = (bf16[48,2048]{1,0:T(8,128)(2,1)S(1)}, bf16[48,2048]{1,0:T(8,128)(2,1)S(1)}, u32[]{:S(2)}, u32[]{:S(2)}) collective-permute-start(bf16[48,2048]{1,0:T(8,128)(2,1)S(1)} %get-tuple-element.19), channel_id=1, source_target_pairs={{0,5},{1,4},{2,7},{3,6},{4,1},{5,0},{6,3},{7,2},{8,13},{9,12},{10,... | collective-permute-start | bytes 589832 | tf_op jit(solution)/shard_map/ppermute | solution.py:404
  28.6 6.3 %collective-permute-start.12 = (bf16[288,256]{1,0:T(8,128)(2,1)S(1)}, bf16[288,256]{1,0:T(8,128)(2,1)S(1)}, u32[]{:S(2)}, u32[]{:S(2)}) collective-permute-start(bf16[288,256]{1,0:T(8,128)(2,1)S(1)} %pad_maximum_fusion.1), channel_id=1, source_target_pairs={{0,4},{4,0},{1,5},{5,1},{2,6},{6,2},{3,7},{7,3},{8,12},{12,8},{9,1... | collective-permute-start | bytes 442376 | tf_op jit(solution)/shard_map/ppermute | solution.py:400
  31.6 5.0 %collective-permute-start.6 = (bf16[48,2048]{1,0:T(8,128)(2,1)S(1)}, bf16[48,2048]{1,0:T(8,128)(2,1)S(1)}, u32[]{:S(2)}, u32[]{:S(2)}) collective-permute-start(bf16[48,2048]{1,0:T(8,128)(2,1)S(1)} %get-tuple-element.17.refs_0_), channel_id=1, source_target_pairs={{1,2},{2,1},{5,6},{6,5},{9,10},{10,9},{13,14},{14,13},{17,18},{18,... | collective-permute-start | bytes 589832 | tf_op jit(solution)/shard_map/ppermute | solution.py:400
  32.3 11.1 %collective-permute-start.7 = (bf16[48,2048]{1,0:T(8,128)(2,1)S(1)}, bf16[48,2048]{1,0:T(8,128)(2,1)S(1)}, u32[]{:S(2)}, u32[]{:S(2)}) collective-permute-start(bf16[48,2048]{1,0:T(8,128)(2,1)S(1)} %collective-permute-done.3.refs_4_), channel_id=1, source_target_pairs={{1,0},{2,3},{5,4},{6,7},{9,8},{10,11},{13,12},{14,15},{17,16},{18,... | collective-permute-start | bytes 589832 | tf_op jit(solution)/shard_map/ppermute | solution.py:400
  33.6 12.5 %collective-permute-start.9 = (bf16[48,2048]{1,0:T(8,128)(2,1)S(1)}, bf16[48,2048]{1,0:T(8,128)(2,1)S(1)}, u32[]{:S(2)}, u32[]{:S(2)}) collective-permute-start(bf16[48,2048]{1,0:T(8,128)(2,1)S(1)} %collective-permute-done.4.refs_5_), channel_id=1, source_target_pairs={{1,0},{2,3},{5,4},{6,7},{9,8},{10,11},{13,12},{14,15},{17,16},{18,... | collective-permute-start | bytes 589832 | tf_op jit(solution)/shard_map/ppermute | solution.py:400
  35.0 18.4 %collective-permute-start.15 = (bf16[304,256]{1,0:T(8,128)(2,1)S(1)}, bf16[304,256]{1,0:T(8,128)(2,1)S(1)}, u32[]{:S(2)}, u32[]{:S(2)}) collective-permute-start(bf16[304,256]{1,0:T(8,128)(2,1)S(1)} %pair.2.refs_0_), channel_id=1, source_target_pairs={{0,24},{8,16},{16,8},{24,0},{1,25},{9,17},{17,9},{25,1},{2,26},{10... | collective-permute-start | bytes 466952 | tf_op jit(solution)/shard_map/ppermute | solution.py:400
  35.2 18.9 %collective-permute-start.14 = (bf16[304,256]{1,0:T(8,128)(2,1)S(1)}, bf16[304,256]{1,0:T(8,128)(2,1)S(1)}, u32[]{:S(2)}, u32[]{:S(2)}) collective-permute-start(bf16[304,256]{1,0:T(8,128)(2,1)S(1)} %pair.2.refs_0_), channel_id=1, source_target_pairs={{0,16},{8,24},{16,0},{24,8},{1,17},{9,25},{17,1},{25,9},{2,18},{10... | collective-permute-start | bytes 466952 | tf_op jit(solution)/shard_map/ppermute | solution.py:400
  36.6 18.8 %collective-permute-start.13 = (bf16[304,256]{1,0:T(8,128)(2,1)S(1)}, bf16[304,256]{1,0:T(8,128)(2,1)S(1)}, u32[]{:S(2)}, u32[]{:S(2)}) collective-permute-start(bf16[304,256]{1,0:T(8,128)(2,1)S(1)} %pair.2.refs_0_), channel_id=1, source_target_pairs={{0,8},{8,0},{16,24},{24,16},{1,9},{9,1},{17,25},{25,17},{2,10},{10... | collective-permute-start | bytes 466952 | tf_op jit(solution)/shard_map/ppermute | solution.py:400
  49.8 8.4 %collective-permute-start.11 = (bf16[96,512]{1,0:T(8,128)(2,1)S(1)}, bf16[96,512]{1,0:T(8,128)(2,1)S(1)}, u32[]{:S(2)}, u32[]{:S(2)}) collective-permute-start(bf16[96,512]{1,0:T(8,128)(2,1)S(1)} %dynamic-slice_convert_fusion.1), channel_id=1, source_target_pairs={{0,4},{4,0},{1,5},{5,1},{2,6},{6,2},{3,7},{7,3},{8,12},{12,8},{9,1... | collective-permute-start | bytes 294920 | tf_op jit(solution)/shard_map/ppermute | solution.py:400
  53.4 4.6 %collective-permute-start.18 = (bf16[96,256]{1,0:T(8,128)(2,1)S(1)}, bf16[96,256]{1,0:T(8,128)(2,1)S(1)}, u32[]{:S(2)}, u32[]{:S(2)}) collective-permute-start(bf16[96,256]{1,0:T(8,128)(2,1)S(1)} %pair.3.refs_4_), channel_id=1, source_target_pairs={{0,16},{8,24},{16,0},{24,8},{1,17},{9,25},{17,1},{25,9},{2,18},{10... | collective-permute-start | bytes 147464 | tf_op jit(solution)/shard_map/ppermute | solution.py:400
  61.8 10.1 %collective-permute-start.10 = (bf16[288,512]{1,0:T(8,128)(2,1)S(1)}, bf16[288,512]{1,0:T(8,128)(2,1)S(1)}, u32[]{:S(2)}, u32[]{:S(2)}) collective-permute-start(bf16[288,512]{1,0:T(8,128)(2,1)S(1)} %dynamic-slice_convert_fusion), channel_id=1, source_target_pairs={{0,4},{4,0},{1,5},{5,1},{2,6},{6,2},{3,7},{7,3},{8,12},{12,8},{9,1... | collective-permute-start | bytes 884744 | tf_op jit(solution)/shard_map/ppermute | solution.py:400
  66.5 21.2 %collective-permute-start.28 = (bf16[48,2048]{1,0:T(8,128)(2,1)S(1)}, bf16[48,2048]{1,0:T(8,128)(2,1)S(1)}, u32[]{:S(2)}, u32[]{:S(2)}) collective-permute-start(bf16[48,2048]{1,0:T(8,128)(2,1)S(1)} %fusion.20), channel_id=1, source_target_pairs={{0,1},{3,2},{4,5},{7,6},{8,9},{11,10},{12,13},{15,14},{16,17},{19,... | collective-permute-start | bytes 589832 | tf_op jit(solution)/shard_map/ppermute | solution.py:400
  68.8 22.9 %collective-permute-start.24 = (bf16[48,2048]{1,0:T(8,128)(2,1)S(1)}, bf16[48,2048]{1,0:T(8,128)(2,1)S(1)}, u32[]{:S(2)}, u32[]{:S(2)}) collective-permute-start(bf16[48,2048]{1,0:T(8,128)(2,1)S(1)} %fusion.23), channel_id=1, source_target_pairs={{0,1},{3,2},{4,5},{7,6},{8,9},{11,10},{12,13},{15,14},{16,17},{19,... | collective-permute-start | bytes 589832 | tf_op jit(solution)/shard_map/ppermute | solution.py:400
  74.9 8.5 %collective-permute-start.22 = (bf16[48,512]{1,0:T(8,128)(2,1)S(1)}, bf16[48,512]{1,0:T(8,128)(2,1)S(1)}, u32[]{:S(2)}, u32[]{:S(2)}) collective-permute-start(bf16[48,512]{1,0:T(8,128)(2,1)S(1)} %slice.135), channel_id=1, source_target_pairs={{0,4},{4,0},{1,5},{5,1},{2,6},{6,2},{3,7},{7,3},{8,12},{12,8},{9,1... | collective-permute-start | bytes 147464 | tf_op jit(solution)/shard_map/ppermute | solution.py:400
  76.0 33.6 %collective-permute-start.26 = (bf16[48,4096]{1,0:T(8,128)(2,1)S(1)}, bf16[48,4096]{1,0:T(8,128)(2,1)S(1)}, u32[]{:S(2)}, u32[]{:S(2)}) collective-permute-start(bf16[48,4096]{1,0:T(8,128)(2,1)S(1)} %pad_maximum_fusion), channel_id=1, source_target_pairs={{1,2},{2,1},{5,6},{6,5},{9,10},{10,9},{13,14},{14,13},{17,18},{18,... | collective-permute-start | bytes 1179656 | tf_op jit(solution)/shard_map/ppermute | solution.py:400
  79.6 6.6 %collective-permute-start.27 = (bf16[48,512]{1,0:T(8,128)(2,1)S(1)}, bf16[48,512]{1,0:T(8,128)(2,1)S(1)}, u32[]{:S(2)}, u32[]{:S(2)}) collective-permute-start(bf16[48,512]{1,0:T(8,128)(2,1)S(1)} %slice.137), channel_id=1, source_target_pairs={{0,4},{4,0},{1,5},{5,1},{2,6},{6,2},{3,7},{7,3},{8,12},{12,8},{9,1... | collective-permute-start | bytes 147464 | tf_op jit(solution)/shard_map/ppermute | solution.py:400
  86.2 23.5 %collective-permute-start.23 = (bf16[48,4096]{1,0:T(8,128)(2,1)S(1)}, bf16[48,4096]{1,0:T(8,128)(2,1)S(1)}, u32[]{:S(2)}, u32[]{:S(2)}) collective-permute-start(bf16[48,4096]{1,0:T(8,128)(2,1)S(1)} %convolution_convert_fusion), channel_id=1, source_target_pairs={{1,0},{2,3},{5,4},{6,7},{9,8},{10,11},{13,12},{14,15},{17,16},{18,... | collective-permute-start | bytes 1179656 | tf_op jit(solution)/shard_map/ppermute | solution.py:400
  88.5 16.9 %collective-permute-start.29 = (bf16[48,2048]{1,0:T(8,128)(2,1)S(1)}, bf16[48,2048]{1,0:T(8,128)(2,1)S(1)}, u32[]{:S(2)}, u32[]{:S(2)}) collective-permute-start(bf16[48,2048]{1,0:T(8,128)(2,1)S(1)} %fusion.17), channel_id=1, source_target_pairs={{0,2},{1,3},{2,0},{3,1},{4,6},{5,7},{6,4},{7,5},{8,10},{9,11},{10,... | collective-permute-start | bytes 589832 | tf_op jit(solution)/shard_map/ppermute | solution.py:400
  92.6 17.1 %collective-permute-start.30 = (bf16[48,2048]{1,0:T(8,128)(2,1)S(1)}, bf16[48,2048]{1,0:T(8,128)(2,1)S(1)}, u32[]{:S(2)}, u32[]{:S(2)}) collective-permute-start(bf16[48,2048]{1,0:T(8,128)(2,1)S(1)} %fusion.14), channel_id=1, source_target_pairs={{0,2},{1,3},{2,0},{3,1},{4,6},{5,7},{6,4},{7,5},{8,10},{9,11},{10,... | collective-permute-start | bytes 589832 | tf_op jit(solution)/shard_map/ppermute | solution.py:400
  92.6 17.0 %collective-permute-start.25 = (bf16[48,4096]{1,0:T(8,128)(2,1)S(1)}, bf16[48,4096]{1,0:T(8,128)(2,1)S(1)}, u32[]{:S(2)}, u32[]{:S(2)}) collective-permute-start(bf16[48,4096]{1,0:T(8,128)(2,1)S(1)} %convolution_convert_fusion), channel_id=1, source_target_pairs={{0,1},{3,2},{4,5},{7,6},{8,9},{11,10},{12,13},{15,14},{16,17},{19,... | collective-permute-start | bytes 1179656 | tf_op jit(solution)/shard_map/ppermute | solution.py:400
  (17 other events, 139.5 us)

commit v3 on v2

--- a/solution.py
+++ b/solution.py
@@ -18,7 +18,6 @@
 beta_slow = 1.0
 norm_epsilon = 1e-05
 masked_score = -1e30
-sum_type = jnp.bfloat16
 
 
 def yarn_inverse(head_dim):
@@ -201,15 +200,6 @@
     return [(place, place ^ flip) for place in range(axis_size)]
 
 
-def by_xor(parts, index):
-    count = len(parts)
-    bit = 1
-    while bit < count:
-        parts = [jnp.where((index & bit) != 0, parts[k ^ bit], parts[k]) for k in range(count)]
-        bit *= 2
-    return parts
-
-
 def after(value, *others):
     return lax.optimization_barrier((value,) + others)[0]
 
@@ -284,8 +274,10 @@
 
 
 def stack_kernel(widths, which, *refs):
-    chunks, (out,) = split_chunks(refs, widths)
-    out[...] = stacked_rows(chunks)
+    chunks, outs = split_chunks(refs, widths)
+    outs[0][...] = stacked_rows(chunks)
+    for place, out in zip((0, outs[0].shape[0] * 2 // 3), outs[1:]):
+        out[...] = outs[0][place : place + out.shape[0]]
 
 
 def other_part(value, rows):
@@ -308,15 +300,72 @@
         out[count:, :] = refs[0][...]
 
 
+def facts_kernel(rows, which, here, there, inverse, angles, documents, document_rows):
+    block = here.shape[1]
+    line = lax.broadcasted_iota(jnp.int32, (block, 1), 0)
+    slots = sum((line >= rows * number).astype(jnp.int32) for number in range(1, 4))
+    source = (which[2] ^ slots) * rows + line - rows * slots
+    chosen = lax.broadcasted_iota(jnp.int32, (block, block), 1) == source
+
+    def ordered(row):
+        parts = [
+            jnp.sum(jnp.where(chosen, part[row : row + 1, :].astype(jnp.float32), 0.0), axis=1, keepdims=True)
+            for part in (here, there)
+        ]
+        return jnp.concatenate(
+            [part[place : place + rows] for place in range(0, block, rows) for part in parts], axis=0
+        )
+
+    angles[...] = ordered(1) * inverse[...]
+    column = ordered(0)
+    documents[...] = column
+    count = column.shape[0]
+    same = lax.broadcasted_iota(jnp.int32, (count, count), 0) == lax.broadcasted_iota(
+        jnp.int32, (count, count), 1
+    )
+    wide = document_rows.shape[1]
+    across = jnp.sum(jnp.where(same, column, 0.0), axis=0, keepdims=True)
+    rest = jnp.concatenate(
+        [across[:, wide:], jnp.zeros((1, 2 * wide - count), jnp.float32)], axis=1
+    )
+    number = lax.broadcasted_iota(jnp.int32, document_rows.shape, 0)
+    document_rows[...] = jnp.where(
+        number == 0, across[:, :wide], jnp.where(number == 1, rest, 0.0)
+    ).astype(jnp.bfloat16)
+
+
+def copy_kernel(which, *refs):
+    *parts, out = refs
+    place = 0
+    for part in parts:
+        out[:, place : place + part.shape[1]] = part[...].astype(out.dtype)
+        place += part.shape[1]
+
+
+def join_kernel(which, here, came, out):
+    width = here.shape[1]
+
+    @pl.when(which[1] == 0)
+    def _():
+        out[:, :width] = here[...]
+        out[:, width:] = came[...]
+
+    @pl.when(which[1] != 0)
+    def _():
+        out[:, :width] = came[...]
+        out[:, width:] = here[...]
+
+
 def attention_kernel(
-    slot, blocks, rows, which, kept, came, cosines, sines, query_document, key_document, *refs
+    slot, blocks, rows, which, kept, came, cosines, sines, query_document, *refs
 ):
-    early, late, (out, peaks, totals, summed) = refs[:blocks], refs[blocks : 2 * blocks], refs[2 * blocks :]
+    early, late = refs[:blocks], refs[blocks : 2 * blocks]
+    here, gone, peaks, totals, summed = refs[2 * blocks :]
     tokens, width = came.shape
     heads = width // HEAD_SIZE
     score_scale = HEAD_SIZE ** (-0.5)
-    early_rows = key_document.shape[2] - late[0].shape[0]
     block_rows = 4 * rows
+    early_rows = 2 * block_rows - late[0].shape[0]
     whole = kept[...] + other_part(came[...], rows).astype(jnp.float32)
     stacked = jnp.concatenate(
         [
@@ -351,7 +400,10 @@
             stacked, joined(block, 0), (((1,), (1,)), ((), ())), preferred_element_type=jnp.float32
         )
         places = (place_outer ^ block) * 2 * block_rows + key_place
-        allowed = (places <= row_index) & (key_document[block] == document)
+        lines = early[block][early_rows:, :].astype(jnp.float32)
+        rest = 2 * block_rows - lines.shape[1]
+        key_document = jnp.concatenate([lines[0:1, :], lines[1:2, :rest]], axis=1)
+        allowed = (places <= row_index) & (key_document == document)
         scores = scores.reshape(heads, tokens, -1) * score_scale
         return jnp.where(allowed[None], scores, masked_score).reshape(heads * tokens, -1)
 
@@ -379,7 +431,10 @@
 
     result = (summed[...] / totals[...]).astype(jnp.bfloat16)
     for head in range(heads):
-        out[:, head * HEAD_SIZE : (head + 1) * HEAD_SIZE] = result[head * tokens : (head + 1) * tokens]
+        first = head * tokens
+        columns = slice(head * HEAD_SIZE, (head + 1) * HEAD_SIZE)
+        here[:, columns] = result[first : first + rows]
+        gone[:, columns] = result[first + rows : first + tokens]
 
 
 def short_body(hidden_in, norm_gain, w_query, w_key, value_weight, w_out, doc_ids, positions):
@@ -395,6 +450,8 @@
     bf16 = jnp.bfloat16
     across_inner = swap_pairs(2, 1)
     which = place_inner.reshape(1)
+    places = jnp.stack([place_outer, place_inner, place_tensor])
+    hidden_in, which, places = lax.optimization_barrier((hidden_in, which, places))
 
     def send(value, axis, pairs):
         return lax.ppermute(value, axis, pairs)
@@ -416,49 +473,47 @@
     early = [[mine], [theirs], [one_mine], [one_theirs], [two_mine], [two_theirs]]
 
     facts = jnp.stack([doc_ids, positions])
-    facts = jnp.stack([facts, send(facts, "inner", across_inner)])
-
-    def relative(parts):
-        pieces = [parts[:, k * rows : (k + 1) * rows] for k in range(4)]
-        return jnp.stack(by_xor(pieces, place_tensor)).reshape(-1)
-
-    documents = relative(facts[:, 0])
-    row_positions = relative(facts[:, 1])
-    padding = 16 * 2 * HEAD_SIZE - documents.shape[0]
-    document_rows = jnp.pad(documents, (0, padding)).astype(bf16).reshape(16, 2 * HEAD_SIZE)
-    inverse = jnp.asarray(yarn_inverse(HEAD_SIZE) * 2, dtype=jnp.float32)
+    facts_there = send(after(facts, theirs), "inner", across_inner)
+    inverse = jnp.asarray([yarn_inverse(HEAD_SIZE) * 2], dtype=jnp.float32)
     signs = jnp.asarray([-1.0] * (HEAD_SIZE // 2) + [1.0] * (HEAD_SIZE // 2), dtype=jnp.float32)
     attention_gain = 0.1 * math.log(yarn_factor) + 1.0
-    angles = row_positions.astype(jnp.float32)[:, None] * inverse[None, :]
+    angles, documents, document_rows = call_kernel(
+        functools.partial(facts_kernel, rows), "facts", places, [facts, facts_there, inverse],
+        [None] * 3,
+        [
+            ((4 * slot_rows, HEAD_SIZE), jnp.float32, None),
+            ((4 * slot_rows, 1), jnp.float32, None),
+            ((16, 2 * HEAD_SIZE), bf16, None),
+        ],
+    )
     cosines = jnp.cos(angles) * attention_gain
     sines = jnp.sin(angles) * attention_gain * signs
 
-    tables = (cosines, sines)
-    ends_mine = send(after(two_mine, *tables), "tensor", [(1, 0), (2, 3)])
-    middle_mine = send(after(mine, two_mine, *tables), "tensor", middle)
-    ends_theirs = send(after(two_theirs, *tables), "tensor", [(1, 0), (2, 3)])
-    middle_theirs = send_across(after(others, two_mine, *tables), middle)
-    late = [[middle_mine, ends_mine], [middle_theirs, ends_theirs]]
-
-    def stack(name, chunks):
+    def stack(name, chunks, parts):
         flat = [array for chunk in chunks for array in chunk]
+        out = lambda count: ((count * slot_rows, half_width), bf16, None)
         return call_kernel(
             functools.partial(stack_kernel, [len(chunk) for chunk in chunks]), name, which, flat,
-            [None] * len(flat), [((len(chunks) * rows, half_width), bf16, None)],
+            [None] * len(flat), [out(count) for count in parts],
+        )
+
+    def sent_halves(wholes, kind):
+        count = wholes[0].shape[0]
+        wides = [whole.shape[1] // 2 for whole in wholes]
+        specs = [
+            pl.BlockSpec((count, wide), lambda step, which: (0, 1 - which[1])) for wide in wides
+        ]
+        return call_kernel(
+            copy_kernel, "sent", places, wholes, specs, [((count, sum(wides)), kind, None)]
         )[0]
-
-    def sent_half(whole):
-        wide = whole.shape[1] // 2
-        return lax.dynamic_slice_in_dim(whole, (1 - place_inner) * wide, wide, 1).astype(sum_type)
 
     def project_pair(stacked):
         keys, values = product(stacked, w_key), product(stacked, value_weight)
-        gone = jnp.concatenate([sent_half(keys), sent_half(values)], axis=1)
-        return keys, values, send(gone, "inner", across_inner)
+        return keys, values, send(sent_halves([keys, values], jnp.float32), "inner", across_inner)
 
     def project_query(stacked):
         queries = product(stacked, w_query)
-        return queries, send(sent_half(queries), "inner", across_inner)
+        return queries, send(sent_halves([queries], bf16), "inner", across_inner)
 
     def gather_pairs(pair):
         found = [pair]
@@ -479,19 +534,16 @@
             [((out_rows, 2 * HEAD_SIZE), bf16, None)],
         )[0]
 
-    early_stacked = stack("early_rows", early)
+    early_stacked, own_rows, two_rows = stack("early_rows", early, (3, 1, 1))
+    middle_rows = send(own_rows, "tensor", middle)
+    ends_rows = send(two_rows, "tensor", [(1, 0), (2, 3)])
     early_projected = project_pair(early_stacked)
-    late_stacked = stack("late_rows", late)
+    early_queries, early_came = project_query(early_stacked)
+    late_stacked = stack("late_rows", [[ends_rows, middle_rows]], (1,))[0]
     late_projected = project_pair(late_stacked)
-    early_queries, early_came = project_query(after(early_stacked, late_projected[0]))
     late_queries, late_came = project_query(late_stacked)
     early_pairs = gather_pairs(rotate_pair(early_projected, 0, [document_rows]))
     late_pairs = gather_pairs(rotate_pair(late_projected, early_rows, []))
-    key_documents = jnp.stack(
-        [array[early_rows:].reshape(1, -1)[:, : 4 * slot_rows] for array in early_pairs]
-    ).astype(jnp.int32)
-
-    places = jnp.stack([place_outer, place_inner, place_tensor])
 
     def attend(slot, *wait):
         queries, came = (late_queries, late_came) if slot == 3 else (early_queries, early_came)
@@ -503,28 +555,26 @@
         stacked = query_half // HEAD_SIZE * slot_rows
         return call_kernel(
             functools.partial(attention_kernel, slot, outer_count, rows), "attention", places,
-            [queries, came, cosines, sines, documents[:, None], key_documents] + early_pairs + late_pairs,
+            [queries, came, cosines, sines, documents] + early_pairs + late_pairs,
             [
                 half_spec, rows_spec(query_half, block),
                 rows_spec(HEAD_SIZE, slot), rows_spec(HEAD_SIZE, slot), rows_spec(1, slot),
-            ] + [None] * (1 + 2 * outer_count),
-            [((slot_rows, query_half), bf16, None)],
+            ] + [None] * (2 * outer_count),
+            [((rows, query_half), bf16, None)] * 2,
             scratch=[
                 pltpu.VMEM((stacked, 1), jnp.float32),
                 pltpu.VMEM((stacked, 1), jnp.float32),
                 pltpu.VMEM((stacked, HEAD_SIZE), jnp.float32),
             ],
+        )
+
+    def joined(slot, *wait):
+        here, gone = attend(slot, *wait)
+        came = send(gone, "inner", across_inner)
+        return call_kernel(
+            join_kernel, "join", places, [here, came], [None] * 2,
+            [((rows, 2 * query_half), bf16, None)],
         )[0]
-
-    lower = place_inner == 0
-
-    def joined(slot, *wait):
-        attended = attend(slot, *wait)
-        here = attended[:rows]
-        came = send(attended[rows:], "inner", across_inner)
-        return jnp.concatenate(
-            [jnp.where(lower, here, came), jnp.where(lower, came, here)], axis=1
-        )
 
     out_half = w_out.shape[1] // 2
     left, right = w_out[:, :out_half], w_out[:, out_half:]
@@ -544,7 +594,7 @@
     two_left = send(sum_left.astype(bf16), "tensor", two)
     sum_right = product(rows_2, right) + inward_right.astype(jnp.float32)
     two_right = send(sum_right.astype(bf16), "tensor", two)
-    came_inward = send(after(term_1, inward_right), "tensor", inward)
+    came_inward = send(after(term_1, inward_left), "tensor", inward)
     total = lax.optimization_barrier(product(rows_0, w_out))
     total = total + hidden_in.astype(jnp.float32) + came_outward.astype(jnp.float32)
     total = total + came_inward.astype(jnp.float32) + came_middle.astype(jnp.float32)

time: 112 us -> 108 us (0.964)
  Pallas kernels: 12 us -> 17.4 us
  waiting for transfers between devices: 40.5 us -> 35.7 us
  starting transfers between devices: 41.9 us -> 37.9 us
    ppermute x3 -> x2, starting transfers between devices: 9.3 us -> 1.68 us  [send_across(): return lax.ppermute(value, ('inner', 'tensor'), both)]
    pallas_call x9 -> x18, Pallas kernels: 12 us -> 17.4 us  [call_kernel(): pl.pallas_call(kernel, name=name, grid_spec=pltpu.PrefetchScalarGridSpec(...]
    ppermute x28 -> x27, waiting for transfers between devices: 36.4 us -> 31.1 us  [send(): return lax.ppermute(value, axis, pairs)]
    ppermute x28 -> x27, starting transfers between devices: 32.6 us -> 36.2 us  [send(): return lax.ppermute(value, axis, pairs)]
    ppermute x3 -> x2, waiting for transfers between devices: 4.06 us -> 4.57 us  [send_across(): return lax.ppermute(value, ('inner', 'tensor'), both)]
  transfers between devices with their start and end apart: 31 -> 29, of which waited for: 13 -> 10; matrix products, arithmetic and copies ran while one was open for 11% -> 11% of each run, Pallas kernels for 8% -> 16%
where the time goes in v3:
time: 108 us; the launch traced here: 106 us
  starting transfers between devices  37.9 us (35%)
  waiting for transfers between devices  35.7 us (33%)
  Pallas kernels  17.4 us (16%)
  matrix products  10.3 us (10%)
  other arithmetic  2.53 us (2%)
  local copies, waits for them, and re-layouts  1.83 us (2%)
    ppermute x27, starting transfers between devices, send(): return lax.ppermute(value, axis, pairs)  36.2 us
    ppermute x27, waiting for transfers between devices, send(): return lax.ppermute(value, axis, pairs)  31.1 us
    pallas_call x18, Pallas kernels, call_kernel(): pl.pallas_call(kernel, name=name, grid_spec=pltpu.PrefetchScalarGridSpec(...  17.4 us
    dot_general x12, matrix products, product(): return jnp.dot(left, right, preferred_element_type=jnp.float32)  10.3 us
    ppermute x2, waiting for transfers between devices, send_across(): return lax.ppermute(value, ('inner', 'tensor'), both)  4.57 us
  transfers between devices with their start and end apart: 29, of which 10 were waited for; matrix products, arithmetic and copies ran while one was open for 11% of the time, Pallas kernels for 16%

profile of v3, /device:TPU:2, one launch (start us, length us, event | category | flops | bytes accessed | tf_op | source)
XLA Modules:
  0.0 106.2 jit_solution(16903730676405858012)
XLA Ops:
  2.1 1.6 %collective-permute-start = (bf16[48,2048]{1,0:T(8,128)(2,1)S(1)}, bf16[48,2048]{1,0:T(8,128)(2,1)S(1)}, u32[]{:S(2)}, u32[]{:S(2)}) collective-permute-start(bf16[48,2048]{1,0:T(8,128)(2,1)S(1)} %get-tuple-element.32), channel_id=1, source_target_pairs={{0,4},{4,0},{1,5},{5,1},{2,6},{6,2},{3,7},{7,3},{8,12},{12,8},{9,1... | collective-permute-start | bytes 589832 | tf_op jit(solution)/shard_map/ppermute | solution.py:457
  3.7 2.6 %collective-permute-start.3 = (bf16[48,2048]{1,0:T(8,128)(2,1)S(1)}, bf16[48,2048]{1,0:T(8,128)(2,1)S(1)}, u32[]{:S(2)}, u32[]{:S(2)}) collective-permute-start(bf16[48,2048]{1,0:T(8,128)(2,1)S(1)} %get-tuple-element.31.refs_0_), channel_id=1, source_target_pairs={{0,2},{1,3},{2,0},{3,1},{4,6},{5,7},{6,4},{7,5},{8,10},{9,11},{10,... | collective-permute-start | bytes 589832 | tf_op jit(solution)/shard_map/ppermute | solution.py:457
  6.3 1.6 %collective-permute-start.1 = (bf16[48,2048]{1,0:T(8,128)(2,1)S(1)}, bf16[48,2048]{1,0:T(8,128)(2,1)S(1)}, u32[]{:S(2)}, u32[]{:S(2)}) collective-permute-start(bf16[48,2048]{1,0:T(8,128)(2,1)S(1)} %get-tuple-element.31.refs_0_), channel_id=1, source_target_pairs={{0,1},{1,0},{2,3},{3,2},{4,5},{5,4},{6,7},{7,6},{8,9},{9,8},{10,11... | collective-permute-start | bytes 589832 | tf_op jit(solution)/shard_map/ppermute | solution.py:457
  8.1 1.4 %collective-permute-start.2 = (bf16[48,2048]{1,0:T(8,128)(2,1)S(1)}, bf16[48,2048]{1,0:T(8,128)(2,1)S(1)}, u32[]{:S(2)}, u32[]{:S(2)}) collective-permute-start(bf16[48,2048]{1,0:T(8,128)(2,1)S(1)} %get-tuple-element.32), channel_id=1, source_target_pairs={{0,5},{1,4},{2,7},{3,6},{4,1},{5,0},{6,3},{7,2},{8,13},{9,12},{10,... | collective-permute-start | bytes 589832 | tf_op jit(solution)/shard_map/ppermute | solution.py:461
  10.8 8.4 %collective-permute-done.3.refs_4_ = bf16[48,2048]{1,0:T(8,128)(2,1)S(1)} collective-permute-done((bf16[48,2048]{1,0:T(8,128)(2,1)S(1)}, bf16[48,2048]{1,0:T(8,128)(2,1)S(1)}, u32[]{:S(2)}, u32[]{:S(2)}) %collective-permute-start.3) | collective-permute-done | bytes 196640 | tf_op jit(solution)/shard_map/ppermute | solution.py:457
  19.3 4.4 %collective-permute-done.4.refs_5_ = bf16[48,2048]{1,0:T(8,128)(2,1)S(1)} collective-permute-done((bf16[48,2048]{1,0:T(8,128)(2,1)S(1)}, bf16[48,2048]{1,0:T(8,128)(2,1)S(1)}, u32[]{:S(2)}, u32[]{:S(2)}) %collective-permute-start.4) | collective-permute-done | bytes 196640 | tf_op jit(solution)/shard_map/ppermute | solution.py:461
  25.5 1.6 %collective-permute-start.10 = (f32[288,256]{1,0:T(8,128)S(1)}, f32[288,256]{1,0:T(8,128)S(1)}, u32[]{:S(2)}, u32[]{:S(2)}) collective-permute-start(f32[288,256]{1,0:T(8,128)S(1)} %sent.6), channel_id=1, source_target_pairs={{0,4},{4,0},{1,5},{5,1},{2,6},{6,2},{3,7},{7,3},{8,12},{12,8},{9,1... | collective-permute-start | bytes 884744 | tf_op jit(solution)/shard_map/ppermute | solution.py:457
  29.1 1.4 %fusion.26.refs_0_.kept = f32[288,1024]{1,0:T(8,128)S(1)} fusion(bf16[288,2048]{1,0:T(8,128)(2,1)S(1)} %get-tuple-element.33, bf16[2048,1024]{1,0:T(8,128)(2,1)S(1)} %copy-done.5), kind=kOutput, calls=%fused_computation.21 | convolution fusion | flops 1207959552 | bytes 6553600 | tf_op jit(solution)/shard_map/dot_general | solution.py:273
  35.1 3.4 %collective-permute-done.6.refs_0_ = bf16[96,2048]{1,0:T(8,128)(2,1)S(1)} collective-permute-done((bf16[96,2048]{1,0:T(8,128)(2,1)S(1)}, bf16[96,2048]{1,0:T(8,128)(2,1)S(1)}, u32[]{:S(2)}, u32[]{:S(2)}) %collective-permute-start.6) | collective-permute-done | bytes 393248 | tf_op jit(solution)/shard_map/ppermute | solution.py:457
  41.7 3.3 %collective-permute-done.14.came = f32[96,256]{1,0:T(8,128)S(1)} collective-permute-done((f32[96,256]{1,0:T(8,128)S(1)}, f32[96,256]{1,0:T(8,128)S(1)}, u32[]{:S(2)}, u32[]{:S(2)}) %collective-permute-start.14) | collective-permute-done | bytes 98336 | tf_op jit(solution)/shard_map/ppermute | solution.py:457
  47.5 2.1 %collective-permute-done.8.came = bf16[96,512]{1,0:T(8,128)(2,1)S(1)} collective-permute-done((bf16[96,512]{1,0:T(8,128)(2,1)S(1)}, bf16[96,512]{1,0:T(8,128)(2,1)S(1)}, u32[]{:S(2)}, u32[]{:S(2)}) %collective-permute-start.8) | collective-permute-done | bytes 98336 | tf_op jit(solution)/shard_map/ppermute | solution.py:457
  50.3 2.8 %attention.4 = (bf16[48,512]{1,0:T(8,128)(2,1)S(1)}, bf16[48,512]{1,0:T(8,128)(2,1)S(1)}) custom-call(s32[3]{0:T(128)S(1)} %pad_add_fusion.1.which, f32[96,1024]{1,0:T(8,128)S(1)} %fusion.27.refs_0_.kept, bf16[96,512]{1,0:T(8,128)(2,1)S(1)} %collective-permute-done.8.came, f32[384,128]{1,0:T(8,128)S(1)} %get-tuple-element.52.cosines, ...), custom_call_target="tpu_custom_call" | custom-call | tf_op jit(solution)/shard_map/attention/pallas_call | solution.py:217
  53.1 1.6 %collective-permute-start.18 = (bf16[48,512]{1,0:T(8,128)(2,1)S(1)}, bf16[48,512]{1,0:T(8,128)(2,1)S(1)}, u32[]{:S(2)}, u32[]{:S(2)}) collective-permute-start(bf16[48,512]{1,0:T(8,128)(2,1)S(1)} %get-tuple-element.41), channel_id=1, source_target_pairs={{0,4},{4,0},{1,5},{5,1},{2,6},{6,2},{3,7},{7,3},{8,12},{12,8},{9,1... | collective-permute-start | bytes 147464 | tf_op jit(solution)/shard_map/ppermute | solution.py:457
  54.7 2.8 %attention.7 = (bf16[48,512]{1,0:T(8,128)(2,1)S(1)}, bf16[48,512]{1,0:T(8,128)(2,1)S(1)}) custom-call(s32[3]{0:T(128)S(1)} %pad_add_fusion.1.which, f32[288,1024]{1,0:T(8,128)S(1)} %fusion.26.refs_0_.kept, bf16[288,512]{1,0:T(8,128)(2,1)S(1)} %collective-permute-done.5.came, f32[384,128]{1,0:T(8,128)S(1)} %get-tuple-element.52.cosines, ...), custom_call_target="tpu_custom_call" | custom-call | tf_op jit(solution)/shard_map/attention/pallas_call | solution.py:217
  60.6 6.9 %collective-permute-start.22 = (bf16[48,2048]{1,0:T(8,128)(2,1)S(1)}, bf16[48,2048]{1,0:T(8,128)(2,1)S(1)}, u32[]{:S(2)}, u32[]{:S(2)}) collective-permute-start(bf16[48,2048]{1,0:T(8,128)(2,1)S(1)} %fusion.20), channel_id=1, source_target_pairs={{0,1},{3,2},{4,5},{7,6},{8,9},{11,10},{12,13},{15,14},{16,17},{19,... | collective-permute-start | bytes 589832 | tf_op jit(solution)/shard_map/ppermute | solution.py:457
  68.8 2.8 %attention.6 = (bf16[48,512]{1,0:T(8,128)(2,1)S(1)}, bf16[48,512]{1,0:T(8,128)(2,1)S(1)}) custom-call(s32[3]{0:T(128)S(1)} %pad_add_fusion.1.which, f32[288,1024]{1,0:T(8,128)S(1)} %fusion.26.refs_0_.kept, bf16[288,512]{1,0:T(8,128)(2,1)S(1)} %collective-permute-done.5.came, f32[384,128]{1,0:T(8,128)S(1)} %get-tuple-element.52.cosines, ...), custom_call_target="tpu_custom_call" | custom-call | tf_op jit(solution)/shard_map/attention/pallas_call | solution.py:217
  71.6 1.6 %collective-permute-start.20 = (bf16[48,512]{1,0:T(8,128)(2,1)S(1)}, bf16[48,512]{1,0:T(8,128)(2,1)S(1)}, u32[]{:S(2)}, u32[]{:S(2)}) collective-permute-start(bf16[48,512]{1,0:T(8,128)(2,1)S(1)} %get-tuple-element.46), channel_id=1, source_target_pairs={{0,4},{4,0},{1,5},{5,1},{2,6},{6,2},{3,7},{7,3},{8,12},{12,8},{9,1... | collective-permute-start | bytes 147464 | tf_op jit(solution)/shard_map/ppermute | solution.py:457
  73.2 2.8 %attention.5 = (bf16[48,512]{1,0:T(8,128)(2,1)S(1)}, bf16[48,512]{1,0:T(8,128)(2,1)S(1)}) custom-call(s32[3]{0:T(128)S(1)} %pad_add_fusion.1.which, f32[288,1024]{1,0:T(8,128)S(1)} %fusion.26.refs_0_.kept, bf16[288,512]{1,0:T(8,128)(2,1)S(1)} %collective-permute-done.5.came, f32[384,128]{1,0:T(8,128)S(1)} %get-tuple-element.52.cosines, ...), custom_call_target="tpu_custom_call" | custom-call | tf_op jit(solution)/shard_map/attention/pallas_call | solution.py:217
  78.5 1.6 %convolution_convert_fusion = bf16[48,4096]{1,0:T(8,128)(2,1)S(1)} fusion(bf16[48,1024]{1,0:T(8,128)(2,1)S(1)} %join.6, bf16[1024,4096]{1,0:T(8,128)(2,1)S(1)} %bitcast.28), kind=kOutput, calls=%fused_computation | convolution fusion | flops 402849792 | bytes 8880128 | tf_op jit(solution)/shard_map/dot_general | solution.py:273
  82.8 3.9 %collective-permute-start.28 = (bf16[48,2048]{1,0:T(8,128)(2,1)S(1)}, bf16[48,2048]{1,0:T(8,128)(2,1)S(1)}, u32[]{:S(2)}, u32[]{:S(2)}) collective-permute-start(bf16[48,2048]{1,0:T(8,128)(2,1)S(1)} %fusion.14), channel_id=1, source_target_pairs={{0,2},{1,3},{2,0},{3,1},{4,6},{5,7},{6,4},{7,5},{8,10},{9,11},{10,... | collective-permute-start | bytes 589832 | tf_op jit(solution)/shard_map/ppermute | solution.py:457
  87.6 3.7 %collective-permute-start.23 = (bf16[48,4096]{1,0:T(8,128)(2,1)S(1)}, bf16[48,4096]{1,0:T(8,128)(2,1)S(1)}, u32[]{:S(2)}, u32[]{:S(2)}) collective-permute-start(bf16[48,4096]{1,0:T(8,128)(2,1)S(1)} %convolution_convert_fusion), channel_id=1, source_target_pairs={{0,1},{3,2},{4,5},{7,6},{8,9},{11,10},{12,13},{15,14},{16,17},{19,... | collective-permute-start | bytes 1179656 | tf_op jit(solution)/shard_map/ppermute | solution.py:457
  91.3 1.6 %fusion.32 = f32[48,4096]{1,0:T(8,128)S(1)} fusion(bf16[48,1024]{1,0:T(8,128)(2,1)S(1)} %join.5, bf16[1024,4096]{1,0:T(8,128)(2,1)S(1)} %bitcast.28), kind=kOutput, calls=%fused_computation.27 | convolution fusion | flops 402653184 | bytes 9273344 | tf_op jit(solution)/shard_map/dot_general | solution.py:273
  92.9 8.1 %collective-permute-done.28 = bf16[48,2048]{1,0:T(8,128)(2,1)S(1)} collective-permute-done((bf16[48,2048]{1,0:T(8,128)(2,1)S(1)}, bf16[48,2048]{1,0:T(8,128)(2,1)S(1)}, u32[]{:S(2)}, u32[]{:S(2)}) %collective-permute-start.28) | collective-permute-done | bytes 196640 | tf_op jit(solution)/shard_map/ppermute | solution.py:457
  100.9 4.2 %collective-permute-done.26 = bf16[48,2048]{1,0:T(8,128)(2,1)S(1)} collective-permute-done((bf16[48,2048]{1,0:T(8,128)(2,1)S(1)}, bf16[48,2048]{1,0:T(8,128)(2,1)S(1)}, u32[]{:S(2)}, u32[]{:S(2)}) %collective-permute-start.26) | collective-permute-done | bytes 196640 | tf_op jit(solution)/shard_map/ppermute | solution.py:457
  (90 shorter events, 29.7 us)
Async XLA Ops:
  2.1 8.1 %collective-permute-start = (bf16[48,2048]{1,0:T(8,128)(2,1)S(1)}, bf16[48,2048]{1,0:T(8,128)(2,1)S(1)}, u32[]{:S(2)}, u32[]{:S(2)}) collective-permute-start(bf16[48,2048]{1,0:T(8,128)(2,1)S(1)} %get-tuple-element.32), channel_id=1, source_target_pairs={{0,4},{4,0},{1,5},{5,1},{2,6},{6,2},{3,7},{7,3},{8,12},{12,8},{9,1... | collective-permute-start | bytes 589832 | tf_op jit(solution)/shard_map/ppermute | solution.py:457
  3.7 15.6 %collective-permute-start.3 = (bf16[48,2048]{1,0:T(8,128)(2,1)S(1)}, bf16[48,2048]{1,0:T(8,128)(2,1)S(1)}, u32[]{:S(2)}, u32[]{:S(2)}) collective-permute-start(bf16[48,2048]{1,0:T(8,128)(2,1)S(1)} %get-tuple-element.31.refs_0_), channel_id=1, source_target_pairs={{0,2},{1,3},{2,0},{3,1},{4,6},{5,7},{6,4},{7,5},{8,10},{9,11},{10,... | collective-permute-start | bytes 589832 | tf_op jit(solution)/shard_map/ppermute | solution.py:457
  6.3 13.0 %collective-permute-start.1 = (bf16[48,2048]{1,0:T(8,128)(2,1)S(1)}, bf16[48,2048]{1,0:T(8,128)(2,1)S(1)}, u32[]{:S(2)}, u32[]{:S(2)}) collective-permute-start(bf16[48,2048]{1,0:T(8,128)(2,1)S(1)} %get-tuple-element.31.refs_0_), channel_id=1, source_target_pairs={{0,1},{1,0},{2,3},{3,2},{4,5},{5,4},{6,7},{7,6},{8,9},{9,8},{10,11... | collective-permute-start | bytes 589832 | tf_op jit(solution)/shard_map/ppermute | solution.py:457
  7.9 15.8 %collective-permute-start.4 = (bf16[48,2048]{1,0:T(8,128)(2,1)S(1)}, bf16[48,2048]{1,0:T(8,128)(2,1)S(1)}, u32[]{:S(2)}, u32[]{:S(2)}) collective-permute-start(bf16[48,2048]{1,0:T(8,128)(2,1)S(1)} %get-tuple-element.32), channel_id=1, source_target_pairs={{0,6},{1,7},{2,4},{3,5},{4,2},{5,3},{6,0},{7,1},{8,14},{9,15},{10,... | collective-permute-start | bytes 589832 | tf_op jit(solution)/shard_map/ppermute | solution.py:461
  8.1 15.7 %collective-permute-start.2 = (bf16[48,2048]{1,0:T(8,128)(2,1)S(1)}, bf16[48,2048]{1,0:T(8,128)(2,1)S(1)}, u32[]{:S(2)}, u32[]{:S(2)}) collective-permute-start(bf16[48,2048]{1,0:T(8,128)(2,1)S(1)} %get-tuple-element.32), channel_id=1, source_target_pairs={{0,5},{1,4},{2,7},{3,6},{4,1},{5,0},{6,3},{7,2},{8,13},{9,12},{10,... | collective-permute-start | bytes 589832 | tf_op jit(solution)/shard_map/ppermute | solution.py:461
  10.3 21.5 %collective-permute-start.9 = (s32[2,192]{1,0:T(2,128)S(1)}, s32[2,192]{1,0:T(2,128)S(1)}, u32[]{:S(2)}, u32[]{:S(2)}) collective-permute-start(s32[2,192]{1,0:T(2,128)S(1)} %pad_add_fusion.here), channel_id=1, source_target_pairs={{0,4},{4,0},{1,5},{5,1},{2,6},{6,2},{3,7},{7,3},{8,12},{12,8},{9,1... | collective-permute-start | bytes 4616 | tf_op jit(solution)/shard_map/ppermute | solution.py:457
  25.5 8.7 %collective-permute-start.10 = (f32[288,256]{1,0:T(8,128)S(1)}, f32[288,256]{1,0:T(8,128)S(1)}, u32[]{:S(2)}, u32[]{:S(2)}) collective-permute-start(f32[288,256]{1,0:T(8,128)S(1)} %sent.6), channel_id=1, source_target_pairs={{0,4},{4,0},{1,5},{5,1},{2,6},{6,2},{3,7},{7,3},{8,12},{12,8},{9,1... | collective-permute-start | bytes 884744 | tf_op jit(solution)/shard_map/ppermute | solution.py:457
  27.1 11.3 %collective-permute-start.6 = (bf16[96,2048]{1,0:T(8,128)(2,1)S(1)}, bf16[96,2048]{1,0:T(8,128)(2,1)S(1)}, u32[]{:S(2)}, u32[]{:S(2)}) collective-permute-start(bf16[96,2048]{1,0:T(8,128)(2,1)S(1)} %get-tuple-element.34), channel_id=1, source_target_pairs={{1,0},{2,3},{5,4},{6,7},{9,8},{10,11},{13,12},{14,15},{17,16},{18,... | collective-permute-start | bytes 1179656 | tf_op jit(solution)/shard_map/ppermute | solution.py:457
  28.4 10.0 %collective-permute-start.7 = (bf16[96,2048]{1,0:T(8,128)(2,1)S(1)}, bf16[96,2048]{1,0:T(8,128)(2,1)S(1)}, u32[]{:S(2)}, u32[]{:S(2)}) collective-permute-start(bf16[96,2048]{1,0:T(8,128)(2,1)S(1)} %get-tuple-element.35), channel_id=1, source_target_pairs={{1,2},{2,1},{5,6},{6,5},{9,10},{10,9},{13,14},{14,13},{17,18},{18,... | collective-permute-start | bytes 1179656 | tf_op jit(solution)/shard_map/ppermute | solution.py:457
  31.1 23.6 %collective-permute-start.5 = (bf16[288,512]{1,0:T(8,128)(2,1)S(1)}, bf16[288,512]{1,0:T(8,128)(2,1)S(1)}, u32[]{:S(2)}, u32[]{:S(2)}) collective-permute-start(bf16[288,512]{1,0:T(8,128)(2,1)S(1)} %sent.4), channel_id=1, source_target_pairs={{0,4},{4,0},{1,5},{5,1},{2,6},{6,2},{3,7},{7,3},{8,12},{12,8},{9,1... | collective-permute-start | bytes 884744 | tf_op jit(solution)/shard_map/ppermute | solution.py:457
  34.4 11.2 %collective-permute-start.13 = (bf16[304,256]{1,0:T(8,128)(2,1)S(1)}, bf16[304,256]{1,0:T(8,128)(2,1)S(1)}, u32[]{:S(2)}, u32[]{:S(2)}) collective-permute-start(bf16[304,256]{1,0:T(8,128)(2,1)S(1)} %pair.2.refs_0_), channel_id=1, source_target_pairs={{0,24},{8,16},{16,8},{24,0},{1,25},{9,17},{17,9},{25,1},{2,26},{10... | collective-permute-start | bytes 466952 | tf_op jit(solution)/shard_map/ppermute | solution.py:457
  34.4 11.3 %collective-permute-start.12 = (bf16[304,256]{1,0:T(8,128)(2,1)S(1)}, bf16[304,256]{1,0:T(8,128)(2,1)S(1)}, u32[]{:S(2)}, u32[]{:S(2)}) collective-permute-start(bf16[304,256]{1,0:T(8,128)(2,1)S(1)} %pair.2.refs_0_), channel_id=1, source_target_pairs={{0,16},{8,24},{16,0},{24,8},{1,17},{9,25},{17,1},{25,9},{2,18},{10... | collective-permute-start | bytes 466952 | tf_op jit(solution)/shard_map/ppermute | solution.py:457
  38.5 8.3 %collective-permute-start.11 = (bf16[304,256]{1,0:T(8,128)(2,1)S(1)}, bf16[304,256]{1,0:T(8,128)(2,1)S(1)}, u32[]{:S(2)}, u32[]{:S(2)}) collective-permute-start(bf16[304,256]{1,0:T(8,128)(2,1)S(1)} %pair.2.refs_0_), channel_id=1, source_target_pairs={{0,8},{8,0},{16,24},{24,16},{1,9},{9,1},{17,25},{25,17},{2,10},{10... | collective-permute-start | bytes 466952 | tf_op jit(solution)/shard_map/ppermute | solution.py:457
  39.7 5.3 %collective-permute-start.14 = (f32[96,256]{1,0:T(8,128)S(1)}, f32[96,256]{1,0:T(8,128)S(1)}, u32[]{:S(2)}, u32[]{:S(2)}) collective-permute-start(f32[96,256]{1,0:T(8,128)S(1)} %sent.7), channel_id=1, source_target_pairs={{0,4},{4,0},{1,5},{5,1},{2,6},{6,2},{3,7},{7,3},{8,12},{12,8},{9,1... | collective-permute-start | bytes 294920 | tf_op jit(solution)/shard_map/ppermute | solution.py:457
  57.6 19.1 %collective-permute-start.25 = (bf16[48,512]{1,0:T(8,128)(2,1)S(1)}, bf16[48,512]{1,0:T(8,128)(2,1)S(1)}, u32[]{:S(2)}, u32[]{:S(2)}) collective-permute-start(bf16[48,512]{1,0:T(8,128)(2,1)S(1)} %get-tuple-element.49), channel_id=1, source_target_pairs={{0,4},{4,0},{1,5},{5,1},{2,6},{6,2},{3,7},{7,3},{8,12},{12,8},{9,1... | collective-permute-start | bytes 147464 | tf_op jit(solution)/shard_map/ppermute | solution.py:457
  60.6 26.1 %collective-permute-start.22 = (bf16[48,2048]{1,0:T(8,128)(2,1)S(1)}, bf16[48,2048]{1,0:T(8,128)(2,1)S(1)}, u32[]{:S(2)}, u32[]{:S(2)}) collective-permute-start(bf16[48,2048]{1,0:T(8,128)(2,1)S(1)} %fusion.20), channel_id=1, source_target_pairs={{0,1},{3,2},{4,5},{7,6},{8,9},{11,10},{12,13},{15,14},{16,17},{19,... | collective-permute-start | bytes 589832 | tf_op jit(solution)/shard_map/ppermute | solution.py:457
  67.5 14.4 %collective-permute-start.27 = (bf16[48,2048]{1,0:T(8,128)(2,1)S(1)}, bf16[48,2048]{1,0:T(8,128)(2,1)S(1)}, u32[]{:S(2)}, u32[]{:S(2)}) collective-permute-start(bf16[48,2048]{1,0:T(8,128)(2,1)S(1)} %fusion.23), channel_id=1, source_target_pairs={{0,1},{3,2},{4,5},{7,6},{8,9},{11,10},{12,13},{15,14},{16,17},{19,... | collective-permute-start | bytes 589832 | tf_op jit(solution)/shard_map/ppermute | solution.py:457
  71.6 6.3 %collective-permute-start.20 = (bf16[48,512]{1,0:T(8,128)(2,1)S(1)}, bf16[48,512]{1,0:T(8,128)(2,1)S(1)}, u32[]{:S(2)}, u32[]{:S(2)}) collective-permute-start(bf16[48,512]{1,0:T(8,128)(2,1)S(1)} %get-tuple-element.46), channel_id=1, source_target_pairs={{0,4},{4,0},{1,5},{5,1},{2,6},{6,2},{3,7},{7,3},{8,12},{12,8},{9,1... | collective-permute-start | bytes 147464 | tf_op jit(solution)/shard_map/ppermute | solution.py:457
  76.1 5.3 %collective-permute-start.19 = (bf16[48,512]{1,0:T(8,128)(2,1)S(1)}, bf16[48,512]{1,0:T(8,128)(2,1)S(1)}, u32[]{:S(2)}, u32[]{:S(2)}) collective-permute-start(bf16[48,512]{1,0:T(8,128)(2,1)S(1)} %get-tuple-element.44), channel_id=1, source_target_pairs={{0,4},{4,0},{1,5},{5,1},{2,6},{6,2},{3,7},{7,3},{8,12},{12,8},{9,1... | collective-permute-start | bytes 147464 | tf_op jit(solution)/shard_map/ppermute | solution.py:457
  76.6 28.5 %collective-permute-start.24 = (bf16[48,4096]{1,0:T(8,128)(2,1)S(1)}, bf16[48,4096]{1,0:T(8,128)(2,1)S(1)}, u32[]{:S(2)}, u32[]{:S(2)}) collective-permute-start(bf16[48,4096]{1,0:T(8,128)(2,1)S(1)} %pad_maximum_fusion), channel_id=1, source_target_pairs={{1,2},{2,1},{5,6},{6,5},{9,10},{10,9},{13,14},{14,13},{17,18},{18,... | collective-permute-start | bytes 1179656 | tf_op jit(solution)/shard_map/ppermute | solution.py:457
  80.0 25.1 %collective-permute-start.21 = (bf16[48,4096]{1,0:T(8,128)(2,1)S(1)}, bf16[48,4096]{1,0:T(8,128)(2,1)S(1)}, u32[]{:S(2)}, u32[]{:S(2)}) collective-permute-start(bf16[48,4096]{1,0:T(8,128)(2,1)S(1)} %convolution_convert_fusion), channel_id=1, source_target_pairs={{1,0},{2,3},{5,4},{6,7},{9,8},{10,11},{13,12},{14,15},{17,16},{18,... | collective-permute-start | bytes 1179656 | tf_op jit(solution)/shard_map/ppermute | solution.py:457
  82.8 18.1 %collective-permute-start.28 = (bf16[48,2048]{1,0:T(8,128)(2,1)S(1)}, bf16[48,2048]{1,0:T(8,128)(2,1)S(1)}, u32[]{:S(2)}, u32[]{:S(2)}) collective-permute-start(bf16[48,2048]{1,0:T(8,128)(2,1)S(1)} %fusion.14), channel_id=1, source_target_pairs={{0,2},{1,3},{2,0},{3,1},{4,6},{5,7},{6,4},{7,5},{8,10},{9,11},{10,... | collective-permute-start | bytes 589832 | tf_op jit(solution)/shard_map/ppermute | solution.py:457
  87.5 17.6 %collective-permute-start.26 = (bf16[48,2048]{1,0:T(8,128)(2,1)S(1)}, bf16[48,2048]{1,0:T(8,128)(2,1)S(1)}, u32[]{:S(2)}, u32[]{:S(2)}) collective-permute-start(bf16[48,2048]{1,0:T(8,128)(2,1)S(1)} %fusion.17), channel_id=1, source_target_pairs={{0,2},{1,3},{2,0},{3,1},{4,6},{5,7},{6,4},{7,5},{8,10},{9,11},{10,... | collective-permute-start | bytes 589832 | tf_op jit(solution)/shard_map/ppermute | solution.py:457
  87.6 17.5 %collective-permute-start.23 = (bf16[48,4096]{1,0:T(8,128)(2,1)S(1)}, bf16[48,4096]{1,0:T(8,128)(2,1)S(1)}, u32[]{:S(2)}, u32[]{:S(2)}) collective-permute-start(bf16[48,4096]{1,0:T(8,128)(2,1)S(1)} %convolution_convert_fusion), channel_id=1, source_target_pairs={{0,1},{3,2},{4,5},{7,6},{8,9},{11,10},{12,13},{15,14},{16,17},{19,... | collective-permute-start | bytes 1179656 | tf_op jit(solution)/shard_map/ppermute | solution.py:457
  (15 other events, 140.0 us)

commit v4 on v3

--- a/solution.py
+++ b/solution.py
@@ -473,7 +473,7 @@
     early = [[mine], [theirs], [one_mine], [one_theirs], [two_mine], [two_theirs]]
 
     facts = jnp.stack([doc_ids, positions])
-    facts_there = send(after(facts, theirs), "inner", across_inner)
+    facts_there = send(after(facts, two_theirs), "inner", across_inner)
     inverse = jnp.asarray([yarn_inverse(HEAD_SIZE) * 2], dtype=jnp.float32)
     signs = jnp.asarray([-1.0] * (HEAD_SIZE // 2) + [1.0] * (HEAD_SIZE // 2), dtype=jnp.float32)
     attention_gain = 0.1 * math.log(yarn_factor) + 1.0
@@ -576,30 +576,18 @@
             [((rows, 2 * query_half), bf16, None)],
         )[0]
 
-    out_half = w_out.shape[1] // 2
-    left, right = w_out[:, :out_half], w_out[:, out_half:]
-    inward, outward = [(0, 1), (3, 2)], [(1, 0), (2, 3)]
     rows_3 = joined(3)
     rows_2 = joined(2)
-    term_left = product(rows_3, left).astype(bf16)
-    inward_left = send(term_left, "tensor", inward)
-    term_right = product(rows_3, right).astype(bf16)
-    came_middle = send(jnp.concatenate([term_left, term_right], axis=1), "tensor", middle)
-    inward_right = send(term_right, "tensor", inward)
-    rows_1 = joined(1, term_left, term_right)
-    rows_0 = joined(0, term_left, term_right)
-    term_1 = product(rows_1, w_out).astype(bf16)
-    came_outward = send(term_1, "tensor", outward)
-    sum_left = product(rows_2, left) + after(inward_left, term_1).astype(jnp.float32)
-    two_left = send(sum_left.astype(bf16), "tensor", two)
-    sum_right = product(rows_2, right) + inward_right.astype(jnp.float32)
-    two_right = send(sum_right.astype(bf16), "tensor", two)
-    came_inward = send(after(term_1, inward_left), "tensor", inward)
+    term_3 = product(rows_3, w_out).astype(bf16)
+    came_3 = send(term_3, "tensor", swap_pairs(4, 3))
+    came_2 = send(product(rows_2, w_out).astype(bf16), "tensor", two)
+    rows_1 = joined(1, term_3)
+    came_1 = send(product(rows_1, w_out).astype(bf16), "tensor", one)
+    rows_0 = joined(0, term_3)
     total = lax.optimization_barrier(product(rows_0, w_out))
-    total = total + hidden_in.astype(jnp.float32) + came_outward.astype(jnp.float32)
-    total = total + came_inward.astype(jnp.float32) + came_middle.astype(jnp.float32)
-    came_2 = jnp.concatenate([two_left, two_right], axis=1)
-    return (total + came_2.astype(jnp.float32)).astype(bf16)
+    total = total + hidden_in.astype(jnp.float32) + came_1.astype(jnp.float32)
+    total = total + came_2.astype(jnp.float32) + came_3.astype(jnp.float32)
+    return total.astype(bf16)
 
 
 def solution(mesh):

time: 108 us -> 102 us (0.944)
  starting transfers between devices: 37.9 us -> 29.2 us
  waiting for transfers between devices: 35.7 us -> 39.8 us
    ppermute x27 -> x23, starting transfers between devices: 36.2 us -> 25.2 us  [send(): return lax.ppermute(value, axis, pairs)]
    ppermute x2, waiting for transfers between devices: 4.57 us -> 10.3 us  [send_across(): return lax.ppermute(value, ('inner', 'tensor'), both)]
    ppermute x2, starting transfers between devices: 1.68 us -> 4 us  [send_across(): return lax.ppermute(value, ('inner', 'tensor'), both)]
    ppermute x27 -> x23, waiting for transfers between devices: 31.1 us -> 29.5 us  [send(): return lax.ppermute(value, axis, pairs)]
    dot_general x12 -> x10, matrix products: 10.3 us -> 10.1 us  [product(): return jnp.dot(left, right, preferred_element_type=jnp.float32)]
  transfers between devices with their start and end apart: 29 -> 25, of which waited for: 10 -> 10; matrix products, arithmetic and copies ran while one was open for 11% -> 11% of each run, Pallas kernels for 16% -> 17%
where the time goes in v4:
time: 102 us; the launch traced here: 101 us
  waiting for transfers between devices  39.8 us (39%)
  starting transfers between devices  29.2 us (29%)
  Pallas kernels  17.4 us (17%)
  matrix products  10.1 us (10%)
  other arithmetic  2.46 us (2%)
  local copies, waits for them, and re-layouts  1.83 us (2%)
    ppermute x23, waiting for transfers between devices, send(): return lax.ppermute(value, axis, pairs)  29.5 us
    ppermute x23, starting transfers between devices, send(): return lax.ppermute(value, axis, pairs)  25.2 us
    pallas_call x18, Pallas kernels, call_kernel(): pl.pallas_call(kernel, name=name, grid_spec=pltpu.PrefetchScalarGridSpec(...  17.4 us
    ppermute x2, waiting for transfers between devices, send_across(): return lax.ppermute(value, ('inner', 'tensor'), both)  10.3 us
    dot_general x10, matrix products, product(): return jnp.dot(left, right, preferred_element_type=jnp.float32)  10.1 us
    ppermute x2, starting transfers between devices, send_across(): return lax.ppermute(value, ('inner', 'tensor'), both)  4 us
  transfers between devices with their start and end apart: 25, of which 10 were waited for; matrix products, arithmetic and copies ran while one was open for 11% of the time, Pallas kernels for 17%

profile of v4, /device:TPU:2, one launch (start us, length us, event | category | flops | bytes accessed | tf_op | source)
XLA Modules:
  0.0 101.1 jit_solution(4071213960132393226)
XLA Ops:
  2.1 3.6 %collective-permute-start.4 = (bf16[48,2048]{1,0:T(8,128)(2,1)S(1)}, bf16[48,2048]{1,0:T(8,128)(2,1)S(1)}, u32[]{:S(2)}, u32[]{:S(2)}) collective-permute-start(bf16[48,2048]{1,0:T(8,128)(2,1)S(1)} %get-tuple-element.30), channel_id=1, source_target_pairs={{0,6},{1,7},{2,4},{3,5},{4,2},{5,3},{6,0},{7,1},{8,14},{9,15},{10,... | collective-permute-start | bytes 589832 | tf_op jit(solution)/shard_map/ppermute | solution.py:461
  6.1 1.6 %collective-permute-start.1 = (bf16[48,2048]{1,0:T(8,128)(2,1)S(1)}, bf16[48,2048]{1,0:T(8,128)(2,1)S(1)}, u32[]{:S(2)}, u32[]{:S(2)}) collective-permute-start(bf16[48,2048]{1,0:T(8,128)(2,1)S(1)} %get-tuple-element.29.refs_0_), channel_id=1, source_target_pairs={{0,1},{1,0},{2,3},{3,2},{4,5},{5,4},{6,7},{7,6},{8,9},{9,8},{10,11... | collective-permute-start | bytes 589832 | tf_op jit(solution)/shard_map/ppermute | solution.py:457
  8.0 1.5 %collective-permute-start = (bf16[48,2048]{1,0:T(8,128)(2,1)S(1)}, bf16[48,2048]{1,0:T(8,128)(2,1)S(1)}, u32[]{:S(2)}, u32[]{:S(2)}) collective-permute-start(bf16[48,2048]{1,0:T(8,128)(2,1)S(1)} %get-tuple-element.30), channel_id=1, source_target_pairs={{0,4},{4,0},{1,5},{5,1},{2,6},{6,2},{3,7},{7,3},{8,12},{12,8},{9,1... | collective-permute-start | bytes 589832 | tf_op jit(solution)/shard_map/ppermute | solution.py:457
  10.2 10.0 %collective-permute-done.4.refs_5_ = bf16[48,2048]{1,0:T(8,128)(2,1)S(1)} collective-permute-done((bf16[48,2048]{1,0:T(8,128)(2,1)S(1)}, bf16[48,2048]{1,0:T(8,128)(2,1)S(1)}, u32[]{:S(2)}, u32[]{:S(2)}) %collective-permute-start.4) | collective-permute-done | bytes 196640 | tf_op jit(solution)/shard_map/ppermute | solution.py:461
  20.3 1.5 %collective-permute-start.9 = (s32[2,192]{1,0:T(2,128)S(1)}, s32[2,192]{1,0:T(2,128)S(1)}, u32[]{:S(2)}, u32[]{:S(2)}) collective-permute-start(s32[2,192]{1,0:T(2,128)S(1)} %pad_add_fusion.here), channel_id=1, source_target_pairs={{0,4},{4,0},{1,5},{5,1},{2,6},{6,2},{3,7},{7,3},{8,12},{12,8},{9,1... | collective-permute-start | bytes 4616 | tf_op jit(solution)/shard_map/ppermute | solution.py:457
  21.8 1.6 %collective-permute-done.3.refs_4_ = bf16[48,2048]{1,0:T(8,128)(2,1)S(1)} collective-permute-done((bf16[48,2048]{1,0:T(8,128)(2,1)S(1)}, bf16[48,2048]{1,0:T(8,128)(2,1)S(1)}, u32[]{:S(2)}, u32[]{:S(2)}) %collective-permute-start.3) | collective-permute-done | bytes 196640 | tf_op jit(solution)/shard_map/ppermute | solution.py:457
  25.4 1.5 %collective-permute-start.10 = (f32[288,256]{1,0:T(8,128)S(1)}, f32[288,256]{1,0:T(8,128)S(1)}, u32[]{:S(2)}, u32[]{:S(2)}) collective-permute-start(f32[288,256]{1,0:T(8,128)S(1)} %sent.6), channel_id=1, source_target_pairs={{0,4},{4,0},{1,5},{5,1},{2,6},{6,2},{3,7},{7,3},{8,12},{12,8},{9,1... | collective-permute-start | bytes 884744 | tf_op jit(solution)/shard_map/ppermute | solution.py:457
  29.0 1.4 %fusion.refs_0_.kept = f32[288,1024]{1,0:T(8,128)S(1)} fusion(bf16[288,2048]{1,0:T(8,128)(2,1)S(1)} %get-tuple-element.31, bf16[2048,1024]{1,0:T(8,128)(2,1)S(1)} %copy-done.5), kind=kOutput, calls=%fused_computation.8 | convolution fusion | flops 1207959552 | bytes 6553600 | tf_op jit(solution)/shard_map/dot_general | solution.py:273
  33.2 1.8 %collective-permute-done.10.came = f32[288,256]{1,0:T(8,128)S(1)} collective-permute-done((f32[288,256]{1,0:T(8,128)S(1)}, f32[288,256]{1,0:T(8,128)S(1)}, u32[]{:S(2)}, u32[]{:S(2)}) %collective-permute-start.10) | collective-permute-done | bytes 294944 | tf_op jit(solution)/shard_map/ppermute | solution.py:457
  35.5 2.0 %collective-permute-done.6.refs_0_ = bf16[96,2048]{1,0:T(8,128)(2,1)S(1)} collective-permute-done((bf16[96,2048]{1,0:T(8,128)(2,1)S(1)}, bf16[96,2048]{1,0:T(8,128)(2,1)S(1)}, u32[]{:S(2)}, u32[]{:S(2)}) %collective-permute-start.6) | collective-permute-done | bytes 393248 | tf_op jit(solution)/shard_map/ppermute | solution.py:457
  38.8 1.3 %collective-permute-start.14 = (f32[96,256]{1,0:T(8,128)S(1)}, f32[96,256]{1,0:T(8,128)S(1)}, u32[]{:S(2)}, u32[]{:S(2)}) collective-permute-start(f32[96,256]{1,0:T(8,128)S(1)} %sent.7), channel_id=1, source_target_pairs={{0,4},{4,0},{1,5},{5,1},{2,6},{6,2},{3,7},{7,3},{8,12},{12,8},{9,1... | collective-permute-start | bytes 294920 | tf_op jit(solution)/shard_map/ppermute | solution.py:457
  41.5 2.5 %collective-permute-done.14.came = f32[96,256]{1,0:T(8,128)S(1)} collective-permute-done((f32[96,256]{1,0:T(8,128)S(1)}, f32[96,256]{1,0:T(8,128)S(1)}, u32[]{:S(2)}, u32[]{:S(2)}) %collective-permute-start.14) | collective-permute-done | bytes 98336 | tf_op jit(solution)/shard_map/ppermute | solution.py:457
  50.1 2.8 %attention.4 = (bf16[48,512]{1,0:T(8,128)(2,1)S(1)}, bf16[48,512]{1,0:T(8,128)(2,1)S(1)}) custom-call(s32[3]{0:T(128)S(1)} %pad_add_fusion.1.which, f32[96,1024]{1,0:T(8,128)S(1)} %fusion.1.refs_0_.kept, bf16[96,512]{1,0:T(8,128)(2,1)S(1)} %collective-permute-done.8.came, f32[384,128]{1,0:T(8,128)S(1)} %get-tuple-element.48.cosines, ...), custom_call_target="tpu_custom_call" | custom-call | tf_op jit(solution)/shard_map/attention/pallas_call | solution.py:217
  53.8 2.8 %attention.7 = (bf16[48,512]{1,0:T(8,128)(2,1)S(1)}, bf16[48,512]{1,0:T(8,128)(2,1)S(1)}) custom-call(s32[3]{0:T(128)S(1)} %pad_add_fusion.1.which, f32[288,1024]{1,0:T(8,128)S(1)} %fusion.refs_0_.kept, bf16[288,512]{1,0:T(8,128)(2,1)S(1)} %collective-permute-done.5.came, f32[384,128]{1,0:T(8,128)S(1)} %get-tuple-element.48.cosines, ...), custom_call_target="tpu_custom_call" | custom-call | tf_op jit(solution)/shard_map/attention/pallas_call | solution.py:217
  58.7 1.6 %convolution_convert_fusion.2 = bf16[48,4096]{1,0:T(8,128)(2,1)S(1)} fusion(bf16[48,1024]{1,0:T(8,128)(2,1)S(1)} %join.4, bf16[1024,4096]{1,0:T(8,128)(2,1)S(1)} %bitcast.28), kind=kOutput, calls=%fused_computation.2 | convolution fusion | flops 402849792 | bytes 8880128 | tf_op jit(solution)/shard_map/dot_general | solution.py:273
  60.3 4.6 %collective-permute-start.24 = (bf16[48,4096]{1,0:T(8,128)(2,1)S(1)}, bf16[48,4096]{1,0:T(8,128)(2,1)S(1)}, u32[]{:S(2)}, u32[]{:S(2)}) collective-permute-start(bf16[48,4096]{1,0:T(8,128)(2,1)S(1)} %convolution_convert_fusion.2), channel_id=1, source_target_pairs={{0,3},{1,2},{2,1},{3,0},{4,7},{5,6},{6,5},{7,4},{8,11},{9,10},{10,... | collective-permute-start | bytes 1179656 | tf_op jit(solution)/shard_map/ppermute | solution.py:457
  64.9 2.8 %attention.6 = (bf16[48,512]{1,0:T(8,128)(2,1)S(1)}, bf16[48,512]{1,0:T(8,128)(2,1)S(1)}) custom-call(s32[3]{0:T(128)S(1)} %pad_add_fusion.1.which, f32[288,1024]{1,0:T(8,128)S(1)} %fusion.refs_0_.kept, bf16[288,512]{1,0:T(8,128)(2,1)S(1)} %collective-permute-done.5.came, f32[384,128]{1,0:T(8,128)S(1)} %get-tuple-element.48.cosines, ...), custom_call_target="tpu_custom_call" | custom-call | tf_op jit(solution)/shard_map/attention/pallas_call | solution.py:217
  68.3 2.8 %attention.5 = (bf16[48,512]{1,0:T(8,128)(2,1)S(1)}, bf16[48,512]{1,0:T(8,128)(2,1)S(1)}) custom-call(s32[3]{0:T(128)S(1)} %pad_add_fusion.1.which, f32[288,1024]{1,0:T(8,128)S(1)} %fusion.refs_0_.kept, bf16[288,512]{1,0:T(8,128)(2,1)S(1)} %collective-permute-done.5.came, f32[384,128]{1,0:T(8,128)S(1)} %get-tuple-element.48.cosines, ...), custom_call_target="tpu_custom_call" | custom-call | tf_op jit(solution)/shard_map/attention/pallas_call | solution.py:217
  71.1 1.6 %collective-permute-start.19 = (bf16[48,512]{1,0:T(8,128)(2,1)S(1)}, bf16[48,512]{1,0:T(8,128)(2,1)S(1)}, u32[]{:S(2)}, u32[]{:S(2)}) collective-permute-start(bf16[48,512]{1,0:T(8,128)(2,1)S(1)} %get-tuple-element.42), channel_id=1, source_target_pairs={{0,4},{4,0},{1,5},{5,1},{2,6},{6,2},{3,7},{7,3},{8,12},{12,8},{9,1... | collective-permute-start | bytes 147464 | tf_op jit(solution)/shard_map/ppermute | solution.py:457
  73.2 1.6 %convolution_convert_fusion = bf16[48,4096]{1,0:T(8,128)(2,1)S(1)} fusion(bf16[48,1024]{1,0:T(8,128)(2,1)S(1)} %join.7, bf16[1024,4096]{1,0:T(8,128)(2,1)S(1)} %bitcast.28), kind=kOutput, calls=%fused_computation | convolution fusion | flops 402849792 | bytes 8880128 | tf_op jit(solution)/shard_map/dot_general | solution.py:273
  74.8 1.9 %collective-permute-start.23 = (bf16[48,4096]{1,0:T(8,128)(2,1)S(1)}, bf16[48,4096]{1,0:T(8,128)(2,1)S(1)}, u32[]{:S(2)}, u32[]{:S(2)}) collective-permute-start(bf16[48,4096]{1,0:T(8,128)(2,1)S(1)} %convolution_convert_fusion), channel_id=1, source_target_pairs={{0,2},{1,3},{2,0},{3,1},{4,6},{5,7},{6,4},{7,5},{8,10},{9,11},{10,... | collective-permute-start | bytes 1179656 | tf_op jit(solution)/shard_map/ppermute | solution.py:457
  77.3 1.6 %convolution_convert_fusion.1 = bf16[48,4096]{1,0:T(8,128)(2,1)S(1)} fusion(bf16[48,1024]{1,0:T(8,128)(2,1)S(1)} %join.6, bf16[1024,4096]{1,0:T(8,128)(2,1)S(1)} %bitcast.28), kind=kOutput, calls=%fused_computation.1 | convolution fusion | flops 402849792 | bytes 8880128 | tf_op jit(solution)/shard_map/dot_general | solution.py:273
  79.8 1.6 %fusion.6 = f32[48,4096]{1,0:T(8,128)S(1)} fusion(bf16[48,1024]{1,0:T(8,128)(2,1)S(1)} %join.5, bf16[1024,4096]{1,0:T(8,128)(2,1)S(1)} %bitcast.28), kind=kOutput, calls=%fused_computation.14 | convolution fusion | flops 402653184 | bytes 9273344 | tf_op jit(solution)/shard_map/dot_general | solution.py:273
  81.4 18.7 %collective-permute-done.23 = bf16[48,4096]{1,0:T(8,128)(2,1)S(1)} collective-permute-done((bf16[48,4096]{1,0:T(8,128)(2,1)S(1)}, bf16[48,4096]{1,0:T(8,128)(2,1)S(1)}, u32[]{:S(2)}, u32[]{:S(2)}) %collective-permute-start.23) | collective-permute-done | bytes 393248 | tf_op jit(solution)/shard_map/ppermute | solution.py:457
  (79 shorter events, 26.0 us)
Async XLA Ops:
  2.1 18.2 %collective-permute-start.4 = (bf16[48,2048]{1,0:T(8,128)(2,1)S(1)}, bf16[48,2048]{1,0:T(8,128)(2,1)S(1)}, u32[]{:S(2)}, u32[]{:S(2)}) collective-permute-start(bf16[48,2048]{1,0:T(8,128)(2,1)S(1)} %get-tuple-element.30), channel_id=1, source_target_pairs={{0,6},{1,7},{2,4},{3,5},{4,2},{5,3},{6,0},{7,1},{8,14},{9,15},{10,... | collective-permute-start | bytes 589832 | tf_op jit(solution)/shard_map/ppermute | solution.py:461
  5.7 17.7 %collective-permute-start.3 = (bf16[48,2048]{1,0:T(8,128)(2,1)S(1)}, bf16[48,2048]{1,0:T(8,128)(2,1)S(1)}, u32[]{:S(2)}, u32[]{:S(2)}) collective-permute-start(bf16[48,2048]{1,0:T(8,128)(2,1)S(1)} %get-tuple-element.29.refs_0_), channel_id=1, source_target_pairs={{0,2},{1,3},{2,0},{3,1},{4,6},{5,7},{6,4},{7,5},{8,10},{9,11},{10,... | collective-permute-start | bytes 589832 | tf_op jit(solution)/shard_map/ppermute | solution.py:457
  6.1 17.4 %collective-permute-start.1 = (bf16[48,2048]{1,0:T(8,128)(2,1)S(1)}, bf16[48,2048]{1,0:T(8,128)(2,1)S(1)}, u32[]{:S(2)}, u32[]{:S(2)}) collective-permute-start(bf16[48,2048]{1,0:T(8,128)(2,1)S(1)} %get-tuple-element.29.refs_0_), channel_id=1, source_target_pairs={{0,1},{1,0},{2,3},{3,2},{4,5},{5,4},{6,7},{7,6},{8,9},{9,8},{10,11... | collective-permute-start | bytes 589832 | tf_op jit(solution)/shard_map/ppermute | solution.py:457
  7.6 16.1 %collective-permute-start.2 = (bf16[48,2048]{1,0:T(8,128)(2,1)S(1)}, bf16[48,2048]{1,0:T(8,128)(2,1)S(1)}, u32[]{:S(2)}, u32[]{:S(2)}) collective-permute-start(bf16[48,2048]{1,0:T(8,128)(2,1)S(1)} %get-tuple-element.30), channel_id=1, source_target_pairs={{0,5},{1,4},{2,7},{3,6},{4,1},{5,0},{6,3},{7,2},{8,13},{9,12},{10,... | collective-permute-start | bytes 589832 | tf_op jit(solution)/shard_map/ppermute | solution.py:461
  8.0 15.7 %collective-permute-start = (bf16[48,2048]{1,0:T(8,128)(2,1)S(1)}, bf16[48,2048]{1,0:T(8,128)(2,1)S(1)}, u32[]{:S(2)}, u32[]{:S(2)}) collective-permute-start(bf16[48,2048]{1,0:T(8,128)(2,1)S(1)} %get-tuple-element.30), channel_id=1, source_target_pairs={{0,4},{4,0},{1,5},{5,1},{2,6},{6,2},{3,7},{7,3},{8,12},{12,8},{9,1... | collective-permute-start | bytes 589832 | tf_op jit(solution)/shard_map/ppermute | solution.py:457
  20.3 11.3 %collective-permute-start.9 = (s32[2,192]{1,0:T(2,128)S(1)}, s32[2,192]{1,0:T(2,128)S(1)}, u32[]{:S(2)}, u32[]{:S(2)}) collective-permute-start(s32[2,192]{1,0:T(2,128)S(1)} %pad_add_fusion.here), channel_id=1, source_target_pairs={{0,4},{4,0},{1,5},{5,1},{2,6},{6,2},{3,7},{7,3},{8,12},{12,8},{9,1... | collective-permute-start | bytes 4616 | tf_op jit(solution)/shard_map/ppermute | solution.py:457
  25.4 9.5 %collective-permute-start.10 = (f32[288,256]{1,0:T(8,128)S(1)}, f32[288,256]{1,0:T(8,128)S(1)}, u32[]{:S(2)}, u32[]{:S(2)}) collective-permute-start(f32[288,256]{1,0:T(8,128)S(1)} %sent.6), channel_id=1, source_target_pairs={{0,4},{4,0},{1,5},{5,1},{2,6},{6,2},{3,7},{7,3},{8,12},{12,8},{9,1... | collective-permute-start | bytes 884744 | tf_op jit(solution)/shard_map/ppermute | solution.py:457
  26.9 10.6 %collective-permute-start.6 = (bf16[96,2048]{1,0:T(8,128)(2,1)S(1)}, bf16[96,2048]{1,0:T(8,128)(2,1)S(1)}, u32[]{:S(2)}, u32[]{:S(2)}) collective-permute-start(bf16[96,2048]{1,0:T(8,128)(2,1)S(1)} %get-tuple-element.32), channel_id=1, source_target_pairs={{1,0},{2,3},{5,4},{6,7},{9,8},{10,11},{13,12},{14,15},{17,16},{18,... | collective-permute-start | bytes 1179656 | tf_op jit(solution)/shard_map/ppermute | solution.py:457
  28.3 9.2 %collective-permute-start.7 = (bf16[96,2048]{1,0:T(8,128)(2,1)S(1)}, bf16[96,2048]{1,0:T(8,128)(2,1)S(1)}, u32[]{:S(2)}, u32[]{:S(2)}) collective-permute-start(bf16[96,2048]{1,0:T(8,128)(2,1)S(1)} %get-tuple-element.33), channel_id=1, source_target_pairs={{1,2},{2,1},{5,6},{6,5},{9,10},{10,9},{13,14},{14,13},{17,18},{18,... | collective-permute-start | bytes 1179656 | tf_op jit(solution)/shard_map/ppermute | solution.py:457
  31.0 22.8 %collective-permute-start.5 = (bf16[288,512]{1,0:T(8,128)(2,1)S(1)}, bf16[288,512]{1,0:T(8,128)(2,1)S(1)}, u32[]{:S(2)}, u32[]{:S(2)}) collective-permute-start(bf16[288,512]{1,0:T(8,128)(2,1)S(1)} %sent.4), channel_id=1, source_target_pairs={{0,4},{4,0},{1,5},{5,1},{2,6},{6,2},{3,7},{7,3},{8,12},{12,8},{9,1... | collective-permute-start | bytes 884744 | tf_op jit(solution)/shard_map/ppermute | solution.py:457
  35.1 10.3 %collective-permute-start.13 = (bf16[304,256]{1,0:T(8,128)(2,1)S(1)}, bf16[304,256]{1,0:T(8,128)(2,1)S(1)}, u32[]{:S(2)}, u32[]{:S(2)}) collective-permute-start(bf16[304,256]{1,0:T(8,128)(2,1)S(1)} %pair.2.refs_0_), channel_id=1, source_target_pairs={{0,24},{8,16},{16,8},{24,0},{1,25},{9,17},{17,9},{25,1},{2,26},{10... | collective-permute-start | bytes 466952 | tf_op jit(solution)/shard_map/ppermute | solution.py:457
  35.2 10.3 %collective-permute-start.12 = (bf16[304,256]{1,0:T(8,128)(2,1)S(1)}, bf16[304,256]{1,0:T(8,128)(2,1)S(1)}, u32[]{:S(2)}, u32[]{:S(2)}) collective-permute-start(bf16[304,256]{1,0:T(8,128)(2,1)S(1)} %pair.2.refs_0_), channel_id=1, source_target_pairs={{0,16},{8,24},{16,0},{24,8},{1,17},{9,25},{17,1},{25,9},{2,18},{10... | collective-permute-start | bytes 466952 | tf_op jit(solution)/shard_map/ppermute | solution.py:457
  37.5 9.1 %collective-permute-start.11 = (bf16[304,256]{1,0:T(8,128)(2,1)S(1)}, bf16[304,256]{1,0:T(8,128)(2,1)S(1)}, u32[]{:S(2)}, u32[]{:S(2)}) collective-permute-start(bf16[304,256]{1,0:T(8,128)(2,1)S(1)} %pair.2.refs_0_), channel_id=1, source_target_pairs={{0,8},{8,0},{16,24},{24,16},{1,9},{9,1},{17,25},{25,17},{2,10},{10... | collective-permute-start | bytes 466952 | tf_op jit(solution)/shard_map/ppermute | solution.py:457
  38.8 5.3 %collective-permute-start.14 = (f32[96,256]{1,0:T(8,128)S(1)}, f32[96,256]{1,0:T(8,128)S(1)}, u32[]{:S(2)}, u32[]{:S(2)}) collective-permute-start(f32[96,256]{1,0:T(8,128)S(1)} %sent.7), channel_id=1, source_target_pairs={{0,4},{4,0},{1,5},{5,1},{2,6},{6,2},{3,7},{7,3},{8,12},{12,8},{9,1... | collective-permute-start | bytes 294920 | tf_op jit(solution)/shard_map/ppermute | solution.py:457
  44.0 4.6 %collective-permute-start.8 = (bf16[96,512]{1,0:T(8,128)(2,1)S(1)}, bf16[96,512]{1,0:T(8,128)(2,1)S(1)}, u32[]{:S(2)}, u32[]{:S(2)}) collective-permute-start(bf16[96,512]{1,0:T(8,128)(2,1)S(1)} %sent.5), channel_id=1, source_target_pairs={{0,4},{4,0},{1,5},{5,1},{2,6},{6,2},{3,7},{7,3},{8,12},{12,8},{9,1... | collective-permute-start | bytes 294920 | tf_op jit(solution)/shard_map/ppermute | solution.py:457
  45.4 3.8 %collective-permute-start.17 = (bf16[96,256]{1,0:T(8,128)(2,1)S(1)}, bf16[96,256]{1,0:T(8,128)(2,1)S(1)}, u32[]{:S(2)}, u32[]{:S(2)}) collective-permute-start(bf16[96,256]{1,0:T(8,128)(2,1)S(1)} %pair.3.refs_4_), channel_id=1, source_target_pairs={{0,24},{8,16},{16,8},{24,0},{1,25},{9,17},{17,9},{25,1},{2,26},{10... | collective-permute-start | bytes 147464 | tf_op jit(solution)/shard_map/ppermute | solution.py:457
  45.5 4.6 %collective-permute-start.16 = (bf16[96,256]{1,0:T(8,128)(2,1)S(1)}, bf16[96,256]{1,0:T(8,128)(2,1)S(1)}, u32[]{:S(2)}, u32[]{:S(2)}) collective-permute-start(bf16[96,256]{1,0:T(8,128)(2,1)S(1)} %pair.3.refs_4_), channel_id=1, source_target_pairs={{0,16},{8,24},{16,0},{24,8},{1,17},{9,25},{17,1},{25,9},{2,18},{10... | collective-permute-start | bytes 147464 | tf_op jit(solution)/shard_map/ppermute | solution.py:457
  52.9 5.0 %collective-permute-start.18 = (bf16[48,512]{1,0:T(8,128)(2,1)S(1)}, bf16[48,512]{1,0:T(8,128)(2,1)S(1)}, u32[]{:S(2)}, u32[]{:S(2)}) collective-permute-start(bf16[48,512]{1,0:T(8,128)(2,1)S(1)} %get-tuple-element.39), channel_id=1, source_target_pairs={{0,4},{4,0},{1,5},{5,1},{2,6},{6,2},{3,7},{7,3},{8,12},{12,8},{9,1... | collective-permute-start | bytes 147464 | tf_op jit(solution)/shard_map/ppermute | solution.py:457
  56.6 16.1 %collective-permute-start.22 = (bf16[48,512]{1,0:T(8,128)(2,1)S(1)}, bf16[48,512]{1,0:T(8,128)(2,1)S(1)}, u32[]{:S(2)}, u32[]{:S(2)}) collective-permute-start(bf16[48,512]{1,0:T(8,128)(2,1)S(1)} %get-tuple-element.46), channel_id=1, source_target_pairs={{0,4},{4,0},{1,5},{5,1},{2,6},{6,2},{3,7},{7,3},{8,12},{12,8},{9,1... | collective-permute-start | bytes 147464 | tf_op jit(solution)/shard_map/ppermute | solution.py:457
  60.3 39.8 %collective-permute-start.24 = (bf16[48,4096]{1,0:T(8,128)(2,1)S(1)}, bf16[48,4096]{1,0:T(8,128)(2,1)S(1)}, u32[]{:S(2)}, u32[]{:S(2)}) collective-permute-start(bf16[48,4096]{1,0:T(8,128)(2,1)S(1)} %convolution_convert_fusion.2), channel_id=1, source_target_pairs={{0,3},{1,2},{2,1},{3,0},{4,7},{5,6},{6,5},{7,4},{8,11},{9,10},{10,... | collective-permute-start | bytes 1179656 | tf_op jit(solution)/shard_map/ppermute | solution.py:457
  67.7 9.1 %collective-permute-start.20 = (bf16[48,512]{1,0:T(8,128)(2,1)S(1)}, bf16[48,512]{1,0:T(8,128)(2,1)S(1)}, u32[]{:S(2)}, u32[]{:S(2)}) collective-permute-start(bf16[48,512]{1,0:T(8,128)(2,1)S(1)} %get-tuple-element.44), channel_id=1, source_target_pairs={{0,4},{4,0},{1,5},{5,1},{2,6},{6,2},{3,7},{7,3},{8,12},{12,8},{9,1... | collective-permute-start | bytes 147464 | tf_op jit(solution)/shard_map/ppermute | solution.py:457
  71.1 8.2 %collective-permute-start.19 = (bf16[48,512]{1,0:T(8,128)(2,1)S(1)}, bf16[48,512]{1,0:T(8,128)(2,1)S(1)}, u32[]{:S(2)}, u32[]{:S(2)}) collective-permute-start(bf16[48,512]{1,0:T(8,128)(2,1)S(1)} %get-tuple-element.42), channel_id=1, source_target_pairs={{0,4},{4,0},{1,5},{5,1},{2,6},{6,2},{3,7},{7,3},{8,12},{12,8},{9,1... | collective-permute-start | bytes 147464 | tf_op jit(solution)/shard_map/ppermute | solution.py:457
  74.8 25.3 %collective-permute-start.23 = (bf16[48,4096]{1,0:T(8,128)(2,1)S(1)}, bf16[48,4096]{1,0:T(8,128)(2,1)S(1)}, u32[]{:S(2)}, u32[]{:S(2)}) collective-permute-start(bf16[48,4096]{1,0:T(8,128)(2,1)S(1)} %convolution_convert_fusion), channel_id=1, source_target_pairs={{0,2},{1,3},{2,0},{3,1},{4,6},{5,7},{6,4},{7,5},{8,10},{9,11},{10,... | collective-permute-start | bytes 1179656 | tf_op jit(solution)/shard_map/ppermute | solution.py:457
  78.9 21.2 %collective-permute-start.21 = (bf16[48,4096]{1,0:T(8,128)(2,1)S(1)}, bf16[48,4096]{1,0:T(8,128)(2,1)S(1)}, u32[]{:S(2)}, u32[]{:S(2)}) collective-permute-start(bf16[48,4096]{1,0:T(8,128)(2,1)S(1)} %convolution_convert_fusion.1), channel_id=1, source_target_pairs={{0,1},{1,0},{2,3},{3,2},{4,5},{5,4},{6,7},{7,6},{8,9},{9,8},{10,11... | collective-permute-start | bytes 1179656 | tf_op jit(solution)/shard_map/ppermute | solution.py:457
  (11 other events, 125.8 us)

commit v5 on v4

--- a/solution.py
+++ b/solution.py
@@ -521,6 +521,15 @@
             found.append(send(pair, "outer", swap_pairs(outer_count, flip)))
         return found
 
+    def gather_by_steps(pair):
+        found = {0: pair}
+        bit = outer_count // 2
+        while bit:
+            for flip in list(found):
+                found[flip | bit] = send(found[flip], "outer", swap_pairs(outer_count, bit))
+            bit //= 2
+        return [found[flip] for flip in range(outer_count)]
+
     def rotate_pair(projected, first, extra):
         keys, values, came = projected
         count = came.shape[0]
@@ -542,7 +551,7 @@
     late_stacked = stack("late_rows", [[ends_rows, middle_rows]], (1,))[0]
     late_projected = project_pair(late_stacked)
     late_queries, late_came = project_query(late_stacked)
-    early_pairs = gather_pairs(rotate_pair(early_projected, 0, [document_rows]))
+    early_pairs = gather_by_steps(rotate_pair(early_projected, 0, [document_rows]))
     late_pairs = gather_pairs(rotate_pair(late_projected, early_rows, []))
 
     def attend(slot, *wait):

time: 102 us -> 100 us (0.980)
  starting transfers between devices: 29.2 us -> 28.1 us
    ppermute x23, starting transfers between devices: 25.2 us -> 24.1 us  [send(): return lax.ppermute(value, axis, pairs)]
  transfers between devices with their start and end apart: 25 -> 25, of which waited for: 10 -> 11; matrix products, arithmetic and copies ran while one was open for 11% -> 12% of each run, Pallas kernels for 17% -> 17%
where the time goes in v5:
time: 100 us; the launch traced here: 99.4 us
  waiting for transfers between devices  39.2 us (39%)
  starting transfers between devices  28.1 us (28%)
  Pallas kernels  17.4 us (17%)
  matrix products  10.1 us (10%)
  other arithmetic  2.46 us (2%)
  local copies, waits for them, and re-layouts  1.83 us (2%)
    ppermute x23, waiting for transfers between devices, send(): return lax.ppermute(value, axis, pairs)  28.8 us
    ppermute x23, starting transfers between devices, send(): return lax.ppermute(value, axis, pairs)  24.1 us
    pallas_call x18, Pallas kernels, call_kernel(): pl.pallas_call(kernel, name=name, grid_spec=pltpu.PrefetchScalarGridSpec(...  17.4 us
    ppermute x2, waiting for transfers between devices, send_across(): return lax.ppermute(value, ('inner', 'tensor'), both)  10.3 us
    dot_general x10, matrix products, product(): return jnp.dot(left, right, preferred_element_type=jnp.float32)  10.1 us
    ppermute x2, starting transfers between devices, send_across(): return lax.ppermute(value, ('inner', 'tensor'), both)  4 us
  transfers between devices with their start and end apart: 25, of which 11 were waited for; matrix products, arithmetic and copies ran while one was open for 12% of the time, Pallas kernels for 17%

profile of v5, /device:TPU:2, one launch (start us, length us, event | category | flops | bytes accessed | tf_op | source)
XLA Modules:
  0.0 99.4 jit_solution(13575300411247484237)
XLA Ops:
  2.1 3.6 %collective-permute-start.4 = (bf16[48,2048]{1,0:T(8,128)(2,1)S(1)}, bf16[48,2048]{1,0:T(8,128)(2,1)S(1)}, u32[]{:S(2)}, u32[]{:S(2)}) collective-permute-start(bf16[48,2048]{1,0:T(8,128)(2,1)S(1)} %get-tuple-element.30), channel_id=1, source_target_pairs={{0,6},{1,7},{2,4},{3,5},{4,2},{5,3},{6,0},{7,1},{8,14},{9,15},{10,... | collective-permute-start | bytes 589832 | tf_op jit(solution)/shard_map/ppermute | solution.py:461
  6.1 1.6 %collective-permute-start.1 = (bf16[48,2048]{1,0:T(8,128)(2,1)S(1)}, bf16[48,2048]{1,0:T(8,128)(2,1)S(1)}, u32[]{:S(2)}, u32[]{:S(2)}) collective-permute-start(bf16[48,2048]{1,0:T(8,128)(2,1)S(1)} %get-tuple-element.29.refs_0_), channel_id=1, source_target_pairs={{0,1},{1,0},{2,3},{3,2},{4,5},{5,4},{6,7},{7,6},{8,9},{9,8},{10,11... | collective-permute-start | bytes 589832 | tf_op jit(solution)/shard_map/ppermute | solution.py:457
  8.0 1.5 %collective-permute-start = (bf16[48,2048]{1,0:T(8,128)(2,1)S(1)}, bf16[48,2048]{1,0:T(8,128)(2,1)S(1)}, u32[]{:S(2)}, u32[]{:S(2)}) collective-permute-start(bf16[48,2048]{1,0:T(8,128)(2,1)S(1)} %get-tuple-element.30), channel_id=1, source_target_pairs={{0,4},{4,0},{1,5},{5,1},{2,6},{6,2},{3,7},{7,3},{8,12},{12,8},{9,1... | collective-permute-start | bytes 589832 | tf_op jit(solution)/shard_map/ppermute | solution.py:457
  10.2 10.0 %collective-permute-done.4.refs_5_ = bf16[48,2048]{1,0:T(8,128)(2,1)S(1)} collective-permute-done((bf16[48,2048]{1,0:T(8,128)(2,1)S(1)}, bf16[48,2048]{1,0:T(8,128)(2,1)S(1)}, u32[]{:S(2)}, u32[]{:S(2)}) %collective-permute-start.4) | collective-permute-done | bytes 196640 | tf_op jit(solution)/shard_map/ppermute | solution.py:461
  20.3 1.5 %collective-permute-start.9 = (s32[2,192]{1,0:T(2,128)S(1)}, s32[2,192]{1,0:T(2,128)S(1)}, u32[]{:S(2)}, u32[]{:S(2)}) collective-permute-start(s32[2,192]{1,0:T(2,128)S(1)} %pad_add_fusion.here), channel_id=1, source_target_pairs={{0,4},{4,0},{1,5},{5,1},{2,6},{6,2},{3,7},{7,3},{8,12},{12,8},{9,1... | collective-permute-start | bytes 4616 | tf_op jit(solution)/shard_map/ppermute | solution.py:457
  21.8 1.6 %collective-permute-done.3.refs_4_ = bf16[48,2048]{1,0:T(8,128)(2,1)S(1)} collective-permute-done((bf16[48,2048]{1,0:T(8,128)(2,1)S(1)}, bf16[48,2048]{1,0:T(8,128)(2,1)S(1)}, u32[]{:S(2)}, u32[]{:S(2)}) %collective-permute-start.3) | collective-permute-done | bytes 196640 | tf_op jit(solution)/shard_map/ppermute | solution.py:457
  25.4 1.5 %collective-permute-start.10 = (f32[288,256]{1,0:T(8,128)S(1)}, f32[288,256]{1,0:T(8,128)S(1)}, u32[]{:S(2)}, u32[]{:S(2)}) collective-permute-start(f32[288,256]{1,0:T(8,128)S(1)} %sent.6), channel_id=1, source_target_pairs={{0,4},{4,0},{1,5},{5,1},{2,6},{6,2},{3,7},{7,3},{8,12},{12,8},{9,1... | collective-permute-start | bytes 884744 | tf_op jit(solution)/shard_map/ppermute | solution.py:457
  29.0 1.4 %fusion.refs_0_.kept = f32[288,1024]{1,0:T(8,128)S(1)} fusion(bf16[288,2048]{1,0:T(8,128)(2,1)S(1)} %get-tuple-element.31, bf16[2048,1024]{1,0:T(8,128)(2,1)S(1)} %copy-done.5), kind=kOutput, calls=%fused_computation.8 | convolution fusion | flops 1207959552 | bytes 6553600 | tf_op jit(solution)/shard_map/dot_general | solution.py:273
  33.2 1.8 %collective-permute-done.10.came = f32[288,256]{1,0:T(8,128)S(1)} collective-permute-done((f32[288,256]{1,0:T(8,128)S(1)}, f32[288,256]{1,0:T(8,128)S(1)}, u32[]{:S(2)}, u32[]{:S(2)}) %collective-permute-start.10) | collective-permute-done | bytes 294944 | tf_op jit(solution)/shard_map/ppermute | solution.py:457
  35.4 2.1 %collective-permute-done.6.refs_0_ = bf16[96,2048]{1,0:T(8,128)(2,1)S(1)} collective-permute-done((bf16[96,2048]{1,0:T(8,128)(2,1)S(1)}, bf16[96,2048]{1,0:T(8,128)(2,1)S(1)}, u32[]{:S(2)}, u32[]{:S(2)}) %collective-permute-start.6) | collective-permute-done | bytes 393248 | tf_op jit(solution)/shard_map/ppermute | solution.py:457
  38.8 1.3 %collective-permute-start.14 = (f32[96,256]{1,0:T(8,128)S(1)}, f32[96,256]{1,0:T(8,128)S(1)}, u32[]{:S(2)}, u32[]{:S(2)}) collective-permute-start(f32[96,256]{1,0:T(8,128)S(1)} %sent.7), channel_id=1, source_target_pairs={{0,4},{4,0},{1,5},{5,1},{2,6},{6,2},{3,7},{7,3},{8,12},{12,8},{9,1... | collective-permute-start | bytes 294920 | tf_op jit(solution)/shard_map/ppermute | solution.py:457
  44.3 2.7 %collective-permute-done.8.came = bf16[96,512]{1,0:T(8,128)(2,1)S(1)} collective-permute-done((bf16[96,512]{1,0:T(8,128)(2,1)S(1)}, bf16[96,512]{1,0:T(8,128)(2,1)S(1)}, u32[]{:S(2)}, u32[]{:S(2)}) %collective-permute-start.8) | collective-permute-done | bytes 98336 | tf_op jit(solution)/shard_map/ppermute | solution.py:457
  48.3 2.8 %attention.4 = (bf16[48,512]{1,0:T(8,128)(2,1)S(1)}, bf16[48,512]{1,0:T(8,128)(2,1)S(1)}) custom-call(s32[3]{0:T(128)S(1)} %pad_add_fusion.1.which, f32[96,1024]{1,0:T(8,128)S(1)} %fusion.1.refs_0_.kept, bf16[96,512]{1,0:T(8,128)(2,1)S(1)} %collective-permute-done.8.came, f32[384,128]{1,0:T(8,128)S(1)} %get-tuple-element.48.cosines, ...), custom_call_target="tpu_custom_call" | custom-call | tf_op jit(solution)/shard_map/attention/pallas_call | solution.py:217
  52.4 2.8 %attention.7 = (bf16[48,512]{1,0:T(8,128)(2,1)S(1)}, bf16[48,512]{1,0:T(8,128)(2,1)S(1)}) custom-call(s32[3]{0:T(128)S(1)} %pad_add_fusion.1.which, f32[288,1024]{1,0:T(8,128)S(1)} %fusion.refs_0_.kept, bf16[288,512]{1,0:T(8,128)(2,1)S(1)} %collective-permute-done.5.came, f32[384,128]{1,0:T(8,128)S(1)} %get-tuple-element.48.cosines, ...), custom_call_target="tpu_custom_call" | custom-call | tf_op jit(solution)/shard_map/attention/pallas_call | solution.py:217
  56.9 1.6 %convolution_convert_fusion.2 = bf16[48,4096]{1,0:T(8,128)(2,1)S(1)} fusion(bf16[48,1024]{1,0:T(8,128)(2,1)S(1)} %join.4, bf16[1024,4096]{1,0:T(8,128)(2,1)S(1)} %bitcast.28), kind=kOutput, calls=%fused_computation.2 | convolution fusion | flops 402849792 | bytes 8880128 | tf_op jit(solution)/shard_map/dot_general | solution.py:273
  58.4 4.6 %collective-permute-start.24 = (bf16[48,4096]{1,0:T(8,128)(2,1)S(1)}, bf16[48,4096]{1,0:T(8,128)(2,1)S(1)}, u32[]{:S(2)}, u32[]{:S(2)}) collective-permute-start(bf16[48,4096]{1,0:T(8,128)(2,1)S(1)} %convolution_convert_fusion.2), channel_id=1, source_target_pairs={{0,3},{1,2},{2,1},{3,0},{4,7},{5,6},{6,5},{7,4},{8,11},{9,10},{10,... | collective-permute-start | bytes 1179656 | tf_op jit(solution)/shard_map/ppermute | solution.py:457
  63.0 2.8 %attention.6 = (bf16[48,512]{1,0:T(8,128)(2,1)S(1)}, bf16[48,512]{1,0:T(8,128)(2,1)S(1)}) custom-call(s32[3]{0:T(128)S(1)} %pad_add_fusion.1.which, f32[288,1024]{1,0:T(8,128)S(1)} %fusion.refs_0_.kept, bf16[288,512]{1,0:T(8,128)(2,1)S(1)} %collective-permute-done.5.came, f32[384,128]{1,0:T(8,128)S(1)} %get-tuple-element.48.cosines, ...), custom_call_target="tpu_custom_call" | custom-call | tf_op jit(solution)/shard_map/attention/pallas_call | solution.py:217
  65.8 1.3 %collective-permute-start.20 = (bf16[48,512]{1,0:T(8,128)(2,1)S(1)}, bf16[48,512]{1,0:T(8,128)(2,1)S(1)}, u32[]{:S(2)}, u32[]{:S(2)}) collective-permute-start(bf16[48,512]{1,0:T(8,128)(2,1)S(1)} %get-tuple-element.44), channel_id=1, source_target_pairs={{0,4},{4,0},{1,5},{5,1},{2,6},{6,2},{3,7},{7,3},{8,12},{12,8},{9,1... | collective-permute-start | bytes 147464 | tf_op jit(solution)/shard_map/ppermute | solution.py:457
  67.2 2.8 %attention.5 = (bf16[48,512]{1,0:T(8,128)(2,1)S(1)}, bf16[48,512]{1,0:T(8,128)(2,1)S(1)}) custom-call(s32[3]{0:T(128)S(1)} %pad_add_fusion.1.which, f32[288,1024]{1,0:T(8,128)S(1)} %fusion.refs_0_.kept, bf16[288,512]{1,0:T(8,128)(2,1)S(1)} %collective-permute-done.5.came, f32[384,128]{1,0:T(8,128)S(1)} %get-tuple-element.48.cosines, ...), custom_call_target="tpu_custom_call" | custom-call | tf_op jit(solution)/shard_map/attention/pallas_call | solution.py:217
  71.4 1.6 %convolution_convert_fusion = bf16[48,4096]{1,0:T(8,128)(2,1)S(1)} fusion(bf16[48,1024]{1,0:T(8,128)(2,1)S(1)} %join.7, bf16[1024,4096]{1,0:T(8,128)(2,1)S(1)} %bitcast.28), kind=kOutput, calls=%fused_computation | convolution fusion | flops 402849792 | bytes 8880128 | tf_op jit(solution)/shard_map/dot_general | solution.py:273
  73.0 3.1 %collective-permute-start.23 = (bf16[48,4096]{1,0:T(8,128)(2,1)S(1)}, bf16[48,4096]{1,0:T(8,128)(2,1)S(1)}, u32[]{:S(2)}, u32[]{:S(2)}) collective-permute-start(bf16[48,4096]{1,0:T(8,128)(2,1)S(1)} %convolution_convert_fusion), channel_id=1, source_target_pairs={{0,2},{1,3},{2,0},{3,1},{4,6},{5,7},{6,4},{7,5},{8,10},{9,11},{10,... | collective-permute-start | bytes 1179656 | tf_op jit(solution)/shard_map/ppermute | solution.py:457
  76.6 1.6 %convolution_convert_fusion.1 = bf16[48,4096]{1,0:T(8,128)(2,1)S(1)} fusion(bf16[48,1024]{1,0:T(8,128)(2,1)S(1)} %join.6, bf16[1024,4096]{1,0:T(8,128)(2,1)S(1)} %bitcast.28), kind=kOutput, calls=%fused_computation.1 | convolution fusion | flops 402849792 | bytes 8880128 | tf_op jit(solution)/shard_map/dot_general | solution.py:273
  78.9 1.6 %fusion.6 = f32[48,4096]{1,0:T(8,128)S(1)} fusion(bf16[48,1024]{1,0:T(8,128)(2,1)S(1)} %join.5, bf16[1024,4096]{1,0:T(8,128)(2,1)S(1)} %bitcast.28), kind=kOutput, calls=%fused_computation.14 | convolution fusion | flops 402653184 | bytes 9273344 | tf_op jit(solution)/shard_map/dot_general | solution.py:273
  80.5 17.9 %collective-permute-done.23 = bf16[48,4096]{1,0:T(8,128)(2,1)S(1)} collective-permute-done((bf16[48,4096]{1,0:T(8,128)(2,1)S(1)}, bf16[48,4096]{1,0:T(8,128)(2,1)S(1)}, u32[]{:S(2)}, u32[]{:S(2)}) %collective-permute-start.23) | collective-permute-done | bytes 393248 | tf_op jit(solution)/shard_map/ppermute | solution.py:457
  (79 shorter events, 23.9 us)
Async XLA Ops:
  2.1 18.2 %collective-permute-start.4 = (bf16[48,2048]{1,0:T(8,128)(2,1)S(1)}, bf16[48,2048]{1,0:T(8,128)(2,1)S(1)}, u32[]{:S(2)}, u32[]{:S(2)}) collective-permute-start(bf16[48,2048]{1,0:T(8,128)(2,1)S(1)} %get-tuple-element.30), channel_id=1, source_target_pairs={{0,6},{1,7},{2,4},{3,5},{4,2},{5,3},{6,0},{7,1},{8,14},{9,15},{10,... | collective-permute-start | bytes 589832 | tf_op jit(solution)/shard_map/ppermute | solution.py:461
  5.7 17.7 %collective-permute-start.3 = (bf16[48,2048]{1,0:T(8,128)(2,1)S(1)}, bf16[48,2048]{1,0:T(8,128)(2,1)S(1)}, u32[]{:S(2)}, u32[]{:S(2)}) collective-permute-start(bf16[48,2048]{1,0:T(8,128)(2,1)S(1)} %get-tuple-element.29.refs_0_), channel_id=1, source_target_pairs={{0,2},{1,3},{2,0},{3,1},{4,6},{5,7},{6,4},{7,5},{8,10},{9,11},{10,... | collective-permute-start | bytes 589832 | tf_op jit(solution)/shard_map/ppermute | solution.py:457
  6.1 17.4 %collective-permute-start.1 = (bf16[48,2048]{1,0:T(8,128)(2,1)S(1)}, bf16[48,2048]{1,0:T(8,128)(2,1)S(1)}, u32[]{:S(2)}, u32[]{:S(2)}) collective-permute-start(bf16[48,2048]{1,0:T(8,128)(2,1)S(1)} %get-tuple-element.29.refs_0_), channel_id=1, source_target_pairs={{0,1},{1,0},{2,3},{3,2},{4,5},{5,4},{6,7},{7,6},{8,9},{9,8},{10,11... | collective-permute-start | bytes 589832 | tf_op jit(solution)/shard_map/ppermute | solution.py:457
  7.6 16.1 %collective-permute-start.2 = (bf16[48,2048]{1,0:T(8,128)(2,1)S(1)}, bf16[48,2048]{1,0:T(8,128)(2,1)S(1)}, u32[]{:S(2)}, u32[]{:S(2)}) collective-permute-start(bf16[48,2048]{1,0:T(8,128)(2,1)S(1)} %get-tuple-element.30), channel_id=1, source_target_pairs={{0,5},{1,4},{2,7},{3,6},{4,1},{5,0},{6,3},{7,2},{8,13},{9,12},{10,... | collective-permute-start | bytes 589832 | tf_op jit(solution)/shard_map/ppermute | solution.py:461
  8.0 15.7 %collective-permute-start = (bf16[48,2048]{1,0:T(8,128)(2,1)S(1)}, bf16[48,2048]{1,0:T(8,128)(2,1)S(1)}, u32[]{:S(2)}, u32[]{:S(2)}) collective-permute-start(bf16[48,2048]{1,0:T(8,128)(2,1)S(1)} %get-tuple-element.30), channel_id=1, source_target_pairs={{0,4},{4,0},{1,5},{5,1},{2,6},{6,2},{3,7},{7,3},{8,12},{12,8},{9,1... | collective-permute-start | bytes 589832 | tf_op jit(solution)/shard_map/ppermute | solution.py:457
  20.3 11.3 %collective-permute-start.9 = (s32[2,192]{1,0:T(2,128)S(1)}, s32[2,192]{1,0:T(2,128)S(1)}, u32[]{:S(2)}, u32[]{:S(2)}) collective-permute-start(s32[2,192]{1,0:T(2,128)S(1)} %pad_add_fusion.here), channel_id=1, source_target_pairs={{0,4},{4,0},{1,5},{5,1},{2,6},{6,2},{3,7},{7,3},{8,12},{12,8},{9,1... | collective-permute-start | bytes 4616 | tf_op jit(solution)/shard_map/ppermute | solution.py:457
  25.4 9.5 %collective-permute-start.10 = (f32[288,256]{1,0:T(8,128)S(1)}, f32[288,256]{1,0:T(8,128)S(1)}, u32[]{:S(2)}, u32[]{:S(2)}) collective-permute-start(f32[288,256]{1,0:T(8,128)S(1)} %sent.6), channel_id=1, source_target_pairs={{0,4},{4,0},{1,5},{5,1},{2,6},{6,2},{3,7},{7,3},{8,12},{12,8},{9,1... | collective-permute-start | bytes 884744 | tf_op jit(solution)/shard_map/ppermute | solution.py:457
  26.9 10.6 %collective-permute-start.6 = (bf16[96,2048]{1,0:T(8,128)(2,1)S(1)}, bf16[96,2048]{1,0:T(8,128)(2,1)S(1)}, u32[]{:S(2)}, u32[]{:S(2)}) collective-permute-start(bf16[96,2048]{1,0:T(8,128)(2,1)S(1)} %get-tuple-element.32), channel_id=1, source_target_pairs={{1,0},{2,3},{5,4},{6,7},{9,8},{10,11},{13,12},{14,15},{17,16},{18,... | collective-permute-start | bytes 1179656 | tf_op jit(solution)/shard_map/ppermute | solution.py:457
  28.3 9.2 %collective-permute-start.7 = (bf16[96,2048]{1,0:T(8,128)(2,1)S(1)}, bf16[96,2048]{1,0:T(8,128)(2,1)S(1)}, u32[]{:S(2)}, u32[]{:S(2)}) collective-permute-start(bf16[96,2048]{1,0:T(8,128)(2,1)S(1)} %get-tuple-element.33), channel_id=1, source_target_pairs={{1,2},{2,1},{5,6},{6,5},{9,10},{10,9},{13,14},{14,13},{17,18},{18,... | collective-permute-start | bytes 1179656 | tf_op jit(solution)/shard_map/ppermute | solution.py:457
  31.0 21.4 %collective-permute-start.5 = (bf16[288,512]{1,0:T(8,128)(2,1)S(1)}, bf16[288,512]{1,0:T(8,128)(2,1)S(1)}, u32[]{:S(2)}, u32[]{:S(2)}) collective-permute-start(bf16[288,512]{1,0:T(8,128)(2,1)S(1)} %sent.4), channel_id=1, source_target_pairs={{0,4},{4,0},{1,5},{5,1},{2,6},{6,2},{3,7},{7,3},{8,12},{12,8},{9,1... | collective-permute-start | bytes 884744 | tf_op jit(solution)/shard_map/ppermute | solution.py:457
  35.1 5.3 %collective-permute-start.12 = (bf16[304,256]{1,0:T(8,128)(2,1)S(1)}, bf16[304,256]{1,0:T(8,128)(2,1)S(1)}, u32[]{:S(2)}, u32[]{:S(2)}) collective-permute-start(bf16[304,256]{1,0:T(8,128)(2,1)S(1)} %pair.2.refs_0_), channel_id=1, source_target_pairs={{0,16},{8,24},{16,0},{24,8},{1,17},{9,25},{17,1},{25,9},{2,18},{10... | collective-permute-start | bytes 466952 | tf_op jit(solution)/shard_map/ppermute | solution.py:457
  35.4 8.2 %collective-permute-start.11 = (bf16[304,256]{1,0:T(8,128)(2,1)S(1)}, bf16[304,256]{1,0:T(8,128)(2,1)S(1)}, u32[]{:S(2)}, u32[]{:S(2)}) collective-permute-start(bf16[304,256]{1,0:T(8,128)(2,1)S(1)} %pair.2.refs_0_), channel_id=1, source_target_pairs={{0,8},{8,0},{16,24},{24,16},{1,9},{9,1},{17,25},{25,17},{2,10},{10... | collective-permute-start | bytes 466952 | tf_op jit(solution)/shard_map/ppermute | solution.py:457
  38.8 4.7 %collective-permute-start.14 = (f32[96,256]{1,0:T(8,128)S(1)}, f32[96,256]{1,0:T(8,128)S(1)}, u32[]{:S(2)}, u32[]{:S(2)}) collective-permute-start(f32[96,256]{1,0:T(8,128)S(1)} %sent.7), channel_id=1, source_target_pairs={{0,4},{4,0},{1,5},{5,1},{2,6},{6,2},{3,7},{7,3},{8,12},{12,8},{9,1... | collective-permute-start | bytes 294920 | tf_op jit(solution)/shard_map/ppermute | solution.py:457
  40.4 7.9 %collective-permute-start.13 = (bf16[304,256]{1,0:T(8,128)(2,1)S(1)}, bf16[304,256]{1,0:T(8,128)(2,1)S(1)}, u32[]{:S(2)}, u32[]{:S(2)}) collective-permute-start(bf16[304,256]{1,0:T(8,128)(2,1)S(1)} %collective-permute-done.12.refs_2_), channel_id=1, source_target_pairs={{0,8},{8,0},{16,24},{24,16},{1,9},{9,1},{17,25},{25,17},{2,10},{10... | collective-permute-start | bytes 466952 | tf_op jit(solution)/shard_map/ppermute | solution.py:457
  41.8 5.3 %collective-permute-start.8 = (bf16[96,512]{1,0:T(8,128)(2,1)S(1)}, bf16[96,512]{1,0:T(8,128)(2,1)S(1)}, u32[]{:S(2)}, u32[]{:S(2)}) collective-permute-start(bf16[96,512]{1,0:T(8,128)(2,1)S(1)} %sent.5), channel_id=1, source_target_pairs={{0,4},{4,0},{1,5},{5,1},{2,6},{6,2},{3,7},{7,3},{8,12},{12,8},{9,1... | collective-permute-start | bytes 294920 | tf_op jit(solution)/shard_map/ppermute | solution.py:457
  43.5 3.6 %collective-permute-start.17 = (bf16[96,256]{1,0:T(8,128)(2,1)S(1)}, bf16[96,256]{1,0:T(8,128)(2,1)S(1)}, u32[]{:S(2)}, u32[]{:S(2)}) collective-permute-start(bf16[96,256]{1,0:T(8,128)(2,1)S(1)} %pair.3.refs_4_), channel_id=1, source_target_pairs={{0,24},{8,16},{16,8},{24,0},{1,25},{9,17},{17,9},{25,1},{2,26},{10... | collective-permute-start | bytes 147464 | tf_op jit(solution)/shard_map/ppermute | solution.py:457
  43.6 4.5 %collective-permute-start.16 = (bf16[96,256]{1,0:T(8,128)(2,1)S(1)}, bf16[96,256]{1,0:T(8,128)(2,1)S(1)}, u32[]{:S(2)}, u32[]{:S(2)}) collective-permute-start(bf16[96,256]{1,0:T(8,128)(2,1)S(1)} %pair.3.refs_4_), channel_id=1, source_target_pairs={{0,16},{8,24},{16,0},{24,8},{1,17},{9,25},{17,1},{25,9},{2,18},{10... | collective-permute-start | bytes 147464 | tf_op jit(solution)/shard_map/ppermute | solution.py:457
  51.1 5.0 %collective-permute-start.18 = (bf16[48,512]{1,0:T(8,128)(2,1)S(1)}, bf16[48,512]{1,0:T(8,128)(2,1)S(1)}, u32[]{:S(2)}, u32[]{:S(2)}) collective-permute-start(bf16[48,512]{1,0:T(8,128)(2,1)S(1)} %get-tuple-element.39), channel_id=1, source_target_pairs={{0,4},{4,0},{1,5},{5,1},{2,6},{6,2},{3,7},{7,3},{8,12},{12,8},{9,1... | collective-permute-start | bytes 147464 | tf_op jit(solution)/shard_map/ppermute | solution.py:457
  55.2 15.6 %collective-permute-start.22 = (bf16[48,512]{1,0:T(8,128)(2,1)S(1)}, bf16[48,512]{1,0:T(8,128)(2,1)S(1)}, u32[]{:S(2)}, u32[]{:S(2)}) collective-permute-start(bf16[48,512]{1,0:T(8,128)(2,1)S(1)} %get-tuple-element.46), channel_id=1, source_target_pairs={{0,4},{4,0},{1,5},{5,1},{2,6},{6,2},{3,7},{7,3},{8,12},{12,8},{9,1... | collective-permute-start | bytes 147464 | tf_op jit(solution)/shard_map/ppermute | solution.py:457
  58.4 39.9 %collective-permute-start.24 = (bf16[48,4096]{1,0:T(8,128)(2,1)S(1)}, bf16[48,4096]{1,0:T(8,128)(2,1)S(1)}, u32[]{:S(2)}, u32[]{:S(2)}) collective-permute-start(bf16[48,4096]{1,0:T(8,128)(2,1)S(1)} %convolution_convert_fusion.2), channel_id=1, source_target_pairs={{0,3},{1,2},{2,1},{3,0},{4,7},{5,6},{6,5},{7,4},{8,11},{9,10},{10,... | collective-permute-start | bytes 1179656 | tf_op jit(solution)/shard_map/ppermute | solution.py:457
  65.8 10.2 %collective-permute-start.20 = (bf16[48,512]{1,0:T(8,128)(2,1)S(1)}, bf16[48,512]{1,0:T(8,128)(2,1)S(1)}, u32[]{:S(2)}, u32[]{:S(2)}) collective-permute-start(bf16[48,512]{1,0:T(8,128)(2,1)S(1)} %get-tuple-element.44), channel_id=1, source_target_pairs={{0,4},{4,0},{1,5},{5,1},{2,6},{6,2},{3,7},{7,3},{8,12},{12,8},{9,1... | collective-permute-start | bytes 147464 | tf_op jit(solution)/shard_map/ppermute | solution.py:457
  70.0 8.3 %collective-permute-start.19 = (bf16[48,512]{1,0:T(8,128)(2,1)S(1)}, bf16[48,512]{1,0:T(8,128)(2,1)S(1)}, u32[]{:S(2)}, u32[]{:S(2)}) collective-permute-start(bf16[48,512]{1,0:T(8,128)(2,1)S(1)} %get-tuple-element.42), channel_id=1, source_target_pairs={{0,4},{4,0},{1,5},{5,1},{2,6},{6,2},{3,7},{7,3},{8,12},{12,8},{9,1... | collective-permute-start | bytes 147464 | tf_op jit(solution)/shard_map/ppermute | solution.py:457
  73.0 25.4 %collective-permute-start.23 = (bf16[48,4096]{1,0:T(8,128)(2,1)S(1)}, bf16[48,4096]{1,0:T(8,128)(2,1)S(1)}, u32[]{:S(2)}, u32[]{:S(2)}) collective-permute-start(bf16[48,4096]{1,0:T(8,128)(2,1)S(1)} %convolution_convert_fusion), channel_id=1, source_target_pairs={{0,2},{1,3},{2,0},{3,1},{4,6},{5,7},{6,4},{7,5},{8,10},{9,11},{10,... | collective-permute-start | bytes 1179656 | tf_op jit(solution)/shard_map/ppermute | solution.py:457
  78.2 20.2 %collective-permute-start.21 = (bf16[48,4096]{1,0:T(8,128)(2,1)S(1)}, bf16[48,4096]{1,0:T(8,128)(2,1)S(1)}, u32[]{:S(2)}, u32[]{:S(2)}) collective-permute-start(bf16[48,4096]{1,0:T(8,128)(2,1)S(1)} %convolution_convert_fusion.1), channel_id=1, source_target_pairs={{0,1},{1,0},{2,3},{3,2},{4,5},{5,4},{6,7},{7,6},{8,9},{9,8},{10,11... | collective-permute-start | bytes 1179656 | tf_op jit(solution)/shard_map/ppermute | solution.py:457
  (11 other events, 119.1 us)

commit v6 on v5

--- a/solution.py
+++ b/solution.py
@@ -363,7 +363,7 @@
     here, gone, peaks, totals, summed = refs[2 * blocks :]
     tokens, width = came.shape
     heads = width // HEAD_SIZE
-    score_scale = HEAD_SIZE ** (-0.5)
+    score_scale = HEAD_SIZE ** (-0.5) / math.log(2.0)
     block_rows = 4 * rows
     early_rows = 2 * block_rows - late[0].shape[0]
     whole = kept[...] + other_part(came[...], rows).astype(jnp.float32)
@@ -384,7 +384,7 @@
 
     line = lax.broadcasted_iota(jnp.int32, (tokens, 1), 0)
     second = (line >= rows).astype(jnp.int32)
-    row_index = place_outer * 2 * block_rows + inside(slot, second, line - rows * second)
+    row_place = inside(slot, second, line - rows * second)
     line = lax.broadcasted_iota(jnp.int32, (1, 2 * block_rows), 1)
     slots = sum((line >= 2 * rows * number).astype(jnp.int32) for number in range(1, 4))
     left = line - 2 * rows * slots
@@ -395,15 +395,18 @@
         stop = start + HEAD_SIZE
         return jnp.concatenate([early[block][:early_rows, start:stop], late[block][:, start:stop]], axis=0)
 
+    def key_document(block):
+        lines = early[block][early_rows:, :].astype(jnp.float32)
+        rest = 2 * block_rows - lines.shape[1]
+        return jnp.concatenate([lines[0:1, :], lines[1:2, :rest]], axis=1)
+
     def block_scores(block):
         scores = lax.dot_general(
             stacked, joined(block, 0), (((1,), (1,)), ((), ())), preferred_element_type=jnp.float32
         )
-        places = (place_outer ^ block) * 2 * block_rows + key_place
-        lines = early[block][early_rows:, :].astype(jnp.float32)
-        rest = 2 * block_rows - lines.shape[1]
-        key_document = jnp.concatenate([lines[0:1, :], lines[1:2, :rest]], axis=1)
-        allowed = (places <= row_index) & (key_document == document)
+        allowed = key_document(block) == document
+        if block == 0:
+            allowed = allowed & (key_place <= row_place)
         scores = scores.reshape(heads, tokens, -1) * score_scale
         return jnp.where(allowed[None], scores, masked_score).reshape(heads * tokens, -1)
 
@@ -412,19 +415,20 @@
 
     scores = block_scores(0)
     peak = jnp.max(scores, axis=-1, keepdims=True)
-    weights = jnp.exp(scores - peak)
+    weights = jnp.exp2(scores - peak)
     peaks[...] = peak
     totals[...] = jnp.sum(weights, axis=-1, keepdims=True)
     summed[...] = weighted(0, weights)
+    lowest = jnp.min(document)
     for block in range(1, blocks):
 
-        @pl.when((place_outer ^ block) < place_outer)
+        @pl.when(((place_outer ^ block) < place_outer) & (jnp.max(key_document(block)) >= lowest))
         def _():
             scores = block_scores(block)
             before = peaks[...]
             peak = jnp.maximum(before, jnp.max(scores, axis=-1, keepdims=True))
-            weights = jnp.exp(scores - peak)
-            shrink = jnp.exp(before - peak)
+            weights = jnp.exp2(scores - peak)
+            shrink = jnp.exp2(before - peak)
             peaks[...] = peak
             totals[...] = totals[...] * shrink + jnp.sum(weights, axis=-1, keepdims=True)
             summed[...] = summed[...] * shrink + weighted(block, weights)

time: 100 us -> 98.8 us (0.988); the launches traced: 99.4 us -> 97.1 us
  waiting for transfers between devices: 39.2 us -> 35.8 us
  Pallas kernels: 17.4 us -> 18.5 us
    ppermute x23, waiting for transfers between devices: 28.8 us -> 25.5 us  [send(): return lax.ppermute(value, axis, pairs)]
    pallas_call x18, Pallas kernels: 17.4 us -> 18.5 us  [call_kernel(): pl.pallas_call(kernel, name=name, grid_spec=pltpu.PrefetchScalarGridSpec(...]
  transfers between devices with their start and end apart: 25 -> 25, of which waited for: 11 -> 11; matrix products, arithmetic and copies ran while one was open for 12% -> 12% of each run, Pallas kernels for 17% -> 19%
where the time goes in v6:
time: 98.8 us; the launch traced here: 97.1 us
  waiting for transfers between devices  35.8 us (36%)
  starting transfers between devices  28.1 us (28%)
  Pallas kernels  18.5 us (19%)
  matrix products  10.1 us (10%)
  other arithmetic  2.46 us (2%)
  local copies, waits for them, and re-layouts  1.83 us (2%)
    ppermute x23, waiting for transfers between devices, send(): return lax.ppermute(value, axis, pairs)  25.5 us
    ppermute x23, starting transfers between devices, send(): return lax.ppermute(value, axis, pairs)  24.1 us
    pallas_call x18, Pallas kernels, call_kernel(): pl.pallas_call(kernel, name=name, grid_spec=pltpu.PrefetchScalarGridSpec(...  18.5 us
    ppermute x2, waiting for transfers between devices, send_across(): return lax.ppermute(value, ('inner', 'tensor'), both)  10.3 us
    dot_general x10, matrix products, product(): return jnp.dot(left, right, preferred_element_type=jnp.float32)  10.1 us
    ppermute x2, starting transfers between devices, send_across(): return lax.ppermute(value, ('inner', 'tensor'), both)  4 us
  transfers between devices with their start and end apart: 25, of which 11 were waited for; matrix products, arithmetic and copies ran while one was open for 12% of the time, Pallas kernels for 19%

profile of v6, /device:TPU:2, one launch (start us, length us, event | category | flops | bytes accessed | tf_op | source)
XLA Modules:
  0.0 97.1 jit_solution(10545351043393129761)
XLA Ops:
  2.1 3.6 %collective-permute-start.4 = (bf16[48,2048]{1,0:T(8,128)(2,1)S(1)}, bf16[48,2048]{1,0:T(8,128)(2,1)S(1)}, u32[]{:S(2)}, u32[]{:S(2)}) collective-permute-start(bf16[48,2048]{1,0:T(8,128)(2,1)S(1)} %get-tuple-element.30), channel_id=1, source_target_pairs={{0,6},{1,7},{2,4},{3,5},{4,2},{5,3},{6,0},{7,1},{8,14},{9,15},{10,... | collective-permute-start | bytes 589832 | tf_op jit(solution)/shard_map/ppermute | solution.py:465
  6.1 1.6 %collective-permute-start.1 = (bf16[48,2048]{1,0:T(8,128)(2,1)S(1)}, bf16[48,2048]{1,0:T(8,128)(2,1)S(1)}, u32[]{:S(2)}, u32[]{:S(2)}) collective-permute-start(bf16[48,2048]{1,0:T(8,128)(2,1)S(1)} %get-tuple-element.29.refs_0_), channel_id=1, source_target_pairs={{0,1},{1,0},{2,3},{3,2},{4,5},{5,4},{6,7},{7,6},{8,9},{9,8},{10,11... | collective-permute-start | bytes 589832 | tf_op jit(solution)/shard_map/ppermute | solution.py:461
  8.0 1.5 %collective-permute-start = (bf16[48,2048]{1,0:T(8,128)(2,1)S(1)}, bf16[48,2048]{1,0:T(8,128)(2,1)S(1)}, u32[]{:S(2)}, u32[]{:S(2)}) collective-permute-start(bf16[48,2048]{1,0:T(8,128)(2,1)S(1)} %get-tuple-element.30), channel_id=1, source_target_pairs={{0,4},{4,0},{1,5},{5,1},{2,6},{6,2},{3,7},{7,3},{8,12},{12,8},{9,1... | collective-permute-start | bytes 589832 | tf_op jit(solution)/shard_map/ppermute | solution.py:461
  10.2 10.0 %collective-permute-done.4.refs_5_ = bf16[48,2048]{1,0:T(8,128)(2,1)S(1)} collective-permute-done((bf16[48,2048]{1,0:T(8,128)(2,1)S(1)}, bf16[48,2048]{1,0:T(8,128)(2,1)S(1)}, u32[]{:S(2)}, u32[]{:S(2)}) %collective-permute-start.4) | collective-permute-done | bytes 196640 | tf_op jit(solution)/shard_map/ppermute | solution.py:465
  20.3 1.5 %collective-permute-start.9 = (s32[2,192]{1,0:T(2,128)S(1)}, s32[2,192]{1,0:T(2,128)S(1)}, u32[]{:S(2)}, u32[]{:S(2)}) collective-permute-start(s32[2,192]{1,0:T(2,128)S(1)} %pad_add_fusion.here), channel_id=1, source_target_pairs={{0,4},{4,0},{1,5},{5,1},{2,6},{6,2},{3,7},{7,3},{8,12},{12,8},{9,1... | collective-permute-start | bytes 4616 | tf_op jit(solution)/shard_map/ppermute | solution.py:461
  21.8 1.6 %collective-permute-done.3.refs_4_ = bf16[48,2048]{1,0:T(8,128)(2,1)S(1)} collective-permute-done((bf16[48,2048]{1,0:T(8,128)(2,1)S(1)}, bf16[48,2048]{1,0:T(8,128)(2,1)S(1)}, u32[]{:S(2)}, u32[]{:S(2)}) %collective-permute-start.3) | collective-permute-done | bytes 196640 | tf_op jit(solution)/shard_map/ppermute | solution.py:461
  25.4 1.5 %collective-permute-start.10 = (f32[288,256]{1,0:T(8,128)S(1)}, f32[288,256]{1,0:T(8,128)S(1)}, u32[]{:S(2)}, u32[]{:S(2)}) collective-permute-start(f32[288,256]{1,0:T(8,128)S(1)} %sent.6), channel_id=1, source_target_pairs={{0,4},{4,0},{1,5},{5,1},{2,6},{6,2},{3,7},{7,3},{8,12},{12,8},{9,1... | collective-permute-start | bytes 884744 | tf_op jit(solution)/shard_map/ppermute | solution.py:461
  29.0 1.4 %fusion.refs_0_.kept = f32[288,1024]{1,0:T(8,128)S(1)} fusion(bf16[288,2048]{1,0:T(8,128)(2,1)S(1)} %get-tuple-element.31, bf16[2048,1024]{1,0:T(8,128)(2,1)S(1)} %copy-done.5), kind=kOutput, calls=%fused_computation.8 | convolution fusion | flops 1207959552 | bytes 6553600 | tf_op jit(solution)/shard_map/dot_general | solution.py:273
  33.2 1.8 %collective-permute-done.10.came = f32[288,256]{1,0:T(8,128)S(1)} collective-permute-done((f32[288,256]{1,0:T(8,128)S(1)}, f32[288,256]{1,0:T(8,128)S(1)}, u32[]{:S(2)}, u32[]{:S(2)}) %collective-permute-start.10) | collective-permute-done | bytes 294944 | tf_op jit(solution)/shard_map/ppermute | solution.py:461
  35.4 2.1 %collective-permute-done.6.refs_0_ = bf16[96,2048]{1,0:T(8,128)(2,1)S(1)} collective-permute-done((bf16[96,2048]{1,0:T(8,128)(2,1)S(1)}, bf16[96,2048]{1,0:T(8,128)(2,1)S(1)}, u32[]{:S(2)}, u32[]{:S(2)}) %collective-permute-start.6) | collective-permute-done | bytes 393248 | tf_op jit(solution)/shard_map/ppermute | solution.py:461
  38.8 1.3 %collective-permute-start.14 = (f32[96,256]{1,0:T(8,128)S(1)}, f32[96,256]{1,0:T(8,128)S(1)}, u32[]{:S(2)}, u32[]{:S(2)}) collective-permute-start(f32[96,256]{1,0:T(8,128)S(1)} %sent.7), channel_id=1, source_target_pairs={{0,4},{4,0},{1,5},{5,1},{2,6},{6,2},{3,7},{7,3},{8,12},{12,8},{9,1... | collective-permute-start | bytes 294920 | tf_op jit(solution)/shard_map/ppermute | solution.py:461
  44.3 2.7 %collective-permute-done.8.came = bf16[96,512]{1,0:T(8,128)(2,1)S(1)} collective-permute-done((bf16[96,512]{1,0:T(8,128)(2,1)S(1)}, bf16[96,512]{1,0:T(8,128)(2,1)S(1)}, u32[]{:S(2)}, u32[]{:S(2)}) %collective-permute-start.8) | collective-permute-done | bytes 98336 | tf_op jit(solution)/shard_map/ppermute | solution.py:461
  48.3 3.1 %attention.4 = (bf16[48,512]{1,0:T(8,128)(2,1)S(1)}, bf16[48,512]{1,0:T(8,128)(2,1)S(1)}) custom-call(s32[3]{0:T(128)S(1)} %pad_add_fusion.1.which, f32[96,1024]{1,0:T(8,128)S(1)} %fusion.1.refs_0_.kept, bf16[96,512]{1,0:T(8,128)(2,1)S(1)} %collective-permute-done.8.came, f32[384,128]{1,0:T(8,128)S(1)} %get-tuple-element.48.cosines, ...), custom_call_target="tpu_custom_call" | custom-call | tf_op jit(solution)/shard_map/attention/pallas_call | solution.py:217
  51.4 1.3 %collective-permute-start.18 = (bf16[48,512]{1,0:T(8,128)(2,1)S(1)}, bf16[48,512]{1,0:T(8,128)(2,1)S(1)}, u32[]{:S(2)}, u32[]{:S(2)}) collective-permute-start(bf16[48,512]{1,0:T(8,128)(2,1)S(1)} %get-tuple-element.39), channel_id=1, source_target_pairs={{0,4},{4,0},{1,5},{5,1},{2,6},{6,2},{3,7},{7,3},{8,12},{12,8},{9,1... | collective-permute-start | bytes 147464 | tf_op jit(solution)/shard_map/ppermute | solution.py:461
  52.7 3.1 %attention.7 = (bf16[48,512]{1,0:T(8,128)(2,1)S(1)}, bf16[48,512]{1,0:T(8,128)(2,1)S(1)}) custom-call(s32[3]{0:T(128)S(1)} %pad_add_fusion.1.which, f32[288,1024]{1,0:T(8,128)S(1)} %fusion.refs_0_.kept, bf16[288,512]{1,0:T(8,128)(2,1)S(1)} %collective-permute-done.5.came, f32[384,128]{1,0:T(8,128)S(1)} %get-tuple-element.48.cosines, ...), custom_call_target="tpu_custom_call" | custom-call | tf_op jit(solution)/shard_map/attention/pallas_call | solution.py:217
  57.4 1.6 %convolution_convert_fusion.2 = bf16[48,4096]{1,0:T(8,128)(2,1)S(1)} fusion(bf16[48,1024]{1,0:T(8,128)(2,1)S(1)} %join.4, bf16[1024,4096]{1,0:T(8,128)(2,1)S(1)} %bitcast.28), kind=kOutput, calls=%fused_computation.2 | convolution fusion | flops 402849792 | bytes 8880128 | tf_op jit(solution)/shard_map/dot_general | solution.py:273
  59.0 4.6 %collective-permute-start.24 = (bf16[48,4096]{1,0:T(8,128)(2,1)S(1)}, bf16[48,4096]{1,0:T(8,128)(2,1)S(1)}, u32[]{:S(2)}, u32[]{:S(2)}) collective-permute-start(bf16[48,4096]{1,0:T(8,128)(2,1)S(1)} %convolution_convert_fusion.2), channel_id=1, source_target_pairs={{0,3},{1,2},{2,1},{3,0},{4,7},{5,6},{6,5},{7,4},{8,11},{9,10},{10,... | collective-permute-start | bytes 1179656 | tf_op jit(solution)/shard_map/ppermute | solution.py:461
  63.6 3.1 %attention.6 = (bf16[48,512]{1,0:T(8,128)(2,1)S(1)}, bf16[48,512]{1,0:T(8,128)(2,1)S(1)}) custom-call(s32[3]{0:T(128)S(1)} %pad_add_fusion.1.which, f32[288,1024]{1,0:T(8,128)S(1)} %fusion.refs_0_.kept, bf16[288,512]{1,0:T(8,128)(2,1)S(1)} %collective-permute-done.5.came, f32[384,128]{1,0:T(8,128)S(1)} %get-tuple-element.48.cosines, ...), custom_call_target="tpu_custom_call" | custom-call | tf_op jit(solution)/shard_map/attention/pallas_call | solution.py:217
  68.0 3.1 %attention.5 = (bf16[48,512]{1,0:T(8,128)(2,1)S(1)}, bf16[48,512]{1,0:T(8,128)(2,1)S(1)}) custom-call(s32[3]{0:T(128)S(1)} %pad_add_fusion.1.which, f32[288,1024]{1,0:T(8,128)S(1)} %fusion.refs_0_.kept, bf16[288,512]{1,0:T(8,128)(2,1)S(1)} %collective-permute-done.5.came, f32[384,128]{1,0:T(8,128)S(1)} %get-tuple-element.48.cosines, ...), custom_call_target="tpu_custom_call" | custom-call | tf_op jit(solution)/shard_map/attention/pallas_call | solution.py:217
  72.5 1.6 %convolution_convert_fusion = bf16[48,4096]{1,0:T(8,128)(2,1)S(1)} fusion(bf16[48,1024]{1,0:T(8,128)(2,1)S(1)} %join.7, bf16[1024,4096]{1,0:T(8,128)(2,1)S(1)} %bitcast.28), kind=kOutput, calls=%fused_computation | convolution fusion | flops 402849792 | bytes 8880128 | tf_op jit(solution)/shard_map/dot_general | solution.py:273
  74.1 3.1 %collective-permute-start.23 = (bf16[48,4096]{1,0:T(8,128)(2,1)S(1)}, bf16[48,4096]{1,0:T(8,128)(2,1)S(1)}, u32[]{:S(2)}, u32[]{:S(2)}) collective-permute-start(bf16[48,4096]{1,0:T(8,128)(2,1)S(1)} %convolution_convert_fusion), channel_id=1, source_target_pairs={{0,2},{1,3},{2,0},{3,1},{4,6},{5,7},{6,4},{7,5},{8,10},{9,11},{10,... | collective-permute-start | bytes 1179656 | tf_op jit(solution)/shard_map/ppermute | solution.py:461
  77.7 1.6 %convolution_convert_fusion.1 = bf16[48,4096]{1,0:T(8,128)(2,1)S(1)} fusion(bf16[48,1024]{1,0:T(8,128)(2,1)S(1)} %join.6, bf16[1024,4096]{1,0:T(8,128)(2,1)S(1)} %bitcast.28), kind=kOutput, calls=%fused_computation.1 | convolution fusion | flops 402849792 | bytes 8880128 | tf_op jit(solution)/shard_map/dot_general | solution.py:273
  80.0 1.6 %fusion.6 = f32[48,4096]{1,0:T(8,128)S(1)} fusion(bf16[48,1024]{1,0:T(8,128)(2,1)S(1)} %join.5, bf16[1024,4096]{1,0:T(8,128)(2,1)S(1)} %bitcast.28), kind=kOutput, calls=%fused_computation.14 | convolution fusion | flops 402653184 | bytes 9273344 | tf_op jit(solution)/shard_map/dot_general | solution.py:273
  81.6 14.6 %collective-permute-done.23 = bf16[48,4096]{1,0:T(8,128)(2,1)S(1)} collective-permute-done((bf16[48,4096]{1,0:T(8,128)(2,1)S(1)}, bf16[48,4096]{1,0:T(8,128)(2,1)S(1)}, u32[]{:S(2)}, u32[]{:S(2)}) %collective-permute-start.23) | collective-permute-done | bytes 393248 | tf_op jit(solution)/shard_map/ppermute | solution.py:461
  (79 shorter events, 23.9 us)
Async XLA Ops:
  2.1 18.2 %collective-permute-start.4 = (bf16[48,2048]{1,0:T(8,128)(2,1)S(1)}, bf16[48,2048]{1,0:T(8,128)(2,1)S(1)}, u32[]{:S(2)}, u32[]{:S(2)}) collective-permute-start(bf16[48,2048]{1,0:T(8,128)(2,1)S(1)} %get-tuple-element.30), channel_id=1, source_target_pairs={{0,6},{1,7},{2,4},{3,5},{4,2},{5,3},{6,0},{7,1},{8,14},{9,15},{10,... | collective-permute-start | bytes 589832 | tf_op jit(solution)/shard_map/ppermute | solution.py:465
  5.7 17.7 %collective-permute-start.3 = (bf16[48,2048]{1,0:T(8,128)(2,1)S(1)}, bf16[48,2048]{1,0:T(8,128)(2,1)S(1)}, u32[]{:S(2)}, u32[]{:S(2)}) collective-permute-start(bf16[48,2048]{1,0:T(8,128)(2,1)S(1)} %get-tuple-element.29.refs_0_), channel_id=1, source_target_pairs={{0,2},{1,3},{2,0},{3,1},{4,6},{5,7},{6,4},{7,5},{8,10},{9,11},{10,... | collective-permute-start | bytes 589832 | tf_op jit(solution)/shard_map/ppermute | solution.py:461
  6.1 17.4 %collective-permute-start.1 = (bf16[48,2048]{1,0:T(8,128)(2,1)S(1)}, bf16[48,2048]{1,0:T(8,128)(2,1)S(1)}, u32[]{:S(2)}, u32[]{:S(2)}) collective-permute-start(bf16[48,2048]{1,0:T(8,128)(2,1)S(1)} %get-tuple-element.29.refs_0_), channel_id=1, source_target_pairs={{0,1},{1,0},{2,3},{3,2},{4,5},{5,4},{6,7},{7,6},{8,9},{9,8},{10,11... | collective-permute-start | bytes 589832 | tf_op jit(solution)/shard_map/ppermute | solution.py:461
  7.6 16.1 %collective-permute-start.2 = (bf16[48,2048]{1,0:T(8,128)(2,1)S(1)}, bf16[48,2048]{1,0:T(8,128)(2,1)S(1)}, u32[]{:S(2)}, u32[]{:S(2)}) collective-permute-start(bf16[48,2048]{1,0:T(8,128)(2,1)S(1)} %get-tuple-element.30), channel_id=1, source_target_pairs={{0,5},{1,4},{2,7},{3,6},{4,1},{5,0},{6,3},{7,2},{8,13},{9,12},{10,... | collective-permute-start | bytes 589832 | tf_op jit(solution)/shard_map/ppermute | solution.py:465
  8.0 15.7 %collective-permute-start = (bf16[48,2048]{1,0:T(8,128)(2,1)S(1)}, bf16[48,2048]{1,0:T(8,128)(2,1)S(1)}, u32[]{:S(2)}, u32[]{:S(2)}) collective-permute-start(bf16[48,2048]{1,0:T(8,128)(2,1)S(1)} %get-tuple-element.30), channel_id=1, source_target_pairs={{0,4},{4,0},{1,5},{5,1},{2,6},{6,2},{3,7},{7,3},{8,12},{12,8},{9,1... | collective-permute-start | bytes 589832 | tf_op jit(solution)/shard_map/ppermute | solution.py:461
  20.3 11.3 %collective-permute-start.9 = (s32[2,192]{1,0:T(2,128)S(1)}, s32[2,192]{1,0:T(2,128)S(1)}, u32[]{:S(2)}, u32[]{:S(2)}) collective-permute-start(s32[2,192]{1,0:T(2,128)S(1)} %pad_add_fusion.here), channel_id=1, source_target_pairs={{0,4},{4,0},{1,5},{5,1},{2,6},{6,2},{3,7},{7,3},{8,12},{12,8},{9,1... | collective-permute-start | bytes 4616 | tf_op jit(solution)/shard_map/ppermute | solution.py:461
  25.4 9.5 %collective-permute-start.10 = (f32[288,256]{1,0:T(8,128)S(1)}, f32[288,256]{1,0:T(8,128)S(1)}, u32[]{:S(2)}, u32[]{:S(2)}) collective-permute-start(f32[288,256]{1,0:T(8,128)S(1)} %sent.6), channel_id=1, source_target_pairs={{0,4},{4,0},{1,5},{5,1},{2,6},{6,2},{3,7},{7,3},{8,12},{12,8},{9,1... | collective-permute-start | bytes 884744 | tf_op jit(solution)/shard_map/ppermute | solution.py:461
  26.9 10.6 %collective-permute-start.6 = (bf16[96,2048]{1,0:T(8,128)(2,1)S(1)}, bf16[96,2048]{1,0:T(8,128)(2,1)S(1)}, u32[]{:S(2)}, u32[]{:S(2)}) collective-permute-start(bf16[96,2048]{1,0:T(8,128)(2,1)S(1)} %get-tuple-element.32), channel_id=1, source_target_pairs={{1,0},{2,3},{5,4},{6,7},{9,8},{10,11},{13,12},{14,15},{17,16},{18,... | collective-permute-start | bytes 1179656 | tf_op jit(solution)/shard_map/ppermute | solution.py:461
  28.3 9.2 %collective-permute-start.7 = (bf16[96,2048]{1,0:T(8,128)(2,1)S(1)}, bf16[96,2048]{1,0:T(8,128)(2,1)S(1)}, u32[]{:S(2)}, u32[]{:S(2)}) collective-permute-start(bf16[96,2048]{1,0:T(8,128)(2,1)S(1)} %get-tuple-element.33), channel_id=1, source_target_pairs={{1,2},{2,1},{5,6},{6,5},{9,10},{10,9},{13,14},{14,13},{17,18},{18,... | collective-permute-start | bytes 1179656 | tf_op jit(solution)/shard_map/ppermute | solution.py:461
  31.0 21.7 %collective-permute-start.5 = (bf16[288,512]{1,0:T(8,128)(2,1)S(1)}, bf16[288,512]{1,0:T(8,128)(2,1)S(1)}, u32[]{:S(2)}, u32[]{:S(2)}) collective-permute-start(bf16[288,512]{1,0:T(8,128)(2,1)S(1)} %sent.4), channel_id=1, source_target_pairs={{0,4},{4,0},{1,5},{5,1},{2,6},{6,2},{3,7},{7,3},{8,12},{12,8},{9,1... | collective-permute-start | bytes 884744 | tf_op jit(solution)/shard_map/ppermute | solution.py:461
  35.1 5.3 %collective-permute-start.12 = (bf16[304,256]{1,0:T(8,128)(2,1)S(1)}, bf16[304,256]{1,0:T(8,128)(2,1)S(1)}, u32[]{:S(2)}, u32[]{:S(2)}) collective-permute-start(bf16[304,256]{1,0:T(8,128)(2,1)S(1)} %pair.2.refs_0_), channel_id=1, source_target_pairs={{0,16},{8,24},{16,0},{24,8},{1,17},{9,25},{17,1},{25,9},{2,18},{10... | collective-permute-start | bytes 466952 | tf_op jit(solution)/shard_map/ppermute | solution.py:461
  35.4 8.2 %collective-permute-start.11 = (bf16[304,256]{1,0:T(8,128)(2,1)S(1)}, bf16[304,256]{1,0:T(8,128)(2,1)S(1)}, u32[]{:S(2)}, u32[]{:S(2)}) collective-permute-start(bf16[304,256]{1,0:T(8,128)(2,1)S(1)} %pair.2.refs_0_), channel_id=1, source_target_pairs={{0,8},{8,0},{16,24},{24,16},{1,9},{9,1},{17,25},{25,17},{2,10},{10... | collective-permute-start | bytes 466952 | tf_op jit(solution)/shard_map/ppermute | solution.py:461
  38.8 4.7 %collective-permute-start.14 = (f32[96,256]{1,0:T(8,128)S(1)}, f32[96,256]{1,0:T(8,128)S(1)}, u32[]{:S(2)}, u32[]{:S(2)}) collective-permute-start(f32[96,256]{1,0:T(8,128)S(1)} %sent.7), channel_id=1, source_target_pairs={{0,4},{4,0},{1,5},{5,1},{2,6},{6,2},{3,7},{7,3},{8,12},{12,8},{9,1... | collective-permute-start | bytes 294920 | tf_op jit(solution)/shard_map/ppermute | solution.py:461
  40.4 7.9 %collective-permute-start.13 = (bf16[304,256]{1,0:T(8,128)(2,1)S(1)}, bf16[304,256]{1,0:T(8,128)(2,1)S(1)}, u32[]{:S(2)}, u32[]{:S(2)}) collective-permute-start(bf16[304,256]{1,0:T(8,128)(2,1)S(1)} %collective-permute-done.12.refs_2_), channel_id=1, source_target_pairs={{0,8},{8,0},{16,24},{24,16},{1,9},{9,1},{17,25},{25,17},{2,10},{10... | collective-permute-start | bytes 466952 | tf_op jit(solution)/shard_map/ppermute | solution.py:461
  41.8 5.3 %collective-permute-start.8 = (bf16[96,512]{1,0:T(8,128)(2,1)S(1)}, bf16[96,512]{1,0:T(8,128)(2,1)S(1)}, u32[]{:S(2)}, u32[]{:S(2)}) collective-permute-start(bf16[96,512]{1,0:T(8,128)(2,1)S(1)} %sent.5), channel_id=1, source_target_pairs={{0,4},{4,0},{1,5},{5,1},{2,6},{6,2},{3,7},{7,3},{8,12},{12,8},{9,1... | collective-permute-start | bytes 294920 | tf_op jit(solution)/shard_map/ppermute | solution.py:461
  43.5 3.6 %collective-permute-start.17 = (bf16[96,256]{1,0:T(8,128)(2,1)S(1)}, bf16[96,256]{1,0:T(8,128)(2,1)S(1)}, u32[]{:S(2)}, u32[]{:S(2)}) collective-permute-start(bf16[96,256]{1,0:T(8,128)(2,1)S(1)} %pair.3.refs_4_), channel_id=1, source_target_pairs={{0,24},{8,16},{16,8},{24,0},{1,25},{9,17},{17,9},{25,1},{2,26},{10... | collective-permute-start | bytes 147464 | tf_op jit(solution)/shard_map/ppermute | solution.py:461
  43.6 4.5 %collective-permute-start.16 = (bf16[96,256]{1,0:T(8,128)(2,1)S(1)}, bf16[96,256]{1,0:T(8,128)(2,1)S(1)}, u32[]{:S(2)}, u32[]{:S(2)}) collective-permute-start(bf16[96,256]{1,0:T(8,128)(2,1)S(1)} %pair.3.refs_4_), channel_id=1, source_target_pairs={{0,16},{8,24},{16,0},{24,8},{1,17},{9,25},{17,1},{25,9},{2,18},{10... | collective-permute-start | bytes 147464 | tf_op jit(solution)/shard_map/ppermute | solution.py:461
  51.4 5.2 %collective-permute-start.18 = (bf16[48,512]{1,0:T(8,128)(2,1)S(1)}, bf16[48,512]{1,0:T(8,128)(2,1)S(1)}, u32[]{:S(2)}, u32[]{:S(2)}) collective-permute-start(bf16[48,512]{1,0:T(8,128)(2,1)S(1)} %get-tuple-element.39), channel_id=1, source_target_pairs={{0,4},{4,0},{1,5},{5,1},{2,6},{6,2},{3,7},{7,3},{8,12},{12,8},{9,1... | collective-permute-start | bytes 147464 | tf_op jit(solution)/shard_map/ppermute | solution.py:461
  55.8 16.1 %collective-permute-start.22 = (bf16[48,512]{1,0:T(8,128)(2,1)S(1)}, bf16[48,512]{1,0:T(8,128)(2,1)S(1)}, u32[]{:S(2)}, u32[]{:S(2)}) collective-permute-start(bf16[48,512]{1,0:T(8,128)(2,1)S(1)} %get-tuple-element.46), channel_id=1, source_target_pairs={{0,4},{4,0},{1,5},{5,1},{2,6},{6,2},{3,7},{7,3},{8,12},{12,8},{9,1... | collective-permute-start | bytes 147464 | tf_op jit(solution)/shard_map/ppermute | solution.py:461
  59.0 37.1 %collective-permute-start.24 = (bf16[48,4096]{1,0:T(8,128)(2,1)S(1)}, bf16[48,4096]{1,0:T(8,128)(2,1)S(1)}, u32[]{:S(2)}, u32[]{:S(2)}) collective-permute-start(bf16[48,4096]{1,0:T(8,128)(2,1)S(1)} %convolution_convert_fusion.2), channel_id=1, source_target_pairs={{0,3},{1,2},{2,1},{3,0},{4,7},{5,6},{6,5},{7,4},{8,11},{9,10},{10,... | collective-permute-start | bytes 1179656 | tf_op jit(solution)/shard_map/ppermute | solution.py:461
  66.7 10.5 %collective-permute-start.20 = (bf16[48,512]{1,0:T(8,128)(2,1)S(1)}, bf16[48,512]{1,0:T(8,128)(2,1)S(1)}, u32[]{:S(2)}, u32[]{:S(2)}) collective-permute-start(bf16[48,512]{1,0:T(8,128)(2,1)S(1)} %get-tuple-element.44), channel_id=1, source_target_pairs={{0,4},{4,0},{1,5},{5,1},{2,6},{6,2},{3,7},{7,3},{8,12},{12,8},{9,1... | collective-permute-start | bytes 147464 | tf_op jit(solution)/shard_map/ppermute | solution.py:461
  71.1 8.3 %collective-permute-start.19 = (bf16[48,512]{1,0:T(8,128)(2,1)S(1)}, bf16[48,512]{1,0:T(8,128)(2,1)S(1)}, u32[]{:S(2)}, u32[]{:S(2)}) collective-permute-start(bf16[48,512]{1,0:T(8,128)(2,1)S(1)} %get-tuple-element.42), channel_id=1, source_target_pairs={{0,4},{4,0},{1,5},{5,1},{2,6},{6,2},{3,7},{7,3},{8,12},{12,8},{9,1... | collective-permute-start | bytes 147464 | tf_op jit(solution)/shard_map/ppermute | solution.py:461
  74.1 22.0 %collective-permute-start.23 = (bf16[48,4096]{1,0:T(8,128)(2,1)S(1)}, bf16[48,4096]{1,0:T(8,128)(2,1)S(1)}, u32[]{:S(2)}, u32[]{:S(2)}) collective-permute-start(bf16[48,4096]{1,0:T(8,128)(2,1)S(1)} %convolution_convert_fusion), channel_id=1, source_target_pairs={{0,2},{1,3},{2,0},{3,1},{4,6},{5,7},{6,4},{7,5},{8,10},{9,11},{10,... | collective-permute-start | bytes 1179656 | tf_op jit(solution)/shard_map/ppermute | solution.py:461
  79.3 16.8 %collective-permute-start.21 = (bf16[48,4096]{1,0:T(8,128)(2,1)S(1)}, bf16[48,4096]{1,0:T(8,128)(2,1)S(1)}, u32[]{:S(2)}, u32[]{:S(2)}) collective-permute-start(bf16[48,4096]{1,0:T(8,128)(2,1)S(1)} %convolution_convert_fusion.1), channel_id=1, source_target_pairs={{0,1},{1,0},{2,3},{3,2},{4,5},{5,4},{6,7},{7,6},{8,9},{9,8},{10,11... | collective-permute-start | bytes 1179656 | tf_op jit(solution)/shard_map/ppermute | solution.py:461
  (11 other events, 116.8 us)

commit v7 on v6

--- a/solution.py
+++ b/solution.py
@@ -552,7 +552,7 @@
     ends_rows = send(two_rows, "tensor", [(1, 0), (2, 3)])
     early_projected = project_pair(early_stacked)
     early_queries, early_came = project_query(early_stacked)
-    late_stacked = stack("late_rows", [[ends_rows, middle_rows]], (1,))[0]
+    late_stacked = stack("late_rows", [[middle_rows, ends_rows]], (1,))[0]
     late_projected = project_pair(late_stacked)
     late_queries, late_came = project_query(late_stacked)
     early_pairs = gather_by_steps(rotate_pair(early_projected, 0, [document_rows]))
@@ -593,10 +593,11 @@
     rows_2 = joined(2)
     term_3 = product(rows_3, w_out).astype(bf16)
     came_3 = send(term_3, "tensor", swap_pairs(4, 3))
-    came_2 = send(product(rows_2, w_out).astype(bf16), "tensor", two)
+    term_2 = product(rows_2, w_out).astype(bf16)
+    came_2 = send(term_2, "tensor", two)
     rows_1 = joined(1, term_3)
     came_1 = send(product(rows_1, w_out).astype(bf16), "tensor", one)
-    rows_0 = joined(0, term_3)
+    rows_0 = joined(0, term_2)
     total = lax.optimization_barrier(product(rows_0, w_out))
     total = total + hidden_in.astype(jnp.float32) + came_1.astype(jnp.float32)
     total = total + came_2.astype(jnp.float32) + came_3.astype(jnp.float32)

time: 98.8 us -> 98.3 us (level)
  starting transfers between devices: 28.1 us -> 25.2 us
  waiting for transfers between devices: 35.8 us -> 38.1 us
    ppermute x23, starting transfers between devices: 24.1 us -> 21.2 us  [send(): return lax.ppermute(value, axis, pairs)]
    ppermute x23, waiting for transfers between devices: 25.5 us -> 27.7 us  [send(): return lax.ppermute(value, axis, pairs)]
  transfers between devices with their start and end apart: 25 -> 25, of which waited for: 11 -> 10; matrix products, arithmetic and copies ran while one was open for 12% -> 12% of each run, Pallas kernels for 19% -> 19%
where the time goes in v7:
time: 98.3 us; the launch traced here: 96.6 us
  waiting for transfers between devices  38.1 us (39%)
  starting transfers between devices  25.2 us (26%)
  Pallas kernels  18.5 us (19%)
  matrix products  10.1 us (10%)
  other arithmetic  2.46 us (3%)
  local copies, waits for them, and re-layouts  1.83 us (2%)
    ppermute x23, waiting for transfers between devices, send(): return lax.ppermute(value, axis, pairs)  27.7 us
    ppermute x23, starting transfers between devices, send(): return lax.ppermute(value, axis, pairs)  21.2 us
    pallas_call x18, Pallas kernels, call_kernel(): pl.pallas_call(kernel, name=name, grid_spec=pltpu.PrefetchScalarGridSpec(...  18.5 us
    ppermute x2, waiting for transfers between devices, send_across(): return lax.ppermute(value, ('inner', 'tensor'), both)  10.3 us
    dot_general x10, matrix products, product(): return jnp.dot(left, right, preferred_element_type=jnp.float32)  10.1 us
    ppermute x2, starting transfers between devices, send_across(): return lax.ppermute(value, ('inner', 'tensor'), both)  4 us
  transfers between devices with their start and end apart: 25, of which 10 were waited for; matrix products, arithmetic and copies ran while one was open for 12% of the time, Pallas kernels for 19%

profile of v7, /device:TPU:2, one launch (start us, length us, event | category | flops | bytes accessed | tf_op | source)
XLA Modules:
  0.0 96.6 jit_solution(4775431822579451440)
XLA Ops:
  2.1 3.6 %collective-permute-start.4 = (bf16[48,2048]{1,0:T(8,128)(2,1)S(1)}, bf16[48,2048]{1,0:T(8,128)(2,1)S(1)}, u32[]{:S(2)}, u32[]{:S(2)}) collective-permute-start(bf16[48,2048]{1,0:T(8,128)(2,1)S(1)} %get-tuple-element.31), channel_id=1, source_target_pairs={{0,6},{1,7},{2,4},{3,5},{4,2},{5,3},{6,0},{7,1},{8,14},{9,15},{10,... | collective-permute-start | bytes 589832 | tf_op jit(solution)/shard_map/ppermute | solution.py:465
  6.1 1.6 %collective-permute-start.1 = (bf16[48,2048]{1,0:T(8,128)(2,1)S(1)}, bf16[48,2048]{1,0:T(8,128)(2,1)S(1)}, u32[]{:S(2)}, u32[]{:S(2)}) collective-permute-start(bf16[48,2048]{1,0:T(8,128)(2,1)S(1)} %get-tuple-element.30.refs_0_), channel_id=1, source_target_pairs={{0,1},{1,0},{2,3},{3,2},{4,5},{5,4},{6,7},{7,6},{8,9},{9,8},{10,11... | collective-permute-start | bytes 589832 | tf_op jit(solution)/shard_map/ppermute | solution.py:461
  8.0 1.5 %collective-permute-start = (bf16[48,2048]{1,0:T(8,128)(2,1)S(1)}, bf16[48,2048]{1,0:T(8,128)(2,1)S(1)}, u32[]{:S(2)}, u32[]{:S(2)}) collective-permute-start(bf16[48,2048]{1,0:T(8,128)(2,1)S(1)} %get-tuple-element.31), channel_id=1, source_target_pairs={{0,4},{4,0},{1,5},{5,1},{2,6},{6,2},{3,7},{7,3},{8,12},{12,8},{9,1... | collective-permute-start | bytes 589832 | tf_op jit(solution)/shard_map/ppermute | solution.py:461
  10.2 10.0 %collective-permute-done.4.refs_5_ = bf16[48,2048]{1,0:T(8,128)(2,1)S(1)} collective-permute-done((bf16[48,2048]{1,0:T(8,128)(2,1)S(1)}, bf16[48,2048]{1,0:T(8,128)(2,1)S(1)}, u32[]{:S(2)}, u32[]{:S(2)}) %collective-permute-start.4) | collective-permute-done | bytes 196640 | tf_op jit(solution)/shard_map/ppermute | solution.py:465
  20.3 1.5 %collective-permute-start.6 = (s32[2,192]{1,0:T(2,128)S(1)}, s32[2,192]{1,0:T(2,128)S(1)}, u32[]{:S(2)}, u32[]{:S(2)}) collective-permute-start(s32[2,192]{1,0:T(2,128)S(1)} %pad_add_fusion.here), channel_id=1, source_target_pairs={{0,4},{4,0},{1,5},{5,1},{2,6},{6,2},{3,7},{7,3},{8,12},{12,8},{9,1... | collective-permute-start | bytes 4616 | tf_op jit(solution)/shard_map/ppermute | solution.py:461
  21.8 1.6 %collective-permute-done.3.refs_4_ = bf16[48,2048]{1,0:T(8,128)(2,1)S(1)} collective-permute-done((bf16[48,2048]{1,0:T(8,128)(2,1)S(1)}, bf16[48,2048]{1,0:T(8,128)(2,1)S(1)}, u32[]{:S(2)}, u32[]{:S(2)}) %collective-permute-start.3) | collective-permute-done | bytes 196640 | tf_op jit(solution)/shard_map/ppermute | solution.py:461
  25.4 1.5 %collective-permute-start.7 = (f32[288,256]{1,0:T(8,128)S(1)}, f32[288,256]{1,0:T(8,128)S(1)}, u32[]{:S(2)}, u32[]{:S(2)}) collective-permute-start(f32[288,256]{1,0:T(8,128)S(1)} %sent.5), channel_id=1, source_target_pairs={{0,4},{4,0},{1,5},{5,1},{2,6},{6,2},{3,7},{7,3},{8,12},{12,8},{9,1... | collective-permute-start | bytes 884744 | tf_op jit(solution)/shard_map/ppermute | solution.py:461
  33.2 1.8 %collective-permute-done.7.came = f32[288,256]{1,0:T(8,128)S(1)} collective-permute-done((f32[288,256]{1,0:T(8,128)S(1)}, f32[288,256]{1,0:T(8,128)S(1)}, u32[]{:S(2)}, u32[]{:S(2)}) %collective-permute-start.7) | collective-permute-done | bytes 294944 | tf_op jit(solution)/shard_map/ppermute | solution.py:461
  35.4 4.2 %collective-permute-done.12.refs_1_ = bf16[96,2048]{1,0:T(8,128)(2,1)S(1)} collective-permute-done((bf16[96,2048]{1,0:T(8,128)(2,1)S(1)}, bf16[96,2048]{1,0:T(8,128)(2,1)S(1)}, u32[]{:S(2)}, u32[]{:S(2)}) %collective-permute-start.12) | collective-permute-done | bytes 393248 | tf_op jit(solution)/shard_map/ppermute | solution.py:461
  42.9 1.6 %collective-permute-start.19 = (bf16[96,512]{1,0:T(8,128)(2,1)S(1)}, bf16[96,512]{1,0:T(8,128)(2,1)S(1)}, u32[]{:S(2)}, u32[]{:S(2)}) collective-permute-start(bf16[96,512]{1,0:T(8,128)(2,1)S(1)} %sent.7), channel_id=1, source_target_pairs={{0,4},{4,0},{1,5},{5,1},{2,6},{6,2},{3,7},{7,3},{8,12},{12,8},{9,1... | collective-permute-start | bytes 294920 | tf_op jit(solution)/shard_map/ppermute | solution.py:461
  46.5 1.7 %collective-permute-done.19.came = bf16[96,512]{1,0:T(8,128)(2,1)S(1)} collective-permute-done((bf16[96,512]{1,0:T(8,128)(2,1)S(1)}, bf16[96,512]{1,0:T(8,128)(2,1)S(1)}, u32[]{:S(2)}, u32[]{:S(2)}) %collective-permute-start.19) | collective-permute-done | bytes 98336 | tf_op jit(solution)/shard_map/ppermute | solution.py:461
  50.3 3.1 %attention.6 = (bf16[48,512]{1,0:T(8,128)(2,1)S(1)}, bf16[48,512]{1,0:T(8,128)(2,1)S(1)}) custom-call(s32[3]{0:T(128)S(1)} %pad_add_fusion.1.which, f32[96,1024]{1,0:T(8,128)S(1)} %fusion.6.refs_0_.kept, bf16[96,512]{1,0:T(8,128)(2,1)S(1)} %collective-permute-done.19.came, f32[384,128]{1,0:T(8,128)S(1)} %get-tuple-element.50.cosines, ...), custom_call_target="tpu_custom_call" | custom-call | tf_op jit(solution)/shard_map/attention/pallas_call | solution.py:217
  54.1 3.1 %attention.4 = (bf16[48,512]{1,0:T(8,128)(2,1)S(1)}, bf16[48,512]{1,0:T(8,128)(2,1)S(1)}) custom-call(s32[3]{0:T(128)S(1)} %pad_add_fusion.1.which, f32[288,1024]{1,0:T(8,128)S(1)} %fusion.refs_0_.kept, bf16[288,512]{1,0:T(8,128)(2,1)S(1)} %collective-permute-done.5.came, f32[384,128]{1,0:T(8,128)S(1)} %get-tuple-element.50.cosines, ...), custom_call_target="tpu_custom_call" | custom-call | tf_op jit(solution)/shard_map/attention/pallas_call | solution.py:217
  57.2 1.5 %collective-permute-start.17 = (bf16[48,512]{1,0:T(8,128)(2,1)S(1)}, bf16[48,512]{1,0:T(8,128)(2,1)S(1)}, u32[]{:S(2)}, u32[]{:S(2)}) collective-permute-start(bf16[48,512]{1,0:T(8,128)(2,1)S(1)} %get-tuple-element.40), channel_id=1, source_target_pairs={{0,4},{4,0},{1,5},{5,1},{2,6},{6,2},{3,7},{7,3},{8,12},{12,8},{9,1... | collective-permute-start | bytes 147464 | tf_op jit(solution)/shard_map/ppermute | solution.py:461
  59.5 1.6 %convolution_convert_fusion.1 = bf16[48,4096]{1,0:T(8,128)(2,1)S(1)} fusion(bf16[48,1024]{1,0:T(8,128)(2,1)S(1)} %join.6, bf16[1024,4096]{1,0:T(8,128)(2,1)S(1)} %bitcast.28), kind=kOutput, calls=%fused_computation.1 | convolution fusion | flops 402849792 | bytes 8880128 | tf_op jit(solution)/shard_map/dot_general | solution.py:273
  61.0 3.0 %collective-permute-start.24 = (bf16[48,4096]{1,0:T(8,128)(2,1)S(1)}, bf16[48,4096]{1,0:T(8,128)(2,1)S(1)}, u32[]{:S(2)}, u32[]{:S(2)}) collective-permute-start(bf16[48,4096]{1,0:T(8,128)(2,1)S(1)} %convolution_convert_fusion.1), channel_id=1, source_target_pairs={{0,3},{1,2},{2,1},{3,0},{4,7},{5,6},{6,5},{7,4},{8,11},{9,10},{10,... | collective-permute-start | bytes 1179656 | tf_op jit(solution)/shard_map/ppermute | solution.py:461
  64.0 3.1 %attention.7 = (bf16[48,512]{1,0:T(8,128)(2,1)S(1)}, bf16[48,512]{1,0:T(8,128)(2,1)S(1)}) custom-call(s32[3]{0:T(128)S(1)} %pad_add_fusion.1.which, f32[288,1024]{1,0:T(8,128)S(1)} %fusion.refs_0_.kept, bf16[288,512]{1,0:T(8,128)(2,1)S(1)} %collective-permute-done.5.came, f32[384,128]{1,0:T(8,128)S(1)} %get-tuple-element.50.cosines, ...), custom_call_target="tpu_custom_call" | custom-call | tf_op jit(solution)/shard_map/attention/pallas_call | solution.py:217
  67.1 1.5 %collective-permute-start.21 = (bf16[48,512]{1,0:T(8,128)(2,1)S(1)}, bf16[48,512]{1,0:T(8,128)(2,1)S(1)}, u32[]{:S(2)}, u32[]{:S(2)}) collective-permute-start(bf16[48,512]{1,0:T(8,128)(2,1)S(1)} %get-tuple-element.48), channel_id=1, source_target_pairs={{0,4},{4,0},{1,5},{5,1},{2,6},{6,2},{3,7},{7,3},{8,12},{12,8},{9,1... | collective-permute-start | bytes 147464 | tf_op jit(solution)/shard_map/ppermute | solution.py:461
  69.2 1.6 %convolution_convert_fusion.2 = bf16[48,4096]{1,0:T(8,128)(2,1)S(1)} fusion(bf16[48,1024]{1,0:T(8,128)(2,1)S(1)} %join.4, bf16[1024,4096]{1,0:T(8,128)(2,1)S(1)} %bitcast.28), kind=kOutput, calls=%fused_computation.2 | convolution fusion | flops 402849792 | bytes 8880128 | tf_op jit(solution)/shard_map/dot_general | solution.py:273
  70.8 3.1 %attention.5 = (bf16[48,512]{1,0:T(8,128)(2,1)S(1)}, bf16[48,512]{1,0:T(8,128)(2,1)S(1)}) custom-call(s32[3]{0:T(128)S(1)} %pad_add_fusion.1.which, f32[288,1024]{1,0:T(8,128)S(1)} %fusion.refs_0_.kept, bf16[288,512]{1,0:T(8,128)(2,1)S(1)} %collective-permute-done.5.came, f32[384,128]{1,0:T(8,128)S(1)} %get-tuple-element.50.cosines, ...), custom_call_target="tpu_custom_call" | custom-call | tf_op jit(solution)/shard_map/attention/pallas_call | solution.py:217
  75.1 1.6 %convolution_convert_fusion = bf16[48,4096]{1,0:T(8,128)(2,1)S(1)} fusion(bf16[48,1024]{1,0:T(8,128)(2,1)S(1)} %join.7, bf16[1024,4096]{1,0:T(8,128)(2,1)S(1)} %bitcast.28), kind=kOutput, calls=%fused_computation | convolution fusion | flops 402849792 | bytes 8880128 | tf_op jit(solution)/shard_map/dot_general | solution.py:273
  76.7 1.5 %collective-permute-start.22 = (bf16[48,4096]{1,0:T(8,128)(2,1)S(1)}, bf16[48,4096]{1,0:T(8,128)(2,1)S(1)}, u32[]{:S(2)}, u32[]{:S(2)}) collective-permute-start(bf16[48,4096]{1,0:T(8,128)(2,1)S(1)} %convolution_convert_fusion), channel_id=1, source_target_pairs={{0,1},{1,0},{2,3},{3,2},{4,5},{5,4},{6,7},{7,6},{8,9},{9,8},{10,11... | collective-permute-start | bytes 1179656 | tf_op jit(solution)/shard_map/ppermute | solution.py:461
  78.8 1.6 %fusion.5 = f32[48,4096]{1,0:T(8,128)S(1)} fusion(bf16[48,1024]{1,0:T(8,128)(2,1)S(1)} %join.5, bf16[1024,4096]{1,0:T(8,128)(2,1)S(1)} %bitcast.28), kind=kOutput, calls=%fused_computation.13 | convolution fusion | flops 402653184 | bytes 9273344 | tf_op jit(solution)/shard_map/dot_general | solution.py:273
  80.4 15.1 %collective-permute-done.23 = bf16[48,4096]{1,0:T(8,128)(2,1)S(1)} collective-permute-done((bf16[48,4096]{1,0:T(8,128)(2,1)S(1)}, bf16[48,4096]{1,0:T(8,128)(2,1)S(1)}, u32[]{:S(2)}, u32[]{:S(2)}) %collective-permute-start.23) | collective-permute-done | bytes 393248 | tf_op jit(solution)/shard_map/ppermute | solution.py:461
  (79 shorter events, 24.3 us)
Async XLA Ops:
  2.1 18.2 %collective-permute-start.4 = (bf16[48,2048]{1,0:T(8,128)(2,1)S(1)}, bf16[48,2048]{1,0:T(8,128)(2,1)S(1)}, u32[]{:S(2)}, u32[]{:S(2)}) collective-permute-start(bf16[48,2048]{1,0:T(8,128)(2,1)S(1)} %get-tuple-element.31), channel_id=1, source_target_pairs={{0,6},{1,7},{2,4},{3,5},{4,2},{5,3},{6,0},{7,1},{8,14},{9,15},{10,... | collective-permute-start | bytes 589832 | tf_op jit(solution)/shard_map/ppermute | solution.py:465
  5.7 17.7 %collective-permute-start.3 = (bf16[48,2048]{1,0:T(8,128)(2,1)S(1)}, bf16[48,2048]{1,0:T(8,128)(2,1)S(1)}, u32[]{:S(2)}, u32[]{:S(2)}) collective-permute-start(bf16[48,2048]{1,0:T(8,128)(2,1)S(1)} %get-tuple-element.30.refs_0_), channel_id=1, source_target_pairs={{0,2},{1,3},{2,0},{3,1},{4,6},{5,7},{6,4},{7,5},{8,10},{9,11},{10,... | collective-permute-start | bytes 589832 | tf_op jit(solution)/shard_map/ppermute | solution.py:461
  6.1 17.4 %collective-permute-start.1 = (bf16[48,2048]{1,0:T(8,128)(2,1)S(1)}, bf16[48,2048]{1,0:T(8,128)(2,1)S(1)}, u32[]{:S(2)}, u32[]{:S(2)}) collective-permute-start(bf16[48,2048]{1,0:T(8,128)(2,1)S(1)} %get-tuple-element.30.refs_0_), channel_id=1, source_target_pairs={{0,1},{1,0},{2,3},{3,2},{4,5},{5,4},{6,7},{7,6},{8,9},{9,8},{10,11... | collective-permute-start | bytes 589832 | tf_op jit(solution)/shard_map/ppermute | solution.py:461
  7.6 16.1 %collective-permute-start.2 = (bf16[48,2048]{1,0:T(8,128)(2,1)S(1)}, bf16[48,2048]{1,0:T(8,128)(2,1)S(1)}, u32[]{:S(2)}, u32[]{:S(2)}) collective-permute-start(bf16[48,2048]{1,0:T(8,128)(2,1)S(1)} %get-tuple-element.31), channel_id=1, source_target_pairs={{0,5},{1,4},{2,7},{3,6},{4,1},{5,0},{6,3},{7,2},{8,13},{9,12},{10,... | collective-permute-start | bytes 589832 | tf_op jit(solution)/shard_map/ppermute | solution.py:465
  8.0 15.7 %collective-permute-start = (bf16[48,2048]{1,0:T(8,128)(2,1)S(1)}, bf16[48,2048]{1,0:T(8,128)(2,1)S(1)}, u32[]{:S(2)}, u32[]{:S(2)}) collective-permute-start(bf16[48,2048]{1,0:T(8,128)(2,1)S(1)} %get-tuple-element.31), channel_id=1, source_target_pairs={{0,4},{4,0},{1,5},{5,1},{2,6},{6,2},{3,7},{7,3},{8,12},{12,8},{9,1... | collective-permute-start | bytes 589832 | tf_op jit(solution)/shard_map/ppermute | solution.py:461
  20.3 11.3 %collective-permute-start.6 = (s32[2,192]{1,0:T(2,128)S(1)}, s32[2,192]{1,0:T(2,128)S(1)}, u32[]{:S(2)}, u32[]{:S(2)}) collective-permute-start(s32[2,192]{1,0:T(2,128)S(1)} %pad_add_fusion.here), channel_id=1, source_target_pairs={{0,4},{4,0},{1,5},{5,1},{2,6},{6,2},{3,7},{7,3},{8,12},{12,8},{9,1... | collective-permute-start | bytes 4616 | tf_op jit(solution)/shard_map/ppermute | solution.py:461
  25.4 9.5 %collective-permute-start.7 = (f32[288,256]{1,0:T(8,128)S(1)}, f32[288,256]{1,0:T(8,128)S(1)}, u32[]{:S(2)}, u32[]{:S(2)}) collective-permute-start(f32[288,256]{1,0:T(8,128)S(1)} %sent.5), channel_id=1, source_target_pairs={{0,4},{4,0},{1,5},{5,1},{2,6},{6,2},{3,7},{7,3},{8,12},{12,8},{9,1... | collective-permute-start | bytes 884744 | tf_op jit(solution)/shard_map/ppermute | solution.py:461
  26.9 8.5 %collective-permute-start.11 = (bf16[96,2048]{1,0:T(8,128)(2,1)S(1)}, bf16[96,2048]{1,0:T(8,128)(2,1)S(1)}, u32[]{:S(2)}, u32[]{:S(2)}) collective-permute-start(bf16[96,2048]{1,0:T(8,128)(2,1)S(1)} %get-tuple-element.37), channel_id=1, source_target_pairs={{1,2},{2,1},{5,6},{6,5},{9,10},{10,9},{13,14},{14,13},{17,18},{18,... | collective-permute-start | bytes 1179656 | tf_op jit(solution)/shard_map/ppermute | solution.py:461
  27.7 12.0 %collective-permute-start.12 = (bf16[96,2048]{1,0:T(8,128)(2,1)S(1)}, bf16[96,2048]{1,0:T(8,128)(2,1)S(1)}, u32[]{:S(2)}, u32[]{:S(2)}) collective-permute-start(bf16[96,2048]{1,0:T(8,128)(2,1)S(1)} %get-tuple-element.38), channel_id=1, source_target_pairs={{1,0},{2,3},{5,4},{6,7},{9,8},{10,11},{13,12},{14,15},{17,16},{18,... | collective-permute-start | bytes 1179656 | tf_op jit(solution)/shard_map/ppermute | solution.py:461
  31.0 23.1 %collective-permute-start.5 = (bf16[288,512]{1,0:T(8,128)(2,1)S(1)}, bf16[288,512]{1,0:T(8,128)(2,1)S(1)}, u32[]{:S(2)}, u32[]{:S(2)}) collective-permute-start(bf16[288,512]{1,0:T(8,128)(2,1)S(1)} %sent.4), channel_id=1, source_target_pairs={{0,4},{4,0},{1,5},{5,1},{2,6},{6,2},{3,7},{7,3},{8,12},{12,8},{9,1... | collective-permute-start | bytes 884744 | tf_op jit(solution)/shard_map/ppermute | solution.py:461
  35.1 6.4 %collective-permute-start.9 = (bf16[304,256]{1,0:T(8,128)(2,1)S(1)}, bf16[304,256]{1,0:T(8,128)(2,1)S(1)}, u32[]{:S(2)}, u32[]{:S(2)}) collective-permute-start(bf16[304,256]{1,0:T(8,128)(2,1)S(1)} %pair.2.refs_0_), channel_id=1, source_target_pairs={{0,16},{8,24},{16,0},{24,8},{1,17},{9,25},{17,1},{25,9},{2,18},{10... | collective-permute-start | bytes 466952 | tf_op jit(solution)/shard_map/ppermute | solution.py:461
  35.4 10.4 %collective-permute-start.8 = (bf16[304,256]{1,0:T(8,128)(2,1)S(1)}, bf16[304,256]{1,0:T(8,128)(2,1)S(1)}, u32[]{:S(2)}, u32[]{:S(2)}) collective-permute-start(bf16[304,256]{1,0:T(8,128)(2,1)S(1)} %pair.2.refs_0_), channel_id=1, source_target_pairs={{0,8},{8,0},{16,24},{24,16},{1,9},{9,1},{17,25},{25,17},{2,10},{10... | collective-permute-start | bytes 466952 | tf_op jit(solution)/shard_map/ppermute | solution.py:461
  40.9 4.7 %collective-permute-start.13 = (f32[96,256]{1,0:T(8,128)S(1)}, f32[96,256]{1,0:T(8,128)S(1)}, u32[]{:S(2)}, u32[]{:S(2)}) collective-permute-start(f32[96,256]{1,0:T(8,128)S(1)} %sent.6), channel_id=1, source_target_pairs={{0,4},{4,0},{1,5},{5,1},{2,6},{6,2},{3,7},{7,3},{8,12},{12,8},{9,1... | collective-permute-start | bytes 294920 | tf_op jit(solution)/shard_map/ppermute | solution.py:461
  41.5 8.8 %collective-permute-start.10 = (bf16[304,256]{1,0:T(8,128)(2,1)S(1)}, bf16[304,256]{1,0:T(8,128)(2,1)S(1)}, u32[]{:S(2)}, u32[]{:S(2)}) collective-permute-start(bf16[304,256]{1,0:T(8,128)(2,1)S(1)} %collective-permute-done.9.refs_2_), channel_id=1, source_target_pairs={{0,8},{8,0},{16,24},{24,16},{1,9},{9,1},{17,25},{25,17},{2,10},{10... | collective-permute-start | bytes 466952 | tf_op jit(solution)/shard_map/ppermute | solution.py:461
  42.9 5.3 %collective-permute-start.19 = (bf16[96,512]{1,0:T(8,128)(2,1)S(1)}, bf16[96,512]{1,0:T(8,128)(2,1)S(1)}, u32[]{:S(2)}, u32[]{:S(2)}) collective-permute-start(bf16[96,512]{1,0:T(8,128)(2,1)S(1)} %sent.7), channel_id=1, source_target_pairs={{0,4},{4,0},{1,5},{5,1},{2,6},{6,2},{3,7},{7,3},{8,12},{12,8},{9,1... | collective-permute-start | bytes 294920 | tf_op jit(solution)/shard_map/ppermute | solution.py:461
  45.7 3.6 %collective-permute-start.16 = (bf16[96,256]{1,0:T(8,128)(2,1)S(1)}, bf16[96,256]{1,0:T(8,128)(2,1)S(1)}, u32[]{:S(2)}, u32[]{:S(2)}) collective-permute-start(bf16[96,256]{1,0:T(8,128)(2,1)S(1)} %pair.3.refs_4_), channel_id=1, source_target_pairs={{0,24},{8,16},{16,8},{24,0},{1,25},{9,17},{17,9},{25,1},{2,26},{10... | collective-permute-start | bytes 147464 | tf_op jit(solution)/shard_map/ppermute | solution.py:461
  45.8 4.5 %collective-permute-start.15 = (bf16[96,256]{1,0:T(8,128)(2,1)S(1)}, bf16[96,256]{1,0:T(8,128)(2,1)S(1)}, u32[]{:S(2)}, u32[]{:S(2)}) collective-permute-start(bf16[96,256]{1,0:T(8,128)(2,1)S(1)} %pair.3.refs_4_), channel_id=1, source_target_pairs={{0,16},{8,24},{16,0},{24,8},{1,17},{9,25},{17,1},{25,9},{2,18},{10... | collective-permute-start | bytes 147464 | tf_op jit(solution)/shard_map/ppermute | solution.py:461
  53.4 5.3 %collective-permute-start.20 = (bf16[48,512]{1,0:T(8,128)(2,1)S(1)}, bf16[48,512]{1,0:T(8,128)(2,1)S(1)}, u32[]{:S(2)}, u32[]{:S(2)}) collective-permute-start(bf16[48,512]{1,0:T(8,128)(2,1)S(1)} %get-tuple-element.45), channel_id=1, source_target_pairs={{0,4},{4,0},{1,5},{5,1},{2,6},{6,2},{3,7},{7,3},{8,12},{12,8},{9,1... | collective-permute-start | bytes 147464 | tf_op jit(solution)/shard_map/ppermute | solution.py:461
  57.2 11.4 %collective-permute-start.17 = (bf16[48,512]{1,0:T(8,128)(2,1)S(1)}, bf16[48,512]{1,0:T(8,128)(2,1)S(1)}, u32[]{:S(2)}, u32[]{:S(2)}) collective-permute-start(bf16[48,512]{1,0:T(8,128)(2,1)S(1)} %get-tuple-element.40), channel_id=1, source_target_pairs={{0,4},{4,0},{1,5},{5,1},{2,6},{6,2},{3,7},{7,3},{8,12},{12,8},{9,1... | collective-permute-start | bytes 147464 | tf_op jit(solution)/shard_map/ppermute | solution.py:461
  61.0 34.5 %collective-permute-start.24 = (bf16[48,4096]{1,0:T(8,128)(2,1)S(1)}, bf16[48,4096]{1,0:T(8,128)(2,1)S(1)}, u32[]{:S(2)}, u32[]{:S(2)}) collective-permute-start(bf16[48,4096]{1,0:T(8,128)(2,1)S(1)} %convolution_convert_fusion.1), channel_id=1, source_target_pairs={{0,3},{1,2},{2,1},{3,0},{4,7},{5,6},{6,5},{7,4},{8,11},{9,10},{10,... | collective-permute-start | bytes 1179656 | tf_op jit(solution)/shard_map/ppermute | solution.py:461
  67.1 7.5 %collective-permute-start.21 = (bf16[48,512]{1,0:T(8,128)(2,1)S(1)}, bf16[48,512]{1,0:T(8,128)(2,1)S(1)}, u32[]{:S(2)}, u32[]{:S(2)}) collective-permute-start(bf16[48,512]{1,0:T(8,128)(2,1)S(1)} %get-tuple-element.48), channel_id=1, source_target_pairs={{0,4},{4,0},{1,5},{5,1},{2,6},{6,2},{3,7},{7,3},{8,12},{12,8},{9,1... | collective-permute-start | bytes 147464 | tf_op jit(solution)/shard_map/ppermute | solution.py:461
  70.7 24.8 %collective-permute-start.23 = (bf16[48,4096]{1,0:T(8,128)(2,1)S(1)}, bf16[48,4096]{1,0:T(8,128)(2,1)S(1)}, u32[]{:S(2)}, u32[]{:S(2)}) collective-permute-start(bf16[48,4096]{1,0:T(8,128)(2,1)S(1)} %convolution_convert_fusion.2), channel_id=1, source_target_pairs={{0,2},{1,3},{2,0},{3,1},{4,6},{5,7},{6,4},{7,5},{8,10},{9,11},{10,... | collective-permute-start | bytes 1179656 | tf_op jit(solution)/shard_map/ppermute | solution.py:461
  73.9 4.3 %collective-permute-start.18 = (bf16[48,512]{1,0:T(8,128)(2,1)S(1)}, bf16[48,512]{1,0:T(8,128)(2,1)S(1)}, u32[]{:S(2)}, u32[]{:S(2)}) collective-permute-start(bf16[48,512]{1,0:T(8,128)(2,1)S(1)} %get-tuple-element.43), channel_id=1, source_target_pairs={{0,4},{4,0},{1,5},{5,1},{2,6},{6,2},{3,7},{7,3},{8,12},{12,8},{9,1... | collective-permute-start | bytes 147464 | tf_op jit(solution)/shard_map/ppermute | solution.py:461
  76.7 18.8 %collective-permute-start.22 = (bf16[48,4096]{1,0:T(8,128)(2,1)S(1)}, bf16[48,4096]{1,0:T(8,128)(2,1)S(1)}, u32[]{:S(2)}, u32[]{:S(2)}) collective-permute-start(bf16[48,4096]{1,0:T(8,128)(2,1)S(1)} %convolution_convert_fusion), channel_id=1, source_target_pairs={{0,1},{1,0},{2,3},{3,2},{4,5},{5,4},{6,7},{7,6},{8,9},{9,8},{10,11... | collective-permute-start | bytes 1179656 | tf_op jit(solution)/shard_map/ppermute | solution.py:461
  (11 other events, 119.3 us)

commit v8 on v7

--- a/solution.py
+++ b/solution.py
@@ -401,14 +401,15 @@
         return jnp.concatenate([lines[0:1, :], lines[1:2, :rest]], axis=1)
 
     def block_scores(block):
-        scores = lax.dot_general(
-            stacked, joined(block, 0), (((1,), (1,)), ((), ())), preferred_element_type=jnp.float32
-        )
         allowed = key_document(block) == document
         if block == 0:
             allowed = allowed & (key_place <= row_place)
-        scores = scores.reshape(heads, tokens, -1) * score_scale
-        return jnp.where(allowed[None], scores, masked_score).reshape(heads * tokens, -1)
+        barred = jnp.where(allowed, 0.0, masked_score)
+        scores = lax.dot_general(
+            stacked, joined(block, 0), (((1,), (1,)), ((), ())), preferred_element_type=jnp.float32
+        )
+        scores = scores.reshape(heads, tokens, -1) * score_scale + barred[None]
+        return scores.reshape(heads * tokens, -1)
 
     def weighted(block, weights):
         return product(weights.astype(jnp.bfloat16), joined(block, HEAD_SIZE))
@@ -547,7 +548,8 @@
             [((out_rows, 2 * HEAD_SIZE), bf16, None)],
         )[0]
 
-    early_stacked, own_rows, two_rows = stack("early_rows", early, (3, 1, 1))
+    early_stacked, unused_rows, two_rows = stack("early_rows", early, (3, 1, 1))
+    own_rows = stack("own_rows", [[after(mine, one_mine)], [theirs]], (1,))[0]
     middle_rows = send(own_rows, "tensor", middle)
     ends_rows = send(two_rows, "tensor", [(1, 0), (2, 3)])
     early_projected = project_pair(early_stacked)

time: 98.3 us -> 97.1 us (0.988)
  waiting for transfers between devices: 38.1 us -> 34.2 us
  starting transfers between devices: 25.2 us -> 26.8 us
    ppermute x2, waiting for transfers between devices: 10.3 us -> 7.78 us  [send_across(): return lax.ppermute(value, ('inner', 'tensor'), both)]
    ppermute x23, waiting for transfers between devices: 27.7 us -> 26.4 us  [send(): return lax.ppermute(value, axis, pairs)]
    ppermute x2, starting transfers between devices: 4 us -> 5.01 us  [send_across(): return lax.ppermute(value, ('inner', 'tensor'), both)]
    pallas_call x18 -> x19, Pallas kernels: 18.5 us -> 19.4 us  [call_kernel(): pl.pallas_call(kernel, name=name, grid_spec=pltpu.PrefetchScalarGridSpec(...]
  transfers between devices with their start and end apart: 25 -> 25, of which waited for: 10 -> 10; matrix products, arithmetic and copies ran while one was open for 12% -> 12% of each run, Pallas kernels for 19% -> 20%
where the time goes in v8:
time: 97.1 us; the launch traced here: 95.2 us
  waiting for transfers between devices  34.2 us (35%)
  starting transfers between devices  26.8 us (28%)
  Pallas kernels  19.4 us (20%)
  matrix products  10.1 us (10%)
  other arithmetic  2.46 us (3%)
  local copies, waits for them, and re-layouts  1.82 us (2%)
    ppermute x23, waiting for transfers between devices, send(): return lax.ppermute(value, axis, pairs)  26.4 us
    ppermute x23, starting transfers between devices, send(): return lax.ppermute(value, axis, pairs)  21.8 us
    pallas_call x19, Pallas kernels, call_kernel(): pl.pallas_call(kernel, name=name, grid_spec=pltpu.PrefetchScalarGridSpec(...  19.4 us
    dot_general x10, matrix products, product(): return jnp.dot(left, right, preferred_element_type=jnp.float32)  10.1 us
    ppermute x2, waiting for transfers between devices, send_across(): return lax.ppermute(value, ('inner', 'tensor'), both)  7.78 us
    ppermute x2, starting transfers between devices, send_across(): return lax.ppermute(value, ('inner', 'tensor'), both)  5.01 us
  transfers between devices with their start and end apart: 25, of which 10 were waited for; matrix products, arithmetic and copies ran while one was open for 12% of the time, Pallas kernels for 20%

profile of v8, /device:TPU:2, one launch (start us, length us, event | category | flops | bytes accessed | tf_op | source)
XLA Modules:
  0.0 95.2 jit_solution(5526886530353040069)
XLA Ops:
  2.1 3.6 %collective-permute-start.4 = (bf16[48,2048]{1,0:T(8,128)(2,1)S(1)}, bf16[48,2048]{1,0:T(8,128)(2,1)S(1)}, u32[]{:S(2)}, u32[]{:S(2)}) collective-permute-start(bf16[48,2048]{1,0:T(8,128)(2,1)S(1)} %get-tuple-element.31), channel_id=1, source_target_pairs={{0,6},{1,7},{2,4},{3,5},{4,2},{5,3},{6,0},{7,1},{8,14},{9,15},{10,... | collective-permute-start | bytes 589832 | tf_op jit(solution)/shard_map/ppermute | solution.py:466
  5.7 1.6 %collective-permute-start.1 = (bf16[48,2048]{1,0:T(8,128)(2,1)S(1)}, bf16[48,2048]{1,0:T(8,128)(2,1)S(1)}, u32[]{:S(2)}, u32[]{:S(2)}) collective-permute-start(bf16[48,2048]{1,0:T(8,128)(2,1)S(1)} %get-tuple-element.37.refs_0_), channel_id=1, source_target_pairs={{0,1},{1,0},{2,3},{3,2},{4,5},{5,4},{6,7},{7,6},{8,9},{9,8},{10,11... | collective-permute-start | bytes 589832 | tf_op jit(solution)/shard_map/ppermute | solution.py:462
  10.2 5.8 %collective-permute-done.4.refs_5_ = bf16[48,2048]{1,0:T(8,128)(2,1)S(1)} collective-permute-done((bf16[48,2048]{1,0:T(8,128)(2,1)S(1)}, bf16[48,2048]{1,0:T(8,128)(2,1)S(1)}, u32[]{:S(2)}, u32[]{:S(2)}) %collective-permute-start.4) | collective-permute-done | bytes 196640 | tf_op jit(solution)/shard_map/ppermute | solution.py:466
  16.1 1.5 %collective-permute-start.6 = (s32[2,192]{1,0:T(2,128)S(1)}, s32[2,192]{1,0:T(2,128)S(1)}, u32[]{:S(2)}, u32[]{:S(2)}) collective-permute-start(s32[2,192]{1,0:T(2,128)S(1)} %pad_add_fusion.here), channel_id=1, source_target_pairs={{0,4},{4,0},{1,5},{5,1},{2,6},{6,2},{3,7},{7,3},{8,12},{12,8},{9,1... | collective-permute-start | bytes 4616 | tf_op jit(solution)/shard_map/ppermute | solution.py:462
  17.6 3.3 %collective-permute-done.1.refs_2_ = bf16[48,2048]{1,0:T(8,128)(2,1)S(1)} collective-permute-done((bf16[48,2048]{1,0:T(8,128)(2,1)S(1)}, bf16[48,2048]{1,0:T(8,128)(2,1)S(1)}, u32[]{:S(2)}, u32[]{:S(2)}) %collective-permute-start.1) | collective-permute-done | bytes 196640 | tf_op jit(solution)/shard_map/ppermute | solution.py:462
  21.6 2.0 %collective-permute-done.2.refs_3_ = bf16[48,2048]{1,0:T(8,128)(2,1)S(1)} collective-permute-done((bf16[48,2048]{1,0:T(8,128)(2,1)S(1)}, bf16[48,2048]{1,0:T(8,128)(2,1)S(1)}, u32[]{:S(2)}, u32[]{:S(2)}) %collective-permute-start.2) | collective-permute-done | bytes 196640 | tf_op jit(solution)/shard_map/ppermute | solution.py:466
  26.0 1.6 %collective-permute-start.7 = (f32[288,256]{1,0:T(8,128)S(1)}, f32[288,256]{1,0:T(8,128)S(1)}, u32[]{:S(2)}, u32[]{:S(2)}) collective-permute-start(f32[288,256]{1,0:T(8,128)S(1)} %sent.5), channel_id=1, source_target_pairs={{0,4},{4,0},{1,5},{5,1},{2,6},{6,2},{3,7},{7,3},{8,12},{12,8},{9,1... | collective-permute-start | bytes 884744 | tf_op jit(solution)/shard_map/ppermute | solution.py:462
  27.6 1.4 %collective-permute-start.12 = (bf16[96,2048]{1,0:T(8,128)(2,1)S(1)}, bf16[96,2048]{1,0:T(8,128)(2,1)S(1)}, u32[]{:S(2)}, u32[]{:S(2)}) collective-permute-start(bf16[96,2048]{1,0:T(8,128)(2,1)S(1)} %get-tuple-element.38), channel_id=1, source_target_pairs={{1,0},{2,3},{5,4},{6,7},{9,8},{10,11},{13,12},{14,15},{17,16},{18,... | collective-permute-start | bytes 1179656 | tf_op jit(solution)/shard_map/ppermute | solution.py:462
  29.0 1.4 %fusion.refs_0_.kept = f32[288,1024]{1,0:T(8,128)S(1)} fusion(bf16[288,2048]{1,0:T(8,128)(2,1)S(1)} %get-tuple-element.32, bf16[2048,1024]{1,0:T(8,128)(2,1)S(1)} %copy-done.5), kind=kOutput, calls=%fused_computation.8 | convolution fusion | flops 1207959552 | bytes 6553600 | tf_op jit(solution)/shard_map/dot_general | solution.py:273
  33.2 1.9 %collective-permute-done.7.came = f32[288,256]{1,0:T(8,128)S(1)} collective-permute-done((f32[288,256]{1,0:T(8,128)S(1)}, f32[288,256]{1,0:T(8,128)S(1)}, u32[]{:S(2)}, u32[]{:S(2)}) %collective-permute-start.7) | collective-permute-done | bytes 294944 | tf_op jit(solution)/shard_map/ppermute | solution.py:462
  35.9 3.1 %collective-permute-done.12.refs_1_ = bf16[96,2048]{1,0:T(8,128)(2,1)S(1)} collective-permute-done((bf16[96,2048]{1,0:T(8,128)(2,1)S(1)}, bf16[96,2048]{1,0:T(8,128)(2,1)S(1)}, u32[]{:S(2)}, u32[]{:S(2)}) %collective-permute-start.12) | collective-permute-done | bytes 393248 | tf_op jit(solution)/shard_map/ppermute | solution.py:462
  42.2 2.2 %collective-permute-start.19 = (bf16[96,512]{1,0:T(8,128)(2,1)S(1)}, bf16[96,512]{1,0:T(8,128)(2,1)S(1)}, u32[]{:S(2)}, u32[]{:S(2)}) collective-permute-start(bf16[96,512]{1,0:T(8,128)(2,1)S(1)} %sent.7), channel_id=1, source_target_pairs={{0,4},{4,0},{1,5},{5,1},{2,6},{6,2},{3,7},{7,3},{8,12},{12,8},{9,1... | collective-permute-start | bytes 294920 | tf_op jit(solution)/shard_map/ppermute | solution.py:462
  46.4 1.4 %collective-permute-done.19.came = bf16[96,512]{1,0:T(8,128)(2,1)S(1)} collective-permute-done((bf16[96,512]{1,0:T(8,128)(2,1)S(1)}, bf16[96,512]{1,0:T(8,128)(2,1)S(1)}, u32[]{:S(2)}, u32[]{:S(2)}) %collective-permute-start.19) | collective-permute-done | bytes 98336 | tf_op jit(solution)/shard_map/ppermute | solution.py:462
  50.0 3.1 %attention.6 = (bf16[48,512]{1,0:T(8,128)(2,1)S(1)}, bf16[48,512]{1,0:T(8,128)(2,1)S(1)}) custom-call(s32[3]{0:T(128)S(1)} %pad_add_fusion.1.which, f32[96,1024]{1,0:T(8,128)S(1)} %fusion.6.refs_0_.kept, bf16[96,512]{1,0:T(8,128)(2,1)S(1)} %collective-permute-done.19.came, f32[384,128]{1,0:T(8,128)S(1)} %get-tuple-element.50.cosines, ...), custom_call_target="tpu_custom_call" | custom-call | tf_op jit(solution)/shard_map/attention/pallas_call | solution.py:217
  54.0 3.1 %attention.4 = (bf16[48,512]{1,0:T(8,128)(2,1)S(1)}, bf16[48,512]{1,0:T(8,128)(2,1)S(1)}) custom-call(s32[3]{0:T(128)S(1)} %pad_add_fusion.1.which, f32[288,1024]{1,0:T(8,128)S(1)} %fusion.refs_0_.kept, bf16[288,512]{1,0:T(8,128)(2,1)S(1)} %collective-permute-done.5.came, f32[384,128]{1,0:T(8,128)S(1)} %get-tuple-element.50.cosines, ...), custom_call_target="tpu_custom_call" | custom-call | tf_op jit(solution)/shard_map/attention/pallas_call | solution.py:217
  59.1 1.6 %convolution_convert_fusion.1 = bf16[48,4096]{1,0:T(8,128)(2,1)S(1)} fusion(bf16[48,1024]{1,0:T(8,128)(2,1)S(1)} %join.6, bf16[1024,4096]{1,0:T(8,128)(2,1)S(1)} %bitcast.28), kind=kOutput, calls=%fused_computation.1 | convolution fusion | flops 402849792 | bytes 8880128 | tf_op jit(solution)/shard_map/dot_general | solution.py:273
  60.7 2.5 %collective-permute-start.24 = (bf16[48,4096]{1,0:T(8,128)(2,1)S(1)}, bf16[48,4096]{1,0:T(8,128)(2,1)S(1)}, u32[]{:S(2)}, u32[]{:S(2)}) collective-permute-start(bf16[48,4096]{1,0:T(8,128)(2,1)S(1)} %convolution_convert_fusion.1), channel_id=1, source_target_pairs={{0,3},{1,2},{2,1},{3,0},{4,7},{5,6},{6,5},{7,4},{8,11},{9,10},{10,... | collective-permute-start | bytes 1179656 | tf_op jit(solution)/shard_map/ppermute | solution.py:462
  63.2 3.1 %attention.7 = (bf16[48,512]{1,0:T(8,128)(2,1)S(1)}, bf16[48,512]{1,0:T(8,128)(2,1)S(1)}) custom-call(s32[3]{0:T(128)S(1)} %pad_add_fusion.1.which, f32[288,1024]{1,0:T(8,128)S(1)} %fusion.refs_0_.kept, bf16[288,512]{1,0:T(8,128)(2,1)S(1)} %collective-permute-done.5.came, f32[384,128]{1,0:T(8,128)S(1)} %get-tuple-element.50.cosines, ...), custom_call_target="tpu_custom_call" | custom-call | tf_op jit(solution)/shard_map/attention/pallas_call | solution.py:217
  67.9 1.6 %convolution_convert_fusion.2 = bf16[48,4096]{1,0:T(8,128)(2,1)S(1)} fusion(bf16[48,1024]{1,0:T(8,128)(2,1)S(1)} %join.4, bf16[1024,4096]{1,0:T(8,128)(2,1)S(1)} %bitcast.28), kind=kOutput, calls=%fused_computation.2 | convolution fusion | flops 402849792 | bytes 8880128 | tf_op jit(solution)/shard_map/dot_general | solution.py:273
  69.5 3.1 %attention.5 = (bf16[48,512]{1,0:T(8,128)(2,1)S(1)}, bf16[48,512]{1,0:T(8,128)(2,1)S(1)}) custom-call(s32[3]{0:T(128)S(1)} %pad_add_fusion.1.which, f32[288,1024]{1,0:T(8,128)S(1)} %fusion.refs_0_.kept, bf16[288,512]{1,0:T(8,128)(2,1)S(1)} %collective-permute-done.5.came, f32[384,128]{1,0:T(8,128)S(1)} %get-tuple-element.50.cosines, ...), custom_call_target="tpu_custom_call" | custom-call | tf_op jit(solution)/shard_map/attention/pallas_call | solution.py:217
  74.4 1.6 %convolution_convert_fusion = bf16[48,4096]{1,0:T(8,128)(2,1)S(1)} fusion(bf16[48,1024]{1,0:T(8,128)(2,1)S(1)} %join.7, bf16[1024,4096]{1,0:T(8,128)(2,1)S(1)} %bitcast.28), kind=kOutput, calls=%fused_computation | convolution fusion | flops 402849792 | bytes 8880128 | tf_op jit(solution)/shard_map/dot_general | solution.py:273
  76.0 2.0 %collective-permute-start.22 = (bf16[48,4096]{1,0:T(8,128)(2,1)S(1)}, bf16[48,4096]{1,0:T(8,128)(2,1)S(1)}, u32[]{:S(2)}, u32[]{:S(2)}) collective-permute-start(bf16[48,4096]{1,0:T(8,128)(2,1)S(1)} %convolution_convert_fusion), channel_id=1, source_target_pairs={{0,1},{1,0},{2,3},{3,2},{4,5},{5,4},{6,7},{7,6},{8,9},{9,8},{10,11... | collective-permute-start | bytes 1179656 | tf_op jit(solution)/shard_map/ppermute | solution.py:462
  78.6 1.6 %fusion.5 = f32[48,4096]{1,0:T(8,128)S(1)} fusion(bf16[48,1024]{1,0:T(8,128)(2,1)S(1)} %join.5, bf16[1024,4096]{1,0:T(8,128)(2,1)S(1)} %bitcast.28), kind=kOutput, calls=%fused_computation.13 | convolution fusion | flops 402653184 | bytes 9273344 | tf_op jit(solution)/shard_map/dot_general | solution.py:273
  80.1 14.0 %collective-permute-done.23 = bf16[48,4096]{1,0:T(8,128)(2,1)S(1)} collective-permute-done((bf16[48,4096]{1,0:T(8,128)(2,1)S(1)}, bf16[48,4096]{1,0:T(8,128)(2,1)S(1)}, u32[]{:S(2)}, u32[]{:S(2)}) %collective-permute-start.23) | collective-permute-done | bytes 393248 | tf_op jit(solution)/shard_map/ppermute | solution.py:462
  (80 shorter events, 26.8 us)
Async XLA Ops:
  2.1 13.9 %collective-permute-start.4 = (bf16[48,2048]{1,0:T(8,128)(2,1)S(1)}, bf16[48,2048]{1,0:T(8,128)(2,1)S(1)}, u32[]{:S(2)}, u32[]{:S(2)}) collective-permute-start(bf16[48,2048]{1,0:T(8,128)(2,1)S(1)} %get-tuple-element.31), channel_id=1, source_target_pairs={{0,6},{1,7},{2,4},{3,5},{4,2},{5,3},{6,0},{7,1},{8,14},{9,15},{10,... | collective-permute-start | bytes 589832 | tf_op jit(solution)/shard_map/ppermute | solution.py:466
  5.7 15.1 %collective-permute-start.1 = (bf16[48,2048]{1,0:T(8,128)(2,1)S(1)}, bf16[48,2048]{1,0:T(8,128)(2,1)S(1)}, u32[]{:S(2)}, u32[]{:S(2)}) collective-permute-start(bf16[48,2048]{1,0:T(8,128)(2,1)S(1)} %get-tuple-element.37.refs_0_), channel_id=1, source_target_pairs={{0,1},{1,0},{2,3},{3,2},{4,5},{5,4},{6,7},{7,6},{8,9},{9,8},{10,11... | collective-permute-start | bytes 589832 | tf_op jit(solution)/shard_map/ppermute | solution.py:462
  7.3 13.6 %collective-permute-start = (bf16[48,2048]{1,0:T(8,128)(2,1)S(1)}, bf16[48,2048]{1,0:T(8,128)(2,1)S(1)}, u32[]{:S(2)}, u32[]{:S(2)}) collective-permute-start(bf16[48,2048]{1,0:T(8,128)(2,1)S(1)} %get-tuple-element.31), channel_id=1, source_target_pairs={{0,4},{4,0},{1,5},{5,1},{2,6},{6,2},{3,7},{7,3},{8,12},{12,8},{9,1... | collective-permute-start | bytes 589832 | tf_op jit(solution)/shard_map/ppermute | solution.py:462
  7.8 15.7 %collective-permute-start.2 = (bf16[48,2048]{1,0:T(8,128)(2,1)S(1)}, bf16[48,2048]{1,0:T(8,128)(2,1)S(1)}, u32[]{:S(2)}, u32[]{:S(2)}) collective-permute-start(bf16[48,2048]{1,0:T(8,128)(2,1)S(1)} %get-tuple-element.31), channel_id=1, source_target_pairs={{0,5},{1,4},{2,7},{3,6},{4,1},{5,0},{6,3},{7,2},{8,13},{9,12},{10,... | collective-permute-start | bytes 589832 | tf_op jit(solution)/shard_map/ppermute | solution.py:466
  9.2 14.3 %collective-permute-start.3 = (bf16[48,2048]{1,0:T(8,128)(2,1)S(1)}, bf16[48,2048]{1,0:T(8,128)(2,1)S(1)}, u32[]{:S(2)}, u32[]{:S(2)}) collective-permute-start(bf16[48,2048]{1,0:T(8,128)(2,1)S(1)} %get-tuple-element.37.refs_0_), channel_id=1, source_target_pairs={{0,2},{1,3},{2,0},{3,1},{4,6},{5,7},{6,4},{7,5},{8,10},{9,11},{10,... | collective-permute-start | bytes 589832 | tf_op jit(solution)/shard_map/ppermute | solution.py:462
  16.1 15.5 %collective-permute-start.6 = (s32[2,192]{1,0:T(2,128)S(1)}, s32[2,192]{1,0:T(2,128)S(1)}, u32[]{:S(2)}, u32[]{:S(2)}) collective-permute-start(s32[2,192]{1,0:T(2,128)S(1)} %pad_add_fusion.here), channel_id=1, source_target_pairs={{0,4},{4,0},{1,5},{5,1},{2,6},{6,2},{3,7},{7,3},{8,12},{12,8},{9,1... | collective-permute-start | bytes 4616 | tf_op jit(solution)/shard_map/ppermute | solution.py:462
  20.9 15.0 %collective-permute-start.11 = (bf16[96,2048]{1,0:T(8,128)(2,1)S(1)}, bf16[96,2048]{1,0:T(8,128)(2,1)S(1)}, u32[]{:S(2)}, u32[]{:S(2)}) collective-permute-start(bf16[96,2048]{1,0:T(8,128)(2,1)S(1)} %own_rows.1), channel_id=1, source_target_pairs={{1,2},{2,1},{5,6},{6,5},{9,10},{10,9},{13,14},{14,13},{17,18},{18,... | collective-permute-start | bytes 1179656 | tf_op jit(solution)/shard_map/ppermute | solution.py:462
  26.0 9.1 %collective-permute-start.7 = (f32[288,256]{1,0:T(8,128)S(1)}, f32[288,256]{1,0:T(8,128)S(1)}, u32[]{:S(2)}, u32[]{:S(2)}) collective-permute-start(f32[288,256]{1,0:T(8,128)S(1)} %sent.5), channel_id=1, source_target_pairs={{0,4},{4,0},{1,5},{5,1},{2,6},{6,2},{3,7},{7,3},{8,12},{12,8},{9,1... | collective-permute-start | bytes 884744 | tf_op jit(solution)/shard_map/ppermute | solution.py:462
  27.6 11.4 %collective-permute-start.12 = (bf16[96,2048]{1,0:T(8,128)(2,1)S(1)}, bf16[96,2048]{1,0:T(8,128)(2,1)S(1)}, u32[]{:S(2)}, u32[]{:S(2)}) collective-permute-start(bf16[96,2048]{1,0:T(8,128)(2,1)S(1)} %get-tuple-element.38), channel_id=1, source_target_pairs={{1,0},{2,3},{5,4},{6,7},{9,8},{10,11},{13,12},{14,15},{17,16},{18,... | collective-permute-start | bytes 1179656 | tf_op jit(solution)/shard_map/ppermute | solution.py:462
  31.0 23.0 %collective-permute-start.5 = (bf16[288,512]{1,0:T(8,128)(2,1)S(1)}, bf16[288,512]{1,0:T(8,128)(2,1)S(1)}, u32[]{:S(2)}, u32[]{:S(2)}) collective-permute-start(bf16[288,512]{1,0:T(8,128)(2,1)S(1)} %sent.4), channel_id=1, source_target_pairs={{0,4},{4,0},{1,5},{5,1},{2,6},{6,2},{3,7},{7,3},{8,12},{12,8},{9,1... | collective-permute-start | bytes 884744 | tf_op jit(solution)/shard_map/ppermute | solution.py:462
  35.3 5.6 %collective-permute-start.9 = (bf16[304,256]{1,0:T(8,128)(2,1)S(1)}, bf16[304,256]{1,0:T(8,128)(2,1)S(1)}, u32[]{:S(2)}, u32[]{:S(2)}) collective-permute-start(bf16[304,256]{1,0:T(8,128)(2,1)S(1)} %pair.2.refs_0_), channel_id=1, source_target_pairs={{0,16},{8,24},{16,0},{24,8},{1,17},{9,25},{17,1},{25,9},{2,18},{10... | collective-permute-start | bytes 466952 | tf_op jit(solution)/shard_map/ppermute | solution.py:462
  35.9 9.2 %collective-permute-start.8 = (bf16[304,256]{1,0:T(8,128)(2,1)S(1)}, bf16[304,256]{1,0:T(8,128)(2,1)S(1)}, u32[]{:S(2)}, u32[]{:S(2)}) collective-permute-start(bf16[304,256]{1,0:T(8,128)(2,1)S(1)} %pair.2.refs_0_), channel_id=1, source_target_pairs={{0,8},{8,0},{16,24},{24,16},{1,9},{9,1},{17,25},{25,17},{2,10},{10... | collective-permute-start | bytes 466952 | tf_op jit(solution)/shard_map/ppermute | solution.py:462
  40.2 4.7 %collective-permute-start.13 = (f32[96,256]{1,0:T(8,128)S(1)}, f32[96,256]{1,0:T(8,128)S(1)}, u32[]{:S(2)}, u32[]{:S(2)}) collective-permute-start(f32[96,256]{1,0:T(8,128)S(1)} %sent.6), channel_id=1, source_target_pairs={{0,4},{4,0},{1,5},{5,1},{2,6},{6,2},{3,7},{7,3},{8,12},{12,8},{9,1... | collective-permute-start | bytes 294920 | tf_op jit(solution)/shard_map/ppermute | solution.py:462
  40.8 9.2 %collective-permute-start.10 = (bf16[304,256]{1,0:T(8,128)(2,1)S(1)}, bf16[304,256]{1,0:T(8,128)(2,1)S(1)}, u32[]{:S(2)}, u32[]{:S(2)}) collective-permute-start(bf16[304,256]{1,0:T(8,128)(2,1)S(1)} %collective-permute-done.9.refs_2_), channel_id=1, source_target_pairs={{0,8},{8,0},{16,24},{24,16},{1,9},{9,1},{17,25},{25,17},{2,10},{10... | collective-permute-start | bytes 466952 | tf_op jit(solution)/shard_map/ppermute | solution.py:462
  42.2 5.7 %collective-permute-start.19 = (bf16[96,512]{1,0:T(8,128)(2,1)S(1)}, bf16[96,512]{1,0:T(8,128)(2,1)S(1)}, u32[]{:S(2)}, u32[]{:S(2)}) collective-permute-start(bf16[96,512]{1,0:T(8,128)(2,1)S(1)} %sent.7), channel_id=1, source_target_pairs={{0,4},{4,0},{1,5},{5,1},{2,6},{6,2},{3,7},{7,3},{8,12},{12,8},{9,1... | collective-permute-start | bytes 294920 | tf_op jit(solution)/shard_map/ppermute | solution.py:462
  45.0 4.1 %collective-permute-start.16 = (bf16[96,256]{1,0:T(8,128)(2,1)S(1)}, bf16[96,256]{1,0:T(8,128)(2,1)S(1)}, u32[]{:S(2)}, u32[]{:S(2)}) collective-permute-start(bf16[96,256]{1,0:T(8,128)(2,1)S(1)} %pair.3.refs_4_), channel_id=1, source_target_pairs={{0,24},{8,16},{16,8},{24,0},{1,25},{9,17},{17,9},{25,1},{2,26},{10... | collective-permute-start | bytes 147464 | tf_op jit(solution)/shard_map/ppermute | solution.py:462
  45.1 4.9 %collective-permute-start.15 = (bf16[96,256]{1,0:T(8,128)(2,1)S(1)}, bf16[96,256]{1,0:T(8,128)(2,1)S(1)}, u32[]{:S(2)}, u32[]{:S(2)}) collective-permute-start(bf16[96,256]{1,0:T(8,128)(2,1)S(1)} %pair.3.refs_4_), channel_id=1, source_target_pairs={{0,16},{8,24},{16,0},{24,8},{1,17},{9,25},{17,1},{25,9},{2,18},{10... | collective-permute-start | bytes 147464 | tf_op jit(solution)/shard_map/ppermute | solution.py:462
  53.1 5.3 %collective-permute-start.20 = (bf16[48,512]{1,0:T(8,128)(2,1)S(1)}, bf16[48,512]{1,0:T(8,128)(2,1)S(1)}, u32[]{:S(2)}, u32[]{:S(2)}) collective-permute-start(bf16[48,512]{1,0:T(8,128)(2,1)S(1)} %get-tuple-element.45), channel_id=1, source_target_pairs={{0,4},{4,0},{1,5},{5,1},{2,6},{6,2},{3,7},{7,3},{8,12},{12,8},{9,1... | collective-permute-start | bytes 147464 | tf_op jit(solution)/shard_map/ppermute | solution.py:462
  57.1 10.2 %collective-permute-start.17 = (bf16[48,512]{1,0:T(8,128)(2,1)S(1)}, bf16[48,512]{1,0:T(8,128)(2,1)S(1)}, u32[]{:S(2)}, u32[]{:S(2)}) collective-permute-start(bf16[48,512]{1,0:T(8,128)(2,1)S(1)} %get-tuple-element.40), channel_id=1, source_target_pairs={{0,4},{4,0},{1,5},{5,1},{2,6},{6,2},{3,7},{7,3},{8,12},{12,8},{9,1... | collective-permute-start | bytes 147464 | tf_op jit(solution)/shard_map/ppermute | solution.py:462
  60.7 33.4 %collective-permute-start.24 = (bf16[48,4096]{1,0:T(8,128)(2,1)S(1)}, bf16[48,4096]{1,0:T(8,128)(2,1)S(1)}, u32[]{:S(2)}, u32[]{:S(2)}) collective-permute-start(bf16[48,4096]{1,0:T(8,128)(2,1)S(1)} %convolution_convert_fusion.1), channel_id=1, source_target_pairs={{0,3},{1,2},{2,1},{3,0},{4,7},{5,6},{6,5},{7,4},{8,11},{9,10},{10,... | collective-permute-start | bytes 1179656 | tf_op jit(solution)/shard_map/ppermute | solution.py:462
  66.3 7.5 %collective-permute-start.21 = (bf16[48,512]{1,0:T(8,128)(2,1)S(1)}, bf16[48,512]{1,0:T(8,128)(2,1)S(1)}, u32[]{:S(2)}, u32[]{:S(2)}) collective-permute-start(bf16[48,512]{1,0:T(8,128)(2,1)S(1)} %get-tuple-element.48), channel_id=1, source_target_pairs={{0,4},{4,0},{1,5},{5,1},{2,6},{6,2},{3,7},{7,3},{8,12},{12,8},{9,1... | collective-permute-start | bytes 147464 | tf_op jit(solution)/shard_map/ppermute | solution.py:462
  69.5 24.7 %collective-permute-start.23 = (bf16[48,4096]{1,0:T(8,128)(2,1)S(1)}, bf16[48,4096]{1,0:T(8,128)(2,1)S(1)}, u32[]{:S(2)}, u32[]{:S(2)}) collective-permute-start(bf16[48,4096]{1,0:T(8,128)(2,1)S(1)} %convolution_convert_fusion.2), channel_id=1, source_target_pairs={{0,2},{1,3},{2,0},{3,1},{4,6},{5,7},{6,4},{7,5},{8,10},{9,11},{10,... | collective-permute-start | bytes 1179656 | tf_op jit(solution)/shard_map/ppermute | solution.py:462
  72.7 5.3 %collective-permute-start.18 = (bf16[48,512]{1,0:T(8,128)(2,1)S(1)}, bf16[48,512]{1,0:T(8,128)(2,1)S(1)}, u32[]{:S(2)}, u32[]{:S(2)}) collective-permute-start(bf16[48,512]{1,0:T(8,128)(2,1)S(1)} %get-tuple-element.43), channel_id=1, source_target_pairs={{0,4},{4,0},{1,5},{5,1},{2,6},{6,2},{3,7},{7,3},{8,12},{12,8},{9,1... | collective-permute-start | bytes 147464 | tf_op jit(solution)/shard_map/ppermute | solution.py:462
  76.0 18.2 %collective-permute-start.22 = (bf16[48,4096]{1,0:T(8,128)(2,1)S(1)}, bf16[48,4096]{1,0:T(8,128)(2,1)S(1)}, u32[]{:S(2)}, u32[]{:S(2)}) collective-permute-start(bf16[48,4096]{1,0:T(8,128)(2,1)S(1)} %convolution_convert_fusion), channel_id=1, source_target_pairs={{0,1},{1,0},{2,3},{3,2},{4,5},{5,4},{6,7},{7,6},{8,9},{9,8},{10,11... | collective-permute-start | bytes 1179656 | tf_op jit(solution)/shard_map/ppermute | solution.py:462
  (11 other events, 119.5 us)

commit v9 on v8

--- a/solution.py
+++ b/solution.py
@@ -554,7 +554,7 @@
     ends_rows = send(two_rows, "tensor", [(1, 0), (2, 3)])
     early_projected = project_pair(early_stacked)
     early_queries, early_came = project_query(early_stacked)
-    late_stacked = stack("late_rows", [[middle_rows, ends_rows]], (1,))[0]
+    late_stacked = stack("late_rows", [[ends_rows, middle_rows]], (1,))[0]
     late_projected = project_pair(late_stacked)
     late_queries, late_came = project_query(late_stacked)
     early_pairs = gather_by_steps(rotate_pair(early_projected, 0, [document_rows]))
@@ -599,7 +599,7 @@
     came_2 = send(term_2, "tensor", two)
     rows_1 = joined(1, term_3)
     came_1 = send(product(rows_1, w_out).astype(bf16), "tensor", one)
-    rows_0 = joined(0, term_2)
+    rows_0 = joined(0, term_3)
     total = lax.optimization_barrier(product(rows_0, w_out))
     total = total + hidden_in.astype(jnp.float32) + came_1.astype(jnp.float32)
     total = total + came_2.astype(jnp.float32) + came_3.astype(jnp.float32)

time: 97.1 us -> 97.1 us (level); the launches traced: 95.2 us -> 96.7 us
  waiting for transfers between devices: 34.2 us -> 39.1 us
  Pallas kernels: 19.4 us -> 16 us
    ppermute x23, waiting for transfers between devices: 26.4 us -> 31.3 us  [send(): return lax.ppermute(value, axis, pairs)]
    pallas_call x19, Pallas kernels: 19.4 us -> 16 us  [call_kernel(): pl.pallas_call(kernel, name=name, grid_spec=pltpu.PrefetchScalarGridSpec(...]
  transfers between devices with their start and end apart: 25 -> 25, of which waited for: 10 -> 11; matrix products, arithmetic and copies ran while one was open for 12% -> 12% of each run, Pallas kernels for 20% -> 16%
where the time goes in v9:
time: 97.1 us; the launch traced here: 96.7 us
  waiting for transfers between devices  39.1 us (40%)
  starting transfers between devices  26.8 us (28%)
  Pallas kernels  16 us (16%)
  matrix products  10.1 us (10%)
  other arithmetic  2.46 us (3%)
  local copies, waits for them, and re-layouts  1.82 us (2%)
    ppermute x23, waiting for transfers between devices, send(): return lax.ppermute(value, axis, pairs)  31.3 us
    ppermute x23, starting transfers between devices, send(): return lax.ppermute(value, axis, pairs)  21.8 us
    pallas_call x19, Pallas kernels, call_kernel(): pl.pallas_call(kernel, name=name, grid_spec=pltpu.PrefetchScalarGridSpec(...  16 us
    dot_general x10, matrix products, product(): return jnp.dot(left, right, preferred_element_type=jnp.float32)  10.1 us
    ppermute x2, waiting for transfers between devices, send_across(): return lax.ppermute(value, ('inner', 'tensor'), both)  7.78 us
    ppermute x2, starting transfers between devices, send_across(): return lax.ppermute(value, ('inner', 'tensor'), both)  5.01 us
  transfers between devices with their start and end apart: 25, of which 11 were waited for; matrix products, arithmetic and copies ran while one was open for 12% of the time, Pallas kernels for 16%

profile of v9, /device:TPU:2, one launch (start us, length us, event | category | flops | bytes accessed | tf_op | source)
XLA Modules:
  0.0 96.7 jit_solution(14242522394188701393)
XLA Ops:
  2.1 3.6 %collective-permute-start.4 = (bf16[48,2048]{1,0:T(8,128)(2,1)S(1)}, bf16[48,2048]{1,0:T(8,128)(2,1)S(1)}, u32[]{:S(2)}, u32[]{:S(2)}) collective-permute-start(bf16[48,2048]{1,0:T(8,128)(2,1)S(1)} %get-tuple-element.30), channel_id=1, source_target_pairs={{0,6},{1,7},{2,4},{3,5},{4,2},{5,3},{6,0},{7,1},{8,14},{9,15},{10,... | collective-permute-start | bytes 589832 | tf_op jit(solution)/shard_map/ppermute | solution.py:466
  5.7 1.6 %collective-permute-start.1 = (bf16[48,2048]{1,0:T(8,128)(2,1)S(1)}, bf16[48,2048]{1,0:T(8,128)(2,1)S(1)}, u32[]{:S(2)}, u32[]{:S(2)}) collective-permute-start(bf16[48,2048]{1,0:T(8,128)(2,1)S(1)} %get-tuple-element.33.refs_0_), channel_id=1, source_target_pairs={{0,1},{1,0},{2,3},{3,2},{4,5},{5,4},{6,7},{7,6},{8,9},{9,8},{10,11... | collective-permute-start | bytes 589832 | tf_op jit(solution)/shard_map/ppermute | solution.py:462
  10.2 5.8 %collective-permute-done.4.refs_5_ = bf16[48,2048]{1,0:T(8,128)(2,1)S(1)} collective-permute-done((bf16[48,2048]{1,0:T(8,128)(2,1)S(1)}, bf16[48,2048]{1,0:T(8,128)(2,1)S(1)}, u32[]{:S(2)}, u32[]{:S(2)}) %collective-permute-start.4) | collective-permute-done | bytes 196640 | tf_op jit(solution)/shard_map/ppermute | solution.py:466
  16.1 1.5 %collective-permute-start.9 = (s32[2,192]{1,0:T(2,128)S(1)}, s32[2,192]{1,0:T(2,128)S(1)}, u32[]{:S(2)}, u32[]{:S(2)}) collective-permute-start(s32[2,192]{1,0:T(2,128)S(1)} %pad_add_fusion.here), channel_id=1, source_target_pairs={{0,4},{4,0},{1,5},{5,1},{2,6},{6,2},{3,7},{7,3},{8,12},{12,8},{9,1... | collective-permute-start | bytes 4616 | tf_op jit(solution)/shard_map/ppermute | solution.py:462
  17.6 3.3 %collective-permute-done.1.refs_2_ = bf16[48,2048]{1,0:T(8,128)(2,1)S(1)} collective-permute-done((bf16[48,2048]{1,0:T(8,128)(2,1)S(1)}, bf16[48,2048]{1,0:T(8,128)(2,1)S(1)}, u32[]{:S(2)}, u32[]{:S(2)}) %collective-permute-start.1) | collective-permute-done | bytes 196640 | tf_op jit(solution)/shard_map/ppermute | solution.py:462
  21.6 2.0 %collective-permute-done.2.refs_3_ = bf16[48,2048]{1,0:T(8,128)(2,1)S(1)} collective-permute-done((bf16[48,2048]{1,0:T(8,128)(2,1)S(1)}, bf16[48,2048]{1,0:T(8,128)(2,1)S(1)}, u32[]{:S(2)}, u32[]{:S(2)}) %collective-permute-start.2) | collective-permute-done | bytes 196640 | tf_op jit(solution)/shard_map/ppermute | solution.py:466
  26.0 1.6 %collective-permute-start.10 = (f32[288,256]{1,0:T(8,128)S(1)}, f32[288,256]{1,0:T(8,128)S(1)}, u32[]{:S(2)}, u32[]{:S(2)}) collective-permute-start(f32[288,256]{1,0:T(8,128)S(1)} %sent.6), channel_id=1, source_target_pairs={{0,4},{4,0},{1,5},{5,1},{2,6},{6,2},{3,7},{7,3},{8,12},{12,8},{9,1... | collective-permute-start | bytes 884744 | tf_op jit(solution)/shard_map/ppermute | solution.py:462
  27.6 1.4 %collective-permute-start.6 = (bf16[96,2048]{1,0:T(8,128)(2,1)S(1)}, bf16[96,2048]{1,0:T(8,128)(2,1)S(1)}, u32[]{:S(2)}, u32[]{:S(2)}) collective-permute-start(bf16[96,2048]{1,0:T(8,128)(2,1)S(1)} %get-tuple-element.32), channel_id=1, source_target_pairs={{1,0},{2,3},{5,4},{6,7},{9,8},{10,11},{13,12},{14,15},{17,16},{18,... | collective-permute-start | bytes 1179656 | tf_op jit(solution)/shard_map/ppermute | solution.py:462
  29.0 1.4 %fusion.refs_0_.kept = f32[288,1024]{1,0:T(8,128)S(1)} fusion(bf16[288,2048]{1,0:T(8,128)(2,1)S(1)} %get-tuple-element.31, bf16[2048,1024]{1,0:T(8,128)(2,1)S(1)} %copy-done.5), kind=kOutput, calls=%fused_computation.8 | convolution fusion | flops 1207959552 | bytes 6553600 | tf_op jit(solution)/shard_map/dot_general | solution.py:273
  33.2 1.9 %collective-permute-done.10.came = f32[288,256]{1,0:T(8,128)S(1)} collective-permute-done((f32[288,256]{1,0:T(8,128)S(1)}, f32[288,256]{1,0:T(8,128)S(1)}, u32[]{:S(2)}, u32[]{:S(2)}) %collective-permute-start.10) | collective-permute-done | bytes 294944 | tf_op jit(solution)/shard_map/ppermute | solution.py:462
  35.9 3.1 %collective-permute-done.6.refs_0_ = bf16[96,2048]{1,0:T(8,128)(2,1)S(1)} collective-permute-done((bf16[96,2048]{1,0:T(8,128)(2,1)S(1)}, bf16[96,2048]{1,0:T(8,128)(2,1)S(1)}, u32[]{:S(2)}, u32[]{:S(2)}) %collective-permute-start.6) | collective-permute-done | bytes 393248 | tf_op jit(solution)/shard_map/ppermute | solution.py:462
  42.2 2.2 %collective-permute-start.8 = (bf16[96,512]{1,0:T(8,128)(2,1)S(1)}, bf16[96,512]{1,0:T(8,128)(2,1)S(1)}, u32[]{:S(2)}, u32[]{:S(2)}) collective-permute-start(bf16[96,512]{1,0:T(8,128)(2,1)S(1)} %sent.5), channel_id=1, source_target_pairs={{0,4},{4,0},{1,5},{5,1},{2,6},{6,2},{3,7},{7,3},{8,12},{12,8},{9,1... | collective-permute-start | bytes 294920 | tf_op jit(solution)/shard_map/ppermute | solution.py:462
  46.4 1.4 %collective-permute-done.8.came = bf16[96,512]{1,0:T(8,128)(2,1)S(1)} collective-permute-done((bf16[96,512]{1,0:T(8,128)(2,1)S(1)}, bf16[96,512]{1,0:T(8,128)(2,1)S(1)}, u32[]{:S(2)}, u32[]{:S(2)}) %collective-permute-start.8) | collective-permute-done | bytes 98336 | tf_op jit(solution)/shard_map/ppermute | solution.py:462
  50.0 2.3 %attention.4 = (bf16[48,512]{1,0:T(8,128)(2,1)S(1)}, bf16[48,512]{1,0:T(8,128)(2,1)S(1)}) custom-call(s32[3]{0:T(128)S(1)} %pad_add_fusion.1.which, f32[96,1024]{1,0:T(8,128)S(1)} %fusion.1.refs_0_.kept, bf16[96,512]{1,0:T(8,128)(2,1)S(1)} %collective-permute-done.8.came, f32[384,128]{1,0:T(8,128)S(1)} %get-tuple-element.48.cosines, ...), custom_call_target="tpu_custom_call" | custom-call | tf_op jit(solution)/shard_map/attention/pallas_call | solution.py:217
  53.2 2.3 %attention.7 = (bf16[48,512]{1,0:T(8,128)(2,1)S(1)}, bf16[48,512]{1,0:T(8,128)(2,1)S(1)}) custom-call(s32[3]{0:T(128)S(1)} %pad_add_fusion.1.which, f32[288,1024]{1,0:T(8,128)S(1)} %fusion.refs_0_.kept, bf16[288,512]{1,0:T(8,128)(2,1)S(1)} %collective-permute-done.5.came, f32[384,128]{1,0:T(8,128)S(1)} %get-tuple-element.48.cosines, ...), custom_call_target="tpu_custom_call" | custom-call | tf_op jit(solution)/shard_map/attention/pallas_call | solution.py:217
  57.7 1.6 %convolution_convert_fusion.2 = bf16[48,4096]{1,0:T(8,128)(2,1)S(1)} fusion(bf16[48,1024]{1,0:T(8,128)(2,1)S(1)} %join.4, bf16[1024,4096]{1,0:T(8,128)(2,1)S(1)} %bitcast.28), kind=kOutput, calls=%fused_computation.2 | convolution fusion | flops 402849792 | bytes 8880128 | tf_op jit(solution)/shard_map/dot_general | solution.py:273
  59.3 2.5 %collective-permute-start.24 = (bf16[48,4096]{1,0:T(8,128)(2,1)S(1)}, bf16[48,4096]{1,0:T(8,128)(2,1)S(1)}, u32[]{:S(2)}, u32[]{:S(2)}) collective-permute-start(bf16[48,4096]{1,0:T(8,128)(2,1)S(1)} %convolution_convert_fusion.2), channel_id=1, source_target_pairs={{0,3},{1,2},{2,1},{3,0},{4,7},{5,6},{6,5},{7,4},{8,11},{9,10},{10,... | collective-permute-start | bytes 1179656 | tf_op jit(solution)/shard_map/ppermute | solution.py:462
  61.8 2.3 %attention.6 = (bf16[48,512]{1,0:T(8,128)(2,1)S(1)}, bf16[48,512]{1,0:T(8,128)(2,1)S(1)}) custom-call(s32[3]{0:T(128)S(1)} %pad_add_fusion.1.which, f32[288,1024]{1,0:T(8,128)S(1)} %fusion.refs_0_.kept, bf16[288,512]{1,0:T(8,128)(2,1)S(1)} %collective-permute-done.5.came, f32[384,128]{1,0:T(8,128)S(1)} %get-tuple-element.48.cosines, ...), custom_call_target="tpu_custom_call" | custom-call | tf_op jit(solution)/shard_map/attention/pallas_call | solution.py:217
  65.0 2.3 %attention.5 = (bf16[48,512]{1,0:T(8,128)(2,1)S(1)}, bf16[48,512]{1,0:T(8,128)(2,1)S(1)}) custom-call(s32[3]{0:T(128)S(1)} %pad_add_fusion.1.which, f32[288,1024]{1,0:T(8,128)S(1)} %fusion.refs_0_.kept, bf16[288,512]{1,0:T(8,128)(2,1)S(1)} %collective-permute-done.5.came, f32[384,128]{1,0:T(8,128)S(1)} %get-tuple-element.48.cosines, ...), custom_call_target="tpu_custom_call" | custom-call | tf_op jit(solution)/shard_map/attention/pallas_call | solution.py:217
  69.0 1.6 %convolution_convert_fusion = bf16[48,4096]{1,0:T(8,128)(2,1)S(1)} fusion(bf16[48,1024]{1,0:T(8,128)(2,1)S(1)} %join.7, bf16[1024,4096]{1,0:T(8,128)(2,1)S(1)} %bitcast.28), kind=kOutput, calls=%fused_computation | convolution fusion | flops 402849792 | bytes 8880128 | tf_op jit(solution)/shard_map/dot_general | solution.py:273
  71.3 1.6 %convolution_convert_fusion.1 = bf16[48,4096]{1,0:T(8,128)(2,1)S(1)} fusion(bf16[48,1024]{1,0:T(8,128)(2,1)S(1)} %join.6, bf16[1024,4096]{1,0:T(8,128)(2,1)S(1)} %bitcast.28), kind=kOutput, calls=%fused_computation.1 | convolution fusion | flops 402849792 | bytes 8880128 | tf_op jit(solution)/shard_map/dot_general | solution.py:273
  72.9 2.0 %collective-permute-start.21 = (bf16[48,4096]{1,0:T(8,128)(2,1)S(1)}, bf16[48,4096]{1,0:T(8,128)(2,1)S(1)}, u32[]{:S(2)}, u32[]{:S(2)}) collective-permute-start(bf16[48,4096]{1,0:T(8,128)(2,1)S(1)} %convolution_convert_fusion.1), channel_id=1, source_target_pairs={{0,1},{1,0},{2,3},{3,2},{4,5},{5,4},{6,7},{7,6},{8,9},{9,8},{10,11... | collective-permute-start | bytes 1179656 | tf_op jit(solution)/shard_map/ppermute | solution.py:462
  75.5 1.6 %fusion.6 = f32[48,4096]{1,0:T(8,128)S(1)} fusion(bf16[48,1024]{1,0:T(8,128)(2,1)S(1)} %join.5, bf16[1024,4096]{1,0:T(8,128)(2,1)S(1)} %bitcast.28), kind=kOutput, calls=%fused_computation.14 | convolution fusion | flops 402653184 | bytes 9273344 | tf_op jit(solution)/shard_map/dot_general | solution.py:273
  77.0 18.7 %collective-permute-done.23 = bf16[48,4096]{1,0:T(8,128)(2,1)S(1)} collective-permute-done((bf16[48,4096]{1,0:T(8,128)(2,1)S(1)}, bf16[48,4096]{1,0:T(8,128)(2,1)S(1)}, u32[]{:S(2)}, u32[]{:S(2)}) %collective-permute-start.23) | collective-permute-done | bytes 393248 | tf_op jit(solution)/shard_map/ppermute | solution.py:462
  (80 shorter events, 27.0 us)
Async XLA Ops:
  2.1 13.9 %collective-permute-start.4 = (bf16[48,2048]{1,0:T(8,128)(2,1)S(1)}, bf16[48,2048]{1,0:T(8,128)(2,1)S(1)}, u32[]{:S(2)}, u32[]{:S(2)}) collective-permute-start(bf16[48,2048]{1,0:T(8,128)(2,1)S(1)} %get-tuple-element.30), channel_id=1, source_target_pairs={{0,6},{1,7},{2,4},{3,5},{4,2},{5,3},{6,0},{7,1},{8,14},{9,15},{10,... | collective-permute-start | bytes 589832 | tf_op jit(solution)/shard_map/ppermute | solution.py:466
  5.7 15.1 %collective-permute-start.1 = (bf16[48,2048]{1,0:T(8,128)(2,1)S(1)}, bf16[48,2048]{1,0:T(8,128)(2,1)S(1)}, u32[]{:S(2)}, u32[]{:S(2)}) collective-permute-start(bf16[48,2048]{1,0:T(8,128)(2,1)S(1)} %get-tuple-element.33.refs_0_), channel_id=1, source_target_pairs={{0,1},{1,0},{2,3},{3,2},{4,5},{5,4},{6,7},{7,6},{8,9},{9,8},{10,11... | collective-permute-start | bytes 589832 | tf_op jit(solution)/shard_map/ppermute | solution.py:462
  7.3 13.6 %collective-permute-start = (bf16[48,2048]{1,0:T(8,128)(2,1)S(1)}, bf16[48,2048]{1,0:T(8,128)(2,1)S(1)}, u32[]{:S(2)}, u32[]{:S(2)}) collective-permute-start(bf16[48,2048]{1,0:T(8,128)(2,1)S(1)} %get-tuple-element.30), channel_id=1, source_target_pairs={{0,4},{4,0},{1,5},{5,1},{2,6},{6,2},{3,7},{7,3},{8,12},{12,8},{9,1... | collective-permute-start | bytes 589832 | tf_op jit(solution)/shard_map/ppermute | solution.py:462
  7.8 15.7 %collective-permute-start.2 = (bf16[48,2048]{1,0:T(8,128)(2,1)S(1)}, bf16[48,2048]{1,0:T(8,128)(2,1)S(1)}, u32[]{:S(2)}, u32[]{:S(2)}) collective-permute-start(bf16[48,2048]{1,0:T(8,128)(2,1)S(1)} %get-tuple-element.30), channel_id=1, source_target_pairs={{0,5},{1,4},{2,7},{3,6},{4,1},{5,0},{6,3},{7,2},{8,13},{9,12},{10,... | collective-permute-start | bytes 589832 | tf_op jit(solution)/shard_map/ppermute | solution.py:466
  9.2 14.3 %collective-permute-start.3 = (bf16[48,2048]{1,0:T(8,128)(2,1)S(1)}, bf16[48,2048]{1,0:T(8,128)(2,1)S(1)}, u32[]{:S(2)}, u32[]{:S(2)}) collective-permute-start(bf16[48,2048]{1,0:T(8,128)(2,1)S(1)} %get-tuple-element.33.refs_0_), channel_id=1, source_target_pairs={{0,2},{1,3},{2,0},{3,1},{4,6},{5,7},{6,4},{7,5},{8,10},{9,11},{10,... | collective-permute-start | bytes 589832 | tf_op jit(solution)/shard_map/ppermute | solution.py:462
  16.1 15.5 %collective-permute-start.9 = (s32[2,192]{1,0:T(2,128)S(1)}, s32[2,192]{1,0:T(2,128)S(1)}, u32[]{:S(2)}, u32[]{:S(2)}) collective-permute-start(s32[2,192]{1,0:T(2,128)S(1)} %pad_add_fusion.here), channel_id=1, source_target_pairs={{0,4},{4,0},{1,5},{5,1},{2,6},{6,2},{3,7},{7,3},{8,12},{12,8},{9,1... | collective-permute-start | bytes 4616 | tf_op jit(solution)/shard_map/ppermute | solution.py:462
  20.9 15.0 %collective-permute-start.7 = (bf16[96,2048]{1,0:T(8,128)(2,1)S(1)}, bf16[96,2048]{1,0:T(8,128)(2,1)S(1)}, u32[]{:S(2)}, u32[]{:S(2)}) collective-permute-start(bf16[96,2048]{1,0:T(8,128)(2,1)S(1)} %own_rows.1), channel_id=1, source_target_pairs={{1,2},{2,1},{5,6},{6,5},{9,10},{10,9},{13,14},{14,13},{17,18},{18,... | collective-permute-start | bytes 1179656 | tf_op jit(solution)/shard_map/ppermute | solution.py:462
  26.0 9.1 %collective-permute-start.10 = (f32[288,256]{1,0:T(8,128)S(1)}, f32[288,256]{1,0:T(8,128)S(1)}, u32[]{:S(2)}, u32[]{:S(2)}) collective-permute-start(f32[288,256]{1,0:T(8,128)S(1)} %sent.6), channel_id=1, source_target_pairs={{0,4},{4,0},{1,5},{5,1},{2,6},{6,2},{3,7},{7,3},{8,12},{12,8},{9,1... | collective-permute-start | bytes 884744 | tf_op jit(solution)/shard_map/ppermute | solution.py:462
  27.6 11.4 %collective-permute-start.6 = (bf16[96,2048]{1,0:T(8,128)(2,1)S(1)}, bf16[96,2048]{1,0:T(8,128)(2,1)S(1)}, u32[]{:S(2)}, u32[]{:S(2)}) collective-permute-start(bf16[96,2048]{1,0:T(8,128)(2,1)S(1)} %get-tuple-element.32), channel_id=1, source_target_pairs={{1,0},{2,3},{5,4},{6,7},{9,8},{10,11},{13,12},{14,15},{17,16},{18,... | collective-permute-start | bytes 1179656 | tf_op jit(solution)/shard_map/ppermute | solution.py:462
  31.0 22.2 %collective-permute-start.5 = (bf16[288,512]{1,0:T(8,128)(2,1)S(1)}, bf16[288,512]{1,0:T(8,128)(2,1)S(1)}, u32[]{:S(2)}, u32[]{:S(2)}) collective-permute-start(bf16[288,512]{1,0:T(8,128)(2,1)S(1)} %sent.4), channel_id=1, source_target_pairs={{0,4},{4,0},{1,5},{5,1},{2,6},{6,2},{3,7},{7,3},{8,12},{12,8},{9,1... | collective-permute-start | bytes 884744 | tf_op jit(solution)/shard_map/ppermute | solution.py:462
  35.3 5.6 %collective-permute-start.12 = (bf16[304,256]{1,0:T(8,128)(2,1)S(1)}, bf16[304,256]{1,0:T(8,128)(2,1)S(1)}, u32[]{:S(2)}, u32[]{:S(2)}) collective-permute-start(bf16[304,256]{1,0:T(8,128)(2,1)S(1)} %pair.2.refs_0_), channel_id=1, source_target_pairs={{0,16},{8,24},{16,0},{24,8},{1,17},{9,25},{17,1},{25,9},{2,18},{10... | collective-permute-start | bytes 466952 | tf_op jit(solution)/shard_map/ppermute | solution.py:462
  35.9 9.2 %collective-permute-start.11 = (bf16[304,256]{1,0:T(8,128)(2,1)S(1)}, bf16[304,256]{1,0:T(8,128)(2,1)S(1)}, u32[]{:S(2)}, u32[]{:S(2)}) collective-permute-start(bf16[304,256]{1,0:T(8,128)(2,1)S(1)} %pair.2.refs_0_), channel_id=1, source_target_pairs={{0,8},{8,0},{16,24},{24,16},{1,9},{9,1},{17,25},{25,17},{2,10},{10... | collective-permute-start | bytes 466952 | tf_op jit(solution)/shard_map/ppermute | solution.py:462
  40.2 4.7 %collective-permute-start.14 = (f32[96,256]{1,0:T(8,128)S(1)}, f32[96,256]{1,0:T(8,128)S(1)}, u32[]{:S(2)}, u32[]{:S(2)}) collective-permute-start(f32[96,256]{1,0:T(8,128)S(1)} %sent.7), channel_id=1, source_target_pairs={{0,4},{4,0},{1,5},{5,1},{2,6},{6,2},{3,7},{7,3},{8,12},{12,8},{9,1... | collective-permute-start | bytes 294920 | tf_op jit(solution)/shard_map/ppermute | solution.py:462
  40.8 9.2 %collective-permute-start.13 = (bf16[304,256]{1,0:T(8,128)(2,1)S(1)}, bf16[304,256]{1,0:T(8,128)(2,1)S(1)}, u32[]{:S(2)}, u32[]{:S(2)}) collective-permute-start(bf16[304,256]{1,0:T(8,128)(2,1)S(1)} %collective-permute-done.12.refs_2_), channel_id=1, source_target_pairs={{0,8},{8,0},{16,24},{24,16},{1,9},{9,1},{17,25},{25,17},{2,10},{10... | collective-permute-start | bytes 466952 | tf_op jit(solution)/shard_map/ppermute | solution.py:462
  42.2 5.7 %collective-permute-start.8 = (bf16[96,512]{1,0:T(8,128)(2,1)S(1)}, bf16[96,512]{1,0:T(8,128)(2,1)S(1)}, u32[]{:S(2)}, u32[]{:S(2)}) collective-permute-start(bf16[96,512]{1,0:T(8,128)(2,1)S(1)} %sent.5), channel_id=1, source_target_pairs={{0,4},{4,0},{1,5},{5,1},{2,6},{6,2},{3,7},{7,3},{8,12},{12,8},{9,1... | collective-permute-start | bytes 294920 | tf_op jit(solution)/shard_map/ppermute | solution.py:462
  45.0 4.1 %collective-permute-start.17 = (bf16[96,256]{1,0:T(8,128)(2,1)S(1)}, bf16[96,256]{1,0:T(8,128)(2,1)S(1)}, u32[]{:S(2)}, u32[]{:S(2)}) collective-permute-start(bf16[96,256]{1,0:T(8,128)(2,1)S(1)} %pair.3.refs_4_), channel_id=1, source_target_pairs={{0,24},{8,16},{16,8},{24,0},{1,25},{9,17},{17,9},{25,1},{2,26},{10... | collective-permute-start | bytes 147464 | tf_op jit(solution)/shard_map/ppermute | solution.py:462
  45.1 4.9 %collective-permute-start.16 = (bf16[96,256]{1,0:T(8,128)(2,1)S(1)}, bf16[96,256]{1,0:T(8,128)(2,1)S(1)}, u32[]{:S(2)}, u32[]{:S(2)}) collective-permute-start(bf16[96,256]{1,0:T(8,128)(2,1)S(1)} %pair.3.refs_4_), channel_id=1, source_target_pairs={{0,16},{8,24},{16,0},{24,8},{1,17},{9,25},{17,1},{25,9},{2,18},{10... | collective-permute-start | bytes 147464 | tf_op jit(solution)/shard_map/ppermute | solution.py:462
  52.3 4.7 %collective-permute-start.18 = (bf16[48,512]{1,0:T(8,128)(2,1)S(1)}, bf16[48,512]{1,0:T(8,128)(2,1)S(1)}, u32[]{:S(2)}, u32[]{:S(2)}) collective-permute-start(bf16[48,512]{1,0:T(8,128)(2,1)S(1)} %get-tuple-element.39), channel_id=1, source_target_pairs={{0,4},{4,0},{1,5},{5,1},{2,6},{6,2},{3,7},{7,3},{8,12},{12,8},{9,1... | collective-permute-start | bytes 147464 | tf_op jit(solution)/shard_map/ppermute | solution.py:462
  55.5 13.0 %collective-permute-start.22 = (bf16[48,512]{1,0:T(8,128)(2,1)S(1)}, bf16[48,512]{1,0:T(8,128)(2,1)S(1)}, u32[]{:S(2)}, u32[]{:S(2)}) collective-permute-start(bf16[48,512]{1,0:T(8,128)(2,1)S(1)} %get-tuple-element.46), channel_id=1, source_target_pairs={{0,4},{4,0},{1,5},{5,1},{2,6},{6,2},{3,7},{7,3},{8,12},{12,8},{9,1... | collective-permute-start | bytes 147464 | tf_op jit(solution)/shard_map/ppermute | solution.py:462
  59.3 36.5 %collective-permute-start.24 = (bf16[48,4096]{1,0:T(8,128)(2,1)S(1)}, bf16[48,4096]{1,0:T(8,128)(2,1)S(1)}, u32[]{:S(2)}, u32[]{:S(2)}) collective-permute-start(bf16[48,4096]{1,0:T(8,128)(2,1)S(1)} %convolution_convert_fusion.2), channel_id=1, source_target_pairs={{0,3},{1,2},{2,1},{3,0},{4,7},{5,6},{6,5},{7,4},{8,11},{9,10},{10,... | collective-permute-start | bytes 1179656 | tf_op jit(solution)/shard_map/ppermute | solution.py:462
  64.0 6.7 %collective-permute-start.20 = (bf16[48,512]{1,0:T(8,128)(2,1)S(1)}, bf16[48,512]{1,0:T(8,128)(2,1)S(1)}, u32[]{:S(2)}, u32[]{:S(2)}) collective-permute-start(bf16[48,512]{1,0:T(8,128)(2,1)S(1)} %get-tuple-element.44), channel_id=1, source_target_pairs={{0,4},{4,0},{1,5},{5,1},{2,6},{6,2},{3,7},{7,3},{8,12},{12,8},{9,1... | collective-permute-start | bytes 147464 | tf_op jit(solution)/shard_map/ppermute | solution.py:462
  67.3 7.6 %collective-permute-start.19 = (bf16[48,512]{1,0:T(8,128)(2,1)S(1)}, bf16[48,512]{1,0:T(8,128)(2,1)S(1)}, u32[]{:S(2)}, u32[]{:S(2)}) collective-permute-start(bf16[48,512]{1,0:T(8,128)(2,1)S(1)} %get-tuple-element.42), channel_id=1, source_target_pairs={{0,4},{4,0},{1,5},{5,1},{2,6},{6,2},{3,7},{7,3},{8,12},{12,8},{9,1... | collective-permute-start | bytes 147464 | tf_op jit(solution)/shard_map/ppermute | solution.py:462
  70.6 25.1 %collective-permute-start.23 = (bf16[48,4096]{1,0:T(8,128)(2,1)S(1)}, bf16[48,4096]{1,0:T(8,128)(2,1)S(1)}, u32[]{:S(2)}, u32[]{:S(2)}) collective-permute-start(bf16[48,4096]{1,0:T(8,128)(2,1)S(1)} %convolution_convert_fusion), channel_id=1, source_target_pairs={{0,2},{1,3},{2,0},{3,1},{4,6},{5,7},{6,4},{7,5},{8,10},{9,11},{10,... | collective-permute-start | bytes 1179656 | tf_op jit(solution)/shard_map/ppermute | solution.py:462
  72.9 22.9 %collective-permute-start.21 = (bf16[48,4096]{1,0:T(8,128)(2,1)S(1)}, bf16[48,4096]{1,0:T(8,128)(2,1)S(1)}, u32[]{:S(2)}, u32[]{:S(2)}) collective-permute-start(bf16[48,4096]{1,0:T(8,128)(2,1)S(1)} %convolution_convert_fusion.1), channel_id=1, source_target_pairs={{0,1},{1,0},{2,3},{3,2},{4,5},{5,4},{6,7},{7,6},{8,9},{9,8},{10,11... | collective-permute-start | bytes 1179656 | tf_op jit(solution)/shard_map/ppermute | solution.py:462
  (11 other events, 121.3 us)
